TPU v7x, 32 devices: a whole 2x2x4 slice. The times are simulated.
32 devices in a mesh: dp: 16 (over z, y, core), tensor: 2 (over x).
Axes of the slice: x: 2, y: 2, z: 4, core: 2. Of those that a mesh axis runs over, the one named last changes fastest.
Arguments:
- tokens: bfloat16 [16384, 1024], P(('dp', 'tensor')), may hold values from -6 to 6
- gains: bfloat16 [2, 1024], P(None, ('dp', 'tensor')), may hold values from 0.5 to 1.5
- w_zx: bfloat16 [1024, 2, 1536], P('dp', None, 'tensor'), may hold values from -0.1875 to 0.1875
- w_bc: bfloat16 [1024, 256], P(('dp', 'tensor')), may hold values from -0.1875 to 0.1875
- w_dt: bfloat16 [1024, 24], P('dp', 'tensor'), may hold values from -0.1875 to 0.1875
- conv_x: float32 [5, 1536], P(None, 'tensor'), may hold values from -3 to 3
- conv_bc: float32 [5, 256], replicated, may hold values from -3 to 3
- head_params: float32 [3, 24], P(None, 'tensor'), may hold values from -6 to 2.5, as said below
- w_mo: bfloat16 [1536, 1024], P('tensor', 'dp'), may hold values from -0.4375 to 0.4375
- w_q: bfloat16 [1024, 512], P('dp', 'tensor'), may hold values from -0.1875 to 0.1875
- w_kv: bfloat16 [1024, 2, 128], P('dp', None, 'tensor'), may hold values from -0.1875 to 0.1875
- w_ao: bfloat16 [512, 1024], P('tensor', 'dp'), may hold values from -2 to 2
- w_gu: bfloat16 [1024, 2, 2048], P('dp', None, 'tensor'), may hold values from -0.1875 to 0.1875
- w_down: bfloat16 [2048, 1024], P('tensor', 'dp'), may hold values from -0.25 to 0.25
- cotangent: bfloat16 [16384, 1024], P(('dp', 'tensor')), may hold values from -6 to 6
Outputs:
- layer_out: bfloat16 [16384, 1024], P(('dp', 'tensor'))
- input_grad: bfloat16 [16384, 1024], P(('dp', 'tensor'))
- grad_gains: float32 [2, 1024], P(None, ('dp', 'tensor'))
- grad_zx: float32 [1024, 2, 1536], P('dp', None, 'tensor')
- grad_bc: float32 [1024, 256], P(('dp', 'tensor'))
- grad_dt: float32 [1024, 24], P('dp', 'tensor')
- grad_conv_x: float32 [5, 1536], P(None, 'tensor')
- grad_conv_bc: float32 [5, 256], replicated
- grad_head: float32 [3, 24], P(None, 'tensor')
- grad_mo: float32 [1536, 1024], P('tensor', 'dp')
- grad_q: float32 [1024, 512], P('dp', 'tensor')
- grad_kv: float32 [1024, 2, 128], P('dp', None, 'tensor')
- grad_ao: float32 [512, 1024], P('tensor', 'dp')
- grad_gu: float32 [1024, 2, 2048], P('dp', None, 'tensor')
- grad_down: float32 [2048, 1024], P('tensor', 'dp')
Inputs may be any that keep to these rules, and one draw needn't show every extreme that they name: `head_params`: row 0 holds each head's time step bias, row 1 the logarithm of its decay rate, row 2 its skip coefficient.
All inputs are finite; a program needn't handle non-finite values.
Results may differ from a plain program's by a relative error of at most 0.018.
Values may be sent and summed in bfloat16 or wider, within the bound.
No kernel may reach another device: no remote copies, remote signals or barrier semaphores. Data moves between devices by JAX's collectives and lax.ppermute only.
A program may use at most 192 MiB of HBM per device.

v0:
```python
import math

import jax
import jax.numpy as jnp
from jax import lax
from jax.sharding import PartitionSpec as P

P_SIZE = 64
LEN = 1024
QROWS = 512
SBLOCK = 128


highest = lax.Precision.HIGHEST
epsilon = 1e-05
rope_base = 100000000000.0
masked_score = -1e30


def to_low(values):
    return lax.optimization_barrier(values.astype(jnp.bfloat16)).astype(jnp.float32)


def normalize(values, gain_row):
    inverse_rms = lax.rsqrt(jnp.mean(values * values, axis=-1, keepdims=True) + epsilon)
    return values * inverse_rms * gain_row


def rotary(values):
    length, head_count, head_size = values.shape
    half_size = head_size // 2
    frequency = jnp.exp(
        jnp.arange(half_size, dtype=jnp.float32) * (-2.0 * math.log(rope_base) / head_size)
    )
    angles = jnp.arange(length, dtype=jnp.float32)[:, None] * frequency[None, :]
    cosine = jnp.cos(angles)[:, None, :]
    sine_tab = jnp.sin(angles)[:, None, :]
    first_half = values[..., :half_size]
    second = values[..., half_size:]
    return jnp.concatenate(
        [first_half * cosine - second * sine_tab, second * cosine + first_half * sine_tab], axis=-1
    )


def block_probs(query_block, key_rot, block_start):
    length = key_rot.shape[0]
    head_size = key_rot.shape[-1]
    scores = jnp.einsum("qhgp,khp->hgqk", query_block, key_rot, precision=highest) * head_size ** (
        -0.5
    )
    row_ids = block_start + jnp.arange(QROWS, dtype=jnp.int32)
    columns = jnp.arange(length, dtype=jnp.int32)
    causal = row_ids[:, None] >= columns[None, :]
    scores = jnp.where(causal, scores, masked_score)
    row_max = jnp.max(scores, axis=-1, keepdims=True)
    weights = jnp.exp(scores - row_max)
    return weights / jnp.sum(weights, axis=-1, keepdims=True)


def attend_forward(query_rot, key_rot, value_low):
    length = query_rot.shape[0]

    def score_block(block_start):
        query_block = lax.dynamic_slice_in_dim(query_rot, block_start, QROWS, 0)
        probabilities = block_probs(query_block, key_rot, block_start)
        return jnp.einsum("hgqk,khp->qhgp", to_low(probabilities), value_low, precision=highest)

    starts = jnp.arange(length // QROWS, dtype=jnp.int32) * QROWS
    blocks = lax.map(score_block, starts)
    return blocks.reshape((length,) + query_rot.shape[1:])


def attend_backward(query_rot, key_rot, value_low, out_grad):
    length = query_rot.shape[0]
    head_size = key_rot.shape[-1]

    def grad_block(carry, block_start):
        key_grad, value_grad = carry
        query_block = lax.dynamic_slice_in_dim(query_rot, block_start, QROWS, 0)
        grad_block_out = lax.dynamic_slice_in_dim(out_grad, block_start, QROWS, 0)
        probabilities = block_probs(query_block, key_rot, block_start)
        value_grad = value_grad + jnp.einsum(
            "hgqk,qhgp->khp", to_low(probabilities), grad_block_out, precision=highest
        )
        prob_grad = jnp.einsum("qhgp,khp->hgqk", grad_block_out, value_low, precision=highest)
        inner_sum = jnp.sum(probabilities * prob_grad, axis=-1, keepdims=True)
        score_grad = to_low(probabilities * (prob_grad - inner_sum)) * head_size ** (-0.5)
        query_grad = jnp.einsum("hgqk,khp->qhgp", score_grad, key_rot, precision=highest)
        key_grad = key_grad + jnp.einsum(
            "hgqk,qhgp->khp", score_grad, query_block, precision=highest
        )
        return ((key_grad, value_grad), query_grad)

    starts = jnp.arange(length // QROWS, dtype=jnp.int32) * QROWS
    initial = (jnp.zeros(key_rot.shape, jnp.float32), jnp.zeros(value_low.shape, jnp.float32))
    (key_grad, value_grad), query_blocks = lax.scan(grad_block, initial, starts)
    return (query_blocks.reshape(query_rot.shape), key_grad, value_grad)


def convolve(values, tap_table):
    tap_count = tap_table.shape[0] - 1
    length = values.shape[0]
    padded = jnp.concatenate(
        [jnp.zeros((tap_count - 1, values.shape[1]), jnp.float32), values], axis=0
    )
    summed = tap_table[tap_count][None, :] + padded[0:length] * tap_table[0][None, :]
    for offset in range(1, tap_count):
        summed = summed + padded[offset : offset + length] * tap_table[offset][None, :]
    return summed


def mamba_mix(x_inner, b_and_c, step_raw, gate_z, conv_x, conv_bc, head_params):
    length = x_inner.shape[0]
    head_count = step_raw.shape[1]
    head_size = x_inner.shape[1] // head_count
    state_size = b_and_c.shape[1] // 2
    x_conv = jax.nn.silu(convolve(x_inner, conv_x)).reshape(length, head_count, head_size)
    bc_conv = jax.nn.silu(convolve(b_and_c, conv_bc))
    step_size = jax.nn.softplus(step_raw + head_params[0][None, :])
    decay_rate = step_size * (-jnp.exp(head_params[1]))[None, :]
    blocks = length // SBLOCK
    lower_mask = jnp.arange(SBLOCK)[:, None] >= jnp.arange(SBLOCK)[None, :]

    def scan_block(carried, pieces):
        x_block, b_block, c_block, step_block, decay_block = pieces
        cumulative = jnp.cumsum(decay_block, axis=0)
        spread = jnp.where(
            lower_mask[:, :, None], cumulative[:, None, :] - cumulative[None, :, :], masked_score
        )
        inner_cb = jnp.dot(c_block, b_block.T, precision=highest)
        mixing = jnp.exp(spread) * inner_cb[:, :, None] * step_block[None, :, :]
        local_out = jnp.einsum("tsh,shp->thp", mixing, x_block, precision=highest)
        carried_out = (
            jnp.einsum("tn,hpn->thp", c_block, carried, precision=highest)
            * jnp.exp(cumulative)[:, :, None]
        )
        tail_weight = jnp.exp(cumulative[-1][None, :] - cumulative) * step_block
        fresh_state = jnp.einsum("sh,shp,sn->hpn", tail_weight, x_block, b_block, precision=highest)
        updated = carried * jnp.exp(cumulative[-1])[:, None, None] + fresh_state
        return (updated, local_out + carried_out)

    pieces = (
        x_conv.reshape(blocks, SBLOCK, head_count, head_size),
        bc_conv[:, :state_size].reshape(blocks, SBLOCK, state_size),
        bc_conv[:, state_size:].reshape(blocks, SBLOCK, state_size),
        step_size.reshape(blocks, SBLOCK, head_count),
        decay_rate.reshape(blocks, SBLOCK, head_count),
    )
    initial = jnp.zeros((head_count, head_size, state_size), jnp.float32)
    final_state, outputs = lax.scan(jax.checkpoint(scan_block), initial, pieces)
    mixed = outputs.reshape(length, head_count, head_size) + head_params[2][None, :, None] * x_conv
    return mixed.reshape(length, head_count * head_size) * jax.nn.silu(gate_z)


def swiglu(gate_in, up_in):
    return jax.nn.silu(gate_in) * up_in


def rotate_all(values):
    return jax.vmap(rotary)(values)


def collect(gains, w_zx, w_bc, w_dt, w_mo, w_q, w_kv, w_ao, w_gu, w_down):
    split_full = (
        lax.all_gather(w_zx, "dp", axis=0, tiled=True),
        lax.all_gather(w_dt, "dp", axis=0, tiled=True),
        lax.all_gather(w_mo, "dp", axis=1, tiled=True),
        lax.all_gather(w_q, "dp", axis=0, tiled=True),
        lax.all_gather(w_kv, "dp", axis=0, tiled=True),
        lax.all_gather(w_ao, "dp", axis=1, tiled=True),
        lax.all_gather(w_gu, "dp", axis=0, tiled=True),
        lax.all_gather(w_down, "dp", axis=1, tiled=True),
    )
    shared_full = (
        lax.all_gather(gains, ("dp", "tensor"), axis=1, tiled=True),
        lax.all_gather(w_bc, ("dp", "tensor"), axis=0, tiled=True),
    )
    return (split_full, shared_full)


def local(
    tokens,
    gains,
    w_zx,
    w_bc,
    w_dt,
    conv_x,
    conv_bc,
    head_params,
    w_mo,
    w_q,
    w_kv,
    w_ao,
    w_gu,
    w_down,
    cotangent,
):
    split_full, shared_full = collect(gains, w_zx, w_bc, w_dt, w_mo, w_q, w_kv, w_ao, w_gu, w_down)
    zx_full, dt_full, mo_full, q_full, kv_full, ao_full, gu_full, down_full = split_full
    gain_full, bc_full = shared_full
    gain_one = gain_full[0].astype(jnp.float32)
    gain_two = gain_full[1].astype(jnp.float32)
    seg_in = tokens.astype(jnp.float32)
    normed, norm_back = jax.vjp(normalize, seg_in, gain_one)
    normed_low = normed.astype(jnp.bfloat16)
    n1_all = lax.all_gather(normed_low, "tensor", axis=0, tiled=True)
    rows_all = n1_all.shape[0]
    seq_count = rows_all // LEN
    zx_proj = jnp.einsum("td,dkc->tkc", n1_all, zx_full, preferred_element_type=jnp.float32)
    bc_proj = jnp.dot(n1_all, bc_full, preferred_element_type=jnp.float32)
    step_proj = jnp.dot(n1_all, dt_full, preferred_element_type=jnp.float32)

    def mamba_rows(x_inner, b_and_c, step_raw, gate_z, conv_x_in, conv_bc_in, head_in):

        def split_rows(array_in):
            return array_in.reshape(seq_count, LEN, array_in.shape[-1])

        mapped = jax.vmap(mamba_mix, in_axes=(0, 0, 0, 0, None, None, None))(
            split_rows(x_inner),
            split_rows(b_and_c),
            split_rows(step_raw),
            split_rows(gate_z),
            conv_x_in,
            conv_bc_in,
            head_in,
        )
        return mapped.reshape(rows_all, -1)

    gated, mamba_back = jax.vjp(
        mamba_rows, zx_proj[:, 1], bc_proj, step_proj, zx_proj[:, 0], conv_x, conv_bc, head_params
    )
    gated_low = gated.astype(jnp.bfloat16)
    query_proj = jnp.dot(n1_all, q_full, preferred_element_type=jnp.float32)
    kv_proj = jnp.einsum("td,dkc->tkc", n1_all, kv_full, preferred_element_type=jnp.float32)
    kv_local = kv_proj.shape[2] // P_SIZE
    query_local = query_proj.shape[1] // P_SIZE
    group_size = query_local // kv_local
    queries = query_proj.reshape(seq_count, LEN, query_local, P_SIZE)
    keys_in = kv_proj[:, 0].reshape(seq_count, LEN, kv_local, P_SIZE)
    values_in = kv_proj[:, 1].reshape(seq_count, LEN, kv_local, P_SIZE)
    query_rotated, query_rot_back = jax.vjp(rotate_all, queries)
    key_rotated, key_rot_back = jax.vjp(rotate_all, keys_in)
    query_rounded = to_low(query_rotated).reshape(seq_count, LEN, kv_local, group_size, P_SIZE)
    key_rounded = to_low(key_rotated)
    value_rounded = to_low(values_in)
    attended = jax.vmap(attend_forward)(query_rounded, key_rounded, value_rounded).reshape(
        rows_all, -1
    )
    attended_low = attended.astype(jnp.bfloat16)
    branch_part = jnp.dot(gated_low, mo_full, preferred_element_type=jnp.float32) + jnp.dot(
        attended_low, ao_full, preferred_element_type=jnp.float32
    )
    branch_here = lax.psum_scatter(
        branch_part.astype(jnp.bfloat16), "tensor", scatter_dimension=0, tiled=True
    ).astype(jnp.float32)
    hidden_one = seg_in + branch_here
    normed_two, norm_back_two = jax.vjp(normalize, hidden_one, gain_two)
    n2_all = lax.all_gather(normed_two.astype(jnp.bfloat16), "tensor", axis=0, tiled=True)
    gate_up = jnp.einsum("td,dkc->tkc", n2_all, gu_full, preferred_element_type=jnp.float32)
    activated, swiglu_back = jax.vjp(swiglu, gate_up[:, 0], gate_up[:, 1])
    activated_low = activated.astype(jnp.bfloat16)
    ffn_part = jnp.dot(activated_low, down_full, preferred_element_type=jnp.float32)
    ffn_here = lax.psum_scatter(
        ffn_part.astype(jnp.bfloat16), "tensor", scatter_dimension=0, tiled=True
    ).astype(jnp.float32)
    layer_out = (hidden_one + ffn_here).astype(jnp.bfloat16)
    split_full, shared_full = collect(gains, w_zx, w_bc, w_dt, w_mo, w_q, w_kv, w_ao, w_gu, w_down)
    zx_full, dt_full, mo_full, q_full, kv_full, ao_full, gu_full, down_full = split_full
    gain_full, bc_full = shared_full
    out_grad = cotangent.astype(jnp.float32)
    out_grad_all = lax.all_gather(cotangent, "tensor", axis=0, tiled=True)
    grad_down = jnp.einsum(
        "tf,td->fd", activated_low, out_grad_all, preferred_element_type=jnp.float32
    )
    grad_act = jnp.einsum("td,fd->tf", out_grad_all, down_full, preferred_element_type=jnp.float32)
    grad_gate, grad_up = swiglu_back(grad_act)
    grad_gu_low = jnp.stack([grad_gate, grad_up], axis=1).astype(jnp.bfloat16)
    grad_gu = jnp.einsum("td,tkc->dkc", n2_all, grad_gu_low, preferred_element_type=jnp.float32)
    n2_grad_part = jnp.einsum(
        "tkc,dkc->td", grad_gu_low, gu_full, preferred_element_type=jnp.float32
    )
    n2_grad = lax.psum_scatter(
        n2_grad_part.astype(jnp.bfloat16), "tensor", scatter_dimension=0, tiled=True
    ).astype(jnp.float32)
    hidden_grad_norm, gain_two_grad = norm_back_two(n2_grad)
    hidden_grad = out_grad + hidden_grad_norm
    branch_grad_all = lax.all_gather(hidden_grad.astype(jnp.bfloat16), "tensor", axis=0, tiled=True)
    grad_mo = jnp.einsum(
        "tc,td->cd", gated_low, branch_grad_all, preferred_element_type=jnp.float32
    )
    grad_ao = jnp.einsum(
        "tc,td->cd", attended_low, branch_grad_all, preferred_element_type=jnp.float32
    )
    gated_grad = jnp.einsum(
        "td,cd->tc", branch_grad_all, mo_full, preferred_element_type=jnp.float32
    )
    attended_grad = jnp.einsum(
        "td,cd->tc", branch_grad_all, ao_full, preferred_element_type=jnp.float32
    )
    x_grad, bc_grad_part, step_grad, z_grad, grad_conv_x, grad_conv_bc, grad_head = mamba_back(
        gated_grad
    )
    attended_grad_heads = attended_grad.reshape(seq_count, LEN, kv_local, group_size, P_SIZE)
    rot_query_grad, rot_key_grad, value_grad = jax.vmap(attend_backward)(
        query_rounded, key_rounded, value_rounded, attended_grad_heads
    )
    query_grad = query_rot_back(rot_query_grad.reshape(seq_count, LEN, query_local, P_SIZE))[
        0
    ].reshape(rows_all, -1)
    key_grad = key_rot_back(rot_key_grad)[0].reshape(rows_all, -1)
    kv_grad = jnp.stack([key_grad, value_grad.reshape(rows_all, -1)], axis=1)
    zx_grad_low = jnp.stack([z_grad, x_grad], axis=1).astype(jnp.bfloat16)
    step_grad_low = step_grad.astype(jnp.bfloat16)
    query_grad_low = query_grad.astype(jnp.bfloat16)
    kv_grad_low = kv_grad.astype(jnp.bfloat16)
    grad_zx = jnp.einsum("td,tkc->dkc", n1_all, zx_grad_low, preferred_element_type=jnp.float32)
    grad_dt = jnp.einsum("td,th->dh", n1_all, step_grad_low, preferred_element_type=jnp.float32)
    grad_q = jnp.einsum("td,tc->dc", n1_all, query_grad_low, preferred_element_type=jnp.float32)
    grad_kv = jnp.einsum("td,tkc->dkc", n1_all, kv_grad_low, preferred_element_type=jnp.float32)
    n1_grad_part = jnp.einsum(
        "tkc,dkc->td", zx_grad_low, zx_full, preferred_element_type=jnp.float32
    )
    n1_grad_part = n1_grad_part + jnp.einsum(
        "th,dh->td", step_grad_low, dt_full, preferred_element_type=jnp.float32
    )
    n1_grad_part = n1_grad_part + jnp.einsum(
        "tc,dc->td", query_grad_low, q_full, preferred_element_type=jnp.float32
    )
    n1_grad_part = n1_grad_part + jnp.einsum(
        "tkc,dkc->td", kv_grad_low, kv_full, preferred_element_type=jnp.float32
    )
    bc_grad_here = lax.psum_scatter(
        bc_grad_part.astype(jnp.bfloat16), "tensor", scatter_dimension=0, tiled=True
    )
    grad_bc = jnp.einsum("td,tn->dn", normed_low, bc_grad_here, preferred_element_type=jnp.float32)
    n1_grad = lax.psum_scatter(
        n1_grad_part.astype(jnp.bfloat16), "tensor", scatter_dimension=0, tiled=True
    ).astype(jnp.float32)
    n1_grad = n1_grad + jnp.einsum(
        "tn,dn->td", bc_grad_here, bc_full, preferred_element_type=jnp.float32
    )
    seg_grad, gain_one_grad = norm_back(n1_grad)
    input_grad = (hidden_grad + seg_grad).astype(jnp.bfloat16)
    grad_zx, grad_dt, grad_mo, grad_q, grad_kv, grad_ao, grad_gu, grad_down = (
        lax.psum_scatter(grad_zx, "dp", scatter_dimension=0, tiled=True),
        lax.psum_scatter(grad_dt, "dp", scatter_dimension=0, tiled=True),
        lax.psum_scatter(grad_mo, "dp", scatter_dimension=1, tiled=True),
        lax.psum_scatter(grad_q, "dp", scatter_dimension=0, tiled=True),
        lax.psum_scatter(grad_kv, "dp", scatter_dimension=0, tiled=True),
        lax.psum_scatter(grad_ao, "dp", scatter_dimension=1, tiled=True),
        lax.psum_scatter(grad_gu, "dp", scatter_dimension=0, tiled=True),
        lax.psum_scatter(grad_down, "dp", scatter_dimension=1, tiled=True),
    )
    gain_grads = jnp.stack([gain_one_grad, gain_two_grad], axis=0)
    grad_gains, grad_bc = (
        lax.psum_scatter(gain_grads, ("dp", "tensor"), scatter_dimension=1, tiled=True),
        lax.psum_scatter(grad_bc, ("dp", "tensor"), scatter_dimension=0, tiled=True),
    )
    tensor_index = lax.axis_index("tensor")
    tensor_count = lax.axis_size("tensor")
    conv_cols = conv_x.shape[1]
    head_cols = head_params.shape[1]
    conv_wide = jnp.zeros((conv_x.shape[0], conv_cols * tensor_count), jnp.float32)
    conv_wide = lax.dynamic_update_slice_in_dim(conv_wide, grad_conv_x, tensor_index * conv_cols, 1)
    head_wide = jnp.zeros((head_params.shape[0], head_cols * tensor_count), jnp.float32)
    head_wide = lax.dynamic_update_slice_in_dim(head_wide, grad_head, tensor_index * head_cols, 1)
    conv_total, conv_bc_total, head_total = lax.psum(
        (conv_wide, grad_conv_bc, head_wide), ("dp", "tensor")
    )
    grad_conv_x = lax.dynamic_slice_in_dim(conv_total, tensor_index * conv_cols, conv_cols, 1)
    grad_head = lax.dynamic_slice_in_dim(head_total, tensor_index * head_cols, head_cols, 1)
    return (
        layer_out,
        input_grad,
        grad_gains,
        grad_zx,
        grad_bc,
        grad_dt,
        grad_conv_x,
        conv_bc_total,
        grad_head,
        grad_mo,
        grad_q,
        grad_kv,
        grad_ao,
        grad_gu,
        grad_down,
    )


def solution(mesh):
    placed = (
        P(("dp", "tensor"), None),
        P(None, ("dp", "tensor")),
        P("dp", None, "tensor"),
        P(("dp", "tensor"), None),
        P("dp", "tensor"),
        P(None, "tensor"),
        P(),
        P(None, "tensor"),
        P("tensor", "dp"),
        P("dp", "tensor"),
        P("dp", None, "tensor"),
        P("tensor", "dp"),
        P("dp", None, "tensor"),
        P("tensor", "dp"),
        P(("dp", "tensor"), None),
    )
    return jax.shard_map(
        local,
        mesh=mesh,
        in_specs=placed,
        out_specs=(
            P(("dp", "tensor"), None),
            P(("dp", "tensor"), None),
            P(None, ("dp", "tensor")),
            P("dp", None, "tensor"),
            P(("dp", "tensor"), None),
            P("dp", "tensor"),
            P(None, "tensor"),
            P(),
            P(None, "tensor"),
            P("tensor", "dp"),
            P("dp", "tensor"),
            P("dp", None, "tensor"),
            P("tensor", "dp"),
            P("dp", None, "tensor"),
            P("tensor", "dp"),
        ),
        check_vma=False,
    )
```

profile of v0, /device:TPU:0, one launch (start us, length us, event | category | flops | bytes accessed | tf_op | source)
XLA Modules:
  0.0 2112.3 jit_solution(3943206018281027327)
XLA Ops:
  7.3 69.6 %all-gather = bf16[32,32,2]{1,2,0:T(2,128)(2,1)S(1)} all-gather(bf16[1,32,2]{1,2,0:T(2,128)(2,1)} %bitcast.923), channel_id=1, replica_groups=mesh['dp'=16,'tensor'=2] {'dp','tensor'}, dimensions={0}, use_global_device_ids=true | all-gather | bytes 4224 | tf_op jit(solution)/shard_map/all_gather | solution.py:175
  83.9 72.4 %all_gather.55 = bf16[1024,256]{1,0:T(8,128)(2,1)} all-gather(bf16[32,256]{1,0:T(8,128)(2,1)S(1)} %copy-done.86), channel_id=1, replica_groups=mesh['dp'=16,'tensor'=2] {'dp','tensor'}, dimensions={0}, use_global_device_ids=true | all-gather | bytes 540672 | tf_op jit(solution)/shard_map/all_gather | solution.py:176
  253.1 41.9 %while.69 = (s32[]{:T(128)}, bf16[2,1,512,1,4,64]{2,5,4,3,1,0:T(8,128)(2,1)S(1)}, s32[2]{0:T(128)S(1)}, f32[1,1024,1,4,64]{1,4,3,2,0:T(8,128)S(1)}, f32[1,1024,1...) while((s32[]{:T(128)}, ...), condition=%wide.region_7.8_spmd, body=%wide.region_4.7_spmd.sunk | while | flops 3246912000 | bytes 37270216 | solution.py:69
  322.5 84.8 %while.70 = (s32[]{:T(128)}, f32[1,12,64,128]{3,2,1,0:T(8,128)S(1)}, f32[8,1,128,12,64]{2,4,3,1,0:T(8,128)}, f32[8,1,12,64,128]{4,3,2,1,0:T(8,128)}, f32[8,1,128...) while((s32[]{:T(128)}, ...), condition=%wide.region_3.4_spmd.clone, body=%wide.region_1.3_spmd.clone.sunk | while | flops 479921664 | bytes 4487605 | solution.py:150
  434.4 29.8 %reduce-scatter.20.cloned.1.call-done = bf16[512,1024]{1,0:T(8,128)(2,1)} async-done(((bf16[1024,1024]{1,0:T(8,128)(2,1)}), bf16[512,1024]{1,0:T(8,128)(2,1)}) %reduce-scatter.20.cloned.1.call-update) | async-done | bytes 1048592 | tf_op jit(solution)/shard_map/reduce_scatter | solution.py:253
  470.0 47.6 %all-gather.19.cloned.1.call-done = bf16[1024,2,1024]{2,0,1:T(8,128)(2,1)} async-done(((bf16[64,2,1024]{2,0,1:T(8,128)(2,1)}), bf16[1024,2,1024]{2,0,1:T(8,128)(2,1)}) %all-gather.19.cloned.1.call-update) | async-done | bytes 4194320 | tf_op jit(solution)/shard_map/all_gather | solution.py:171
  517.6 33.1 %all-gather.17.cloned.1.call-done = bf16[1024,1024]{1,0:T(8,128)(2,1)} async-done(((bf16[512,1024]{1,0:T(8,128)(2,1)}), bf16[1024,1024]{1,0:T(8,128)(2,1)}) %all-gather.17.cloned.1.call-update) | async-done | bytes 2097168 | tf_op jit(solution)/shard_map/all_gather | solution.py:258
  561.6 23.9 %all-gather.23.cloned.1.call-done = bf16[1024,1024]{1,0:T(8,128)(2,1)} async-done(((bf16[512,1024]{1,0:T(8,128)(2,1)}), bf16[1024,1024]{1,0:T(8,128)(2,1)}) %all-gather.23.cloned.1.call-update) | async-done | bytes 2097168 | tf_op jit(solution)/shard_map/all_gather | solution.py:271
  585.5 43.8 %all-gather.21.cloned.1.call-done = bf16[1024,1024]{0,1:T(8,128)(2,1)} async-done(((bf16[1024,64]{0,1:T(8,128)(2,1)}), bf16[1024,1024]{0,1:T(8,128)(2,1)}) %all-gather.21.cloned.1.call-update) | async-done | bytes 2097168 | tf_op jit(solution)/shard_map/all_gather | solution.py:172
  647.3 30.5 %reduce-scatter.24.cloned.1.call-done = bf16[512,1024]{1,0:T(8,128)(2,1)} async-done(((bf16[1024,1024]{1,0:T(8,128)(2,1)}), bf16[512,1024]{1,0:T(8,128)(2,1)}) %reduce-scatter.24.cloned.1.call-update) | async-done | bytes 1048592 | tf_op jit(solution)/shard_map/reduce_scatter | solution.py:282
  694.6 22.9 %all-gather.25.cloned.1.call-done = bf16[1024,1024]{1,0:T(8,128)(2,1)} async-done(((bf16[512,1024]{1,0:T(8,128)(2,1)}), bf16[1024,1024]{1,0:T(8,128)(2,1)}) %all-gather.25.cloned.1.call-update) | async-done | bytes 2097168 | tf_op jit(solution)/shard_map/all_gather | solution.py:287
  719.9 150.5 %while.72 = (s32[]{:T(128)}, f32[1,1024,1,64]{1,3,2,0:T(8,128)}, f32[1,1024,1,64]{1,3,2,0:T(8,128)}, f32[2,1,512,1,4,64]{2,0,5,4,3,1:T(2,128)}, s32[2]{0:T(128)S...) while((s32[]{:T(128)}, f32[1,1024,1,64]{1,3,2,0:T(8,128)}, ...), condition=%wide.region_28.29_spmd.clone, body=%wide.region_24.28_spmd.clone.sunk | while | flops 8106273280 | bytes 118307232 | solution.py:96
  892.9 235.5 %while.71 = (s32[]{:T(128)}, f32[1,12,64,128]{3,2,1,0:T(8,128)S(1)}, f32[8,1,128,12,64]{2,0,4,3,1:T(8,128)}, f32[8,1,128,128]{3,2,0,1:T(8,128)S(1)}, f32[8,1,128...) while((s32[]{:T(128)}, ...), condition=%wide.region_23.24_spmd.clone, body=%wide.region_13.23_spmd.clone.sunk | while | flops 1137625088 | bytes 13697935 | solution.py:150
  1265.1 40.2 %all-reduce.31 = (f32[5,1536]{1,0:T(8,128)S(1)}, f32[5,256]{1,0:T(8,128)}, f32[3,24]{1,0:T(4,128)S(1)}) all-reduce(f32[5,1536]{1,0:T(8,128)S(1)} %add_dynamic-update-slice_fusion, f32[5,256]{1,0:T(8,128)S(1)} %pad_add_fusion.6, f32[3,24]{1,0:T(4,128)S(1)} %dynamic_update_slice.73), channel_id=1, replica_groups=mesh['dp'=16,'tensor'=2] {'dp','tensor'}, use_global_device_ids=true, to_apply=%region_43.44 | all-reduce | flops 9032 | bytes 72256 | tf_op jit(solution)/shard_map/psum | solution.py:367
  1308.0 31.6 %reduce-scatter.38.cloned.1.call-done = f32[64,2,64]{2,0,1:T(8,128)} async-done(((f32[1024,2,64]{2,0,1:T(8,128)}), f32[64,2,64]{2,0,1:T(8,128)}) %reduce-scatter.38.cloned.1.call-update) | async-done | bytes 32784 | tf_op jit(solution)/shard_map/reduce_scatter | solution.py:349
  1341.2 31.4 %reduce-scatter.22.cloned.1.call-done = bf16[512,1024]{1,0:T(8,128)(2,1)} async-done(((bf16[1024,1024]{1,0:T(8,128)(2,1)}), bf16[512,1024]{1,0:T(8,128)(2,1)}) %reduce-scatter.22.cloned.1.call-update) | async-done | bytes 1048592 | tf_op jit(solution)/shard_map/reduce_scatter | solution.py:263
  1376.9 132.6 %reduce-scatter.46.cloned.1.call-done = f32[32,2]{1,0:T(8,128)} async-done(((f32[1024,2]{1,0:T(8,128)}), f32[32,2]{1,0:T(8,128)}) %reduce-scatter.46.cloned.1.call-update) | async-done | bytes 272
  1510.8 103.1 %reduce-scatter.42.cloned.1.call-done = f32[64,2,1024]{2,0,1:T(8,128)} async-done(((f32[1024,2,1024]{2,0,1:T(8,128)}), f32[64,2,1024]{2,0,1:T(8,128)}) %reduce-scatter.42.cloned.1.call-update) | async-done | bytes 524304 | tf_op jit(solution)/shard_map/reduce_scatter | solution.py:351
  1616.2 86.5 %reduce-scatter.30.cloned.1.call-done = f32[64,2,768]{2,0,1:T(8,128)} async-done(((f32[1024,2,768]{2,0,1:T(8,128)}), f32[64,2,768]{2,0,1:T(8,128)}) %reduce-scatter.30.cloned.1.call-update) | async-done | bytes 393232 | tf_op jit(solution)/shard_map/reduce_scatter | solution.py:345
  1704.8 74.8 %reduce-scatter.44.cloned.1.call-done = f32[1024,64]{0,1:T(8,128)} async-done(((f32[1024,1024]{0,1:T(8,128)}), f32[1024,64]{0,1:T(8,128)}) %reduce-scatter.44.cloned.1.call-update) | async-done | bytes 262160 | tf_op jit(solution)/shard_map/reduce_scatter | solution.py:352
  1779.6 60.5 %reduce-scatter.36.cloned.1.call-done = f32[64,256]{1,0:T(8,128)} async-done(((f32[1024,256]{1,0:T(8,128)}), f32[64,256]{1,0:T(8,128)}) %reduce-scatter.36.cloned.1.call-update) | async-done | bytes 65552 | tf_op jit(solution)/shard_map/reduce_scatter | solution.py:348
  1840.1 61.1 %reduce-scatter.40.cloned.1.call-done = f32[256,64]{0,1:T(8,128)} async-done(((f32[256,1024]{0,1:T(8,128)}), f32[256,64]{0,1:T(8,128)}) %reduce-scatter.40.cloned.1.call-update) | async-done | bytes 65552 | tf_op jit(solution)/shard_map/reduce_scatter | solution.py:350
  1901.2 137.1 %reduce-scatter.32.cloned.1.call-done = f32[32,256]{1,0:T(8,128)} async-done(((f32[1024,256]{1,0:T(8,128)}), f32[32,256]{1,0:T(8,128)}) %reduce-scatter.32.cloned.1.call-update) | async-done | bytes 32784 | tf_op jit(solution)/shard_map/reduce_scatter | solution.py:357
  2038.4 67.2 %reduce-scatter.34.cloned.1.call-done = f32[768,64]{0,1:T(8,128)} async-done(((f32[768,1024]{0,1:T(8,128)}), f32[768,64]{0,1:T(8,128)}) %reduce-scatter.34.cloned.1.call-update) | async-done | bytes 196624 | tf_op jit(solution)/shard_map/reduce_scatter | solution.py:347
  (919 shorter events, 860.3 us)
Async XLA Ops:
  7.3 231.6 %all-gather.11.cloned.1.call-start = ((), (), s32[]{:S(2)}) async-start(), calls=%async_computation.15 | async-start | bytes 3145728 | tf_op jit(solution)/shard_map/all_gather | solution.py:206
  77.0 604.1 %copy-start.57 = (f32[1,1024]{1,0:T(1,128)}, f32[1,1024]{1,0:T(1,128)S(1)}, u32[]{:S(2)}) copy-start(f32[1,1024]{1,0:T(1,128)S(1)} %get-tuple-element.982) | copy-start | bytes 12292
  81.1 214.6 %all-gather.13.cloned.1.call-start = ((), (), s32[]{:S(2)}) async-start(), calls=%async_computation.16 | async-start | bytes 3342336 | tf_op jit(solution)/shard_map/all_gather | solution.py:165
  81.9 345.7 %all-gather.15.cloned.1.call-start = ((), (), s32[]{:S(2)}) async-start(), calls=%async_computation.17 | async-start | bytes 1671168 | tf_op jit(solution)/shard_map/all_gather | solution.py:167
  82.6 381.6 %reduce-scatter.20.cloned.1.call-start = ((), (), s32[]{:S(2)}) async-start(), calls=%async_computation.18 | async-start | bytes 3145728 | tf_op jit(solution)/shard_map/reduce_scatter | solution.py:253
  433.5 84.1 %all-gather.19.cloned.1.call-start = ((), (), s32[]{:S(2)}) async-start(), calls=%async_computation.20 | async-start | bytes 4456448 | tf_op jit(solution)/shard_map/all_gather | solution.py:171
  434.4 116.4 %all-gather.17.cloned.1.call-start = ((), (), s32[]{:S(2)}) async-start(), calls=%async_computation.19 | async-start | bytes 3145728 | tf_op jit(solution)/shard_map/all_gather | solution.py:258
  468.5 117.0 %all-gather.23.cloned.1.call-start = ((), (), s32[]{:S(2)}) async-start(), calls=%async_computation.23 | async-start | bytes 3145728 | tf_op jit(solution)/shard_map/all_gather | solution.py:271
  469.3 160.1 %all-gather.21.cloned.1.call-start = ((), (), s32[]{:S(2)}) async-start(), calls=%async_computation.21 | async-start | bytes 2228224 | tf_op jit(solution)/shard_map/all_gather | solution.py:172
  470.0 207.8 %reduce-scatter.24.cloned.1.call-start = ((), (), s32[]{:S(2)}) async-start(), calls=%async_computation.24 | async-start | bytes 3145728 | tf_op jit(solution)/shard_map/reduce_scatter | solution.py:282
  647.1 70.4 %all-gather.25.cloned.1.call-start = ((), (), s32[]{:S(2)}) async-start(), calls=%async_computation.25 | async-start | bytes 3145728 | tf_op jit(solution)/shard_map/all_gather | solution.py:287
  684.2 512.8 %reduce-scatter.28.cloned.1.call-start = ((), (), s32[]{:S(2)}) async-start(), calls=%async_computation.27 | async-start | bytes 786432 | tf_op jit(solution)/shard_map/reduce_scatter | solution.py:332
  1169.0 50.3 %reduce-scatter.26.cloned.1.call-start = ((), (), s32[]{:S(2)}) async-start(), calls=%async_computation.26 | async-start | bytes 3145728 | tf_op jit(solution)/shard_map/reduce_scatter | solution.py:336
  1187.2 119.3 %reduce-scatter.48.cloned.1.call-start = ((), (), s32[]{:S(2)}) async-start(), calls=%async_computation.37 | async-start | bytes 557056
  1188.9 150.8 %reduce-scatter.38.cloned.1.call-start = ((), (), s32[]{:S(2)}) async-start(), calls=%async_computation.32 | async-start | bytes 1114112 | tf_op jit(solution)/shard_map/reduce_scatter | solution.py:349
  1190.9 181.7 %reduce-scatter.22.cloned.1.call-start = ((), (), s32[]{:S(2)}) async-start(), calls=%async_computation.22 | async-start | bytes 3145728 | tf_op jit(solution)/shard_map/reduce_scatter | solution.py:263
  1197.0 312.5 %reduce-scatter.46.cloned.1.call-start = ((), (), s32[]{:S(2)}) async-start(), calls=%async_computation.36 | async-start | bytes 540672
  1224.1 389.8 %reduce-scatter.42.cloned.1.call-start = ((), (), s32[]{:S(2)}) async-start(), calls=%async_computation.34 | async-start | bytes 8912896 | tf_op jit(solution)/shard_map/reduce_scatter | solution.py:351
  1234.9 467.8 %reduce-scatter.30.cloned.1.call-start = ((), (), s32[]{:S(2)}) async-start(), calls=%async_computation.28 | async-start | bytes 6684672 | tf_op jit(solution)/shard_map/reduce_scatter | solution.py:345
  1242.3 537.3 %reduce-scatter.44.cloned.1.call-start = ((), (), s32[]{:S(2)}) async-start(), calls=%async_computation.35 | async-start | bytes 4456448 | tf_op jit(solution)/shard_map/reduce_scatter | solution.py:352
  1249.0 591.1 %reduce-scatter.36.cloned.1.call-start = ((), (), s32[]{:S(2)}) async-start(), calls=%async_computation.31 | async-start | bytes 1114112 | tf_op jit(solution)/shard_map/reduce_scatter | solution.py:348
  1252.1 649.1 %reduce-scatter.40.cloned.1.call-start = ((), (), s32[]{:S(2)}) async-start(), calls=%async_computation.33 | async-start | bytes 1114112 | tf_op jit(solution)/shard_map/reduce_scatter | solution.py:350
  1255.9 782.4 %reduce-scatter.32.cloned.1.call-start = ((), (), s32[]{:S(2)}) async-start(), calls=%async_computation.29 | async-start | bytes 1081344 | tf_op jit(solution)/shard_map/reduce_scatter | solution.py:357
  1257.5 848.0 %reduce-scatter.34.cloned.1.call-start = ((), (), s32[]{:S(2)}) async-start(), calls=%async_computation.30 | async-start | bytes 3342336 | tf_op jit(solution)/shard_map/reduce_scatter | solution.py:347
  (124 other events, 3873.9 us)
Sparse Core Ops, SparseCore 0:
  81.2 32.8 all-gather.10
  117.0 45.3 all-gather.12
  164.6 39.3 all-gather.14
  433.6 30.5 reduce-scatter.19
  467.0 50.5 all-gather.18
  519.1 31.5 all-gather.16
  552.4 33.1 all-gather.22
  587.9 41.3 all-gather.20
  647.2 30.5 reduce-scatter.23
  684.3 33.1 all-gather.24
  1169.1 14.5 reduce-scatter.27
  1187.3 31.9 reduce-scatter.25
  1222.9 55.7 reduce-scatter.47
  1283.2 56.4 reduce-scatter.37
  1341.7 30.8 reduce-scatter.21
  1375.3 134.1 reduce-scatter.45
  1513.4 100.4 reduce-scatter.41
  1617.7 84.9 reduce-scatter.29
  1707.6 71.8 reduce-scatter.43
  1783.6 56.4 reduce-scatter.35
  1844.8 56.4 reduce-scatter.39
  1904.0 134.2 reduce-scatter.31
  2043.2 62.2 reduce-scatter.33
where the time goes:
time: 2130 us; the launch traced here: 2110 us
  waiting for transfers between devices  1040 us (49%)
  matrix products  338 us (16%)
  local copies, waits for them, and re-layouts  292 us (14%)
  blocking collectives  261 us (12%)
  other arithmetic  126 us (6%)
  loops' own time  36.4 us (2%)
    reduce_scatter x1, waiting for transfers between devices, local(): lax.psum_scatter(grad_bc, ('dp', 'tensor'), scatter_dimension=0, tiled=True)  137 us
    unnamed x25, waiting for transfers between devices  135 us
    reduce_scatter x1, waiting for transfers between devices, local(): lax.psum_scatter(grad_gu, 'dp', scatter_dimension=0, tiled=True)  103 us
    dynamic_update_slice x24, local copies, waits for them, and re-layouts, mamba_mix(): final_state, outputs = lax.scan(jax.checkpoint(scan_block), initial, pieces)  88.6 us
    reduce_scatter x1, waiting for transfers between devices, local(): lax.psum_scatter(grad_zx, 'dp', scatter_dimension=0, tiled=True)  86.5 us
    reduce_scatter x1, waiting for transfers between devices, local(): lax.psum_scatter(grad_down, 'dp', scatter_dimension=1, tiled=True)  74.8 us
    all_gather x1, blocking collectives, collect(): lax.all_gather(w_bc, ('dp', 'tensor'), axis=0, tiled=True)  72.4 us
    all_gather x1, blocking collectives, collect(): lax.all_gather(gains, ('dp', 'tensor'), axis=1, tiled=True)  69.6 us
  transfers between devices with their start and end apart: 23, of which 18 were waited for; matrix products, arithmetic and copies ran while one was open for 14% of the time, Pallas kernels for 0%

commit v1 on v0

v1 whole, which is shorter than its diff:
```python
import math

import jax
import jax.numpy as jnp
from jax import lax
from jax.experimental import pallas as pl
from jax.experimental.pallas import tpu as pltpu
from jax.sharding import PartitionSpec as P

P_SIZE = 64
LEN = 1024
CHUNK = 128
LANES = 128
QBLOCK = 256
HEAD_ROWS = 16

highest = lax.Precision.HIGHEST
epsilon = 1e-05
rope_base = 100000000000.0
masked_score = -1e30
f32 = jnp.float32
bf16 = jnp.bfloat16

NN = (((1,), (0,)), ((), ()))
NT = (((1,), (1,)), ((), ()))
TN = (((0,), (0,)), ((), ()))


def mm(left, right, dims=NN):
    return lax.dot_general(left, right, dims, preferred_element_type=f32)


def mm_exact(left, right, dims=NN):
    return lax.dot_general(left, right, dims, precision=highest, preferred_element_type=f32)


def low_lanes(shape):
    return lax.broadcasted_iota(jnp.int32, shape, 1) < P_SIZE


def softplus(values):
    return jnp.maximum(values, 0.0) + jnp.log1p(jnp.exp(-jnp.abs(values)))


def sigmoid(values):
    return 1.0 / (1.0 + jnp.exp(-values))


def at_or_after():
    rows = lax.broadcasted_iota(jnp.int32, (CHUNK, CHUNK), 0)
    columns = lax.broadcasted_iota(jnp.int32, (CHUNK, CHUNK), 1)
    return rows, columns


def convolved(ext_ref, taps_ref):
    taps = taps_ref.shape[0] - 1
    total = taps_ref[taps : taps + 1, :] + ext_ref[5 : 5 + CHUNK, :] * taps_ref[0:1, :]
    for k in range(1, taps):
        total = total + ext_ref[5 + k : 5 + k + CHUNK, :] * taps_ref[k : k + 1, :]
    return total


def pair_columns(table, pair):
    low = low_lanes((table.shape[0], LANES))
    return jnp.where(low, table[:, 2 * pair : 2 * pair + 1], table[:, 2 * pair + 1 : 2 * pair + 2])


def split_heads(values):
    low = low_lanes(values.shape)
    zero = jnp.zeros_like(values)
    return jnp.concatenate([jnp.where(low, values, zero), jnp.where(low, zero, values)], axis=0)


def mixer_forward_kernel(
    z_ref, u_ref, bc_ref, dr_ref, cx_ref, cbc_ref, hp_ref, g_ref, y_ref, h_ref, state, ext_u, ext_bc
):
    chunks = LEN // CHUNK
    first = lax.rem(pl.program_id(0), chunks) == 0
    pairs = u_ref.shape[1] // LANES
    states = bc_ref.shape[1] // 2

    @pl.when(first)
    def _():
        state[...] = jnp.zeros_like(state)
        ext_u[0:8, :] = jnp.zeros_like(ext_u[0:8, :])
        ext_bc[0:8, :] = jnp.zeros_like(ext_bc[0:8, :])

    @pl.when(jnp.logical_not(first))
    def _():
        ext_u[0:8, :] = ext_u[CHUNK : CHUNK + 8, :]
        ext_bc[0:8, :] = ext_bc[CHUNK : CHUNK + 8, :]

    ext_u[8 : 8 + CHUNK, :] = u_ref[...]
    ext_bc[8 : 8 + CHUNK, :] = bc_ref[...]
    v_x = convolved(ext_u, cx_ref)
    x = v_x * sigmoid(v_x)
    v_bc = convolved(ext_bc, cbc_ref)
    sc = (v_bc * sigmoid(v_bc)).astype(bf16)
    b_low, c_low = sc[:, :states], sc[:, states:]
    step = softplus(dr_ref[...] + hp_ref[0:1, :])
    decay = -step * jnp.exp(hp_ref[1:2, :])
    rows, columns = at_or_after()
    causal = rows >= columns
    cum = mm_exact(causal.astype(f32), decay)
    cum_t = cum.T
    inner = mm(c_low, b_low, NT)
    held = state[...]
    held_low = held.astype(bf16)
    h_ref[...] = held_low
    carried = mm(c_low, held_low)
    z = z_ref[...]
    gate = z * sigmoid(z)
    fresh = []
    for pair in range(pairs):
        at = slice(pair * LANES, (pair + 1) * LANES)
        x_pair = x[:, at]
        cum_pair = pair_columns(cum, pair)
        last = cum_pair[CHUNK - 1 : CHUNK, :]
        x_step = x_pair * pair_columns(step, pair)
        mixing = []
        for head in (2 * pair, 2 * pair + 1):
            spread = cum[:, head : head + 1] - cum_t[head : head + 1, :]
            mixing.append((jnp.exp(jnp.where(causal, spread, masked_score)) * inner).astype(bf16))
        out = mm(jnp.concatenate(mixing, axis=1), split_heads(x_step.astype(bf16)))
        out = out + carried[:, at] * jnp.exp(cum_pair)
        out = out + pair_columns(hp_ref[2:3, :], pair) * x_pair
        y_ref[:, at] = out.astype(bf16)
        g_ref[:, at] = (out * gate[:, at]).astype(bf16)
        fresh.append((x_step * jnp.exp(last - cum_pair)).astype(bf16))
        held_scale = jnp.exp(last)
        state[:, at] = held[:, at] * held_scale
    state[...] += mm(b_low, jnp.concatenate(fresh, axis=1), TN)


def mixer_backward_kernel(
    z_ref,
    u_ref,
    bc_ref,
    dr_ref,
    u_before_ref,
    bc_before_ref,
    y_ref,
    dg_ref,
    h_ref,
    att_ref,
    cx_ref,
    cbc_ref,
    hp_ref,
    hpt_ref,
    dproj_ref,
    wide_ref,
    bc_acc_ref,
    head_ref,
    state,
    ext_u,
    ext_bc,
    after_u,
    after_bc,
    da_rows,
):
    chunks = LEN // CHUNK
    step_id = pl.program_id(0)
    within = lax.rem(step_id, chunks)
    inner_cols = u_ref.shape[1]
    bc_cols = bc_ref.shape[1]
    pairs = inner_cols // LANES
    states = bc_cols // 2
    taps = cx_ref.shape[0] - 1

    @pl.when(step_id == 0)
    def _():
        wide_ref[...] = jnp.zeros_like(wide_ref)
        bc_acc_ref[...] = jnp.zeros_like(bc_acc_ref)
        head_ref[...] = jnp.zeros_like(head_ref)
        da_rows[...] = jnp.zeros_like(da_rows)

    @pl.when(within == 0)
    def _():
        state[...] = jnp.zeros_like(state)
        after_u[CHUNK:, :] = jnp.zeros_like(after_u[CHUNK:, :])
        after_bc[CHUNK:, :] = jnp.zeros_like(after_bc[CHUNK:, :])

    @pl.when(within > 0)
    def _():
        after_u[CHUNK:, :] = after_u[0:8, :]
        after_bc[CHUNK:, :] = after_bc[0:8, :]

    is_start = within == chunks - 1
    ext_u[0:8, :] = jnp.where(is_start, 0.0, u_before_ref[...])
    ext_bc[0:8, :] = jnp.where(is_start, 0.0, bc_before_ref[...])
    ext_u[8 : 8 + CHUNK, :] = u_ref[...]
    ext_bc[8 : 8 + CHUNK, :] = bc_ref[...]
    v_x = convolved(ext_u, cx_ref)
    sig_x = sigmoid(v_x)
    x = v_x * sig_x
    v_bc = convolved(ext_bc, cbc_ref)
    sig_bc = sigmoid(v_bc)
    sc = (v_bc * sig_bc).astype(bf16)
    b_low, c_low = sc[:, :states], sc[:, states:]
    raw = dr_ref[...]
    step = softplus(raw + hp_ref[0:1, :])
    decay = -step * jnp.exp(hp_ref[1:2, :])
    rows, columns = at_or_after()
    causal = rows >= columns
    cum = mm_exact(causal.astype(f32), decay)
    cum_t = cum.T
    inner_t = mm(b_low, c_low, NT)
    held_low = h_ref[...]
    carried = mm(c_low, held_low)
    next_grad = state[...]
    next_low = next_grad.astype(bf16)
    from_next = mm(b_low, next_low)
    z = z_ref[...]
    sig_z = sigmoid(z)
    gate = z * sig_z
    dg = dg_ref[...].astype(f32)
    dproj_ref[:, 0:inner_cols] = (
        dg * y_ref[...].astype(f32) * (sig_z * (1.0 + z * (1.0 - sig_z)))
    ).astype(bf16)
    dy = dg * gate
    later = rows <= columns
    reaches = causal.astype(bf16)
    inner_grad = jnp.zeros((CHUNK, CHUNK), f32)
    carry_terms, tail_terms, step_terms, dye_parts, xw_parts, held_terms = [], [], [], [], [], []
    for pair in range(pairs):
        at = slice(pair * LANES, (pair + 1) * LANES)
        x_pair = x[:, at]
        dy_pair = dy[:, at]
        cum_pair = pair_columns(cum, pair)
        last = cum_pair[CHUNK - 1 : CHUNK, :]
        step_pair = pair_columns(step, pair)
        x_step = x_pair * step_pair
        dy_low = dy_pair.astype(bf16)
        both = mm(split_heads(x_step.astype(bf16)), dy_low, NT)
        mixing, products = [], []
        for part, head in enumerate((2 * pair, 2 * pair + 1)):
            spread = cum_t[head : head + 1, :] - cum[:, head : head + 1]
            decayed = jnp.exp(jnp.where(later, spread, masked_score))
            grad_part = decayed * both[part * CHUNK : (part + 1) * CHUNK, :]
            inner_grad = inner_grad + grad_part
            products.append((grad_part * inner_t).astype(bf16))
            mixing.append((decayed * inner_t).astype(bf16))
        reach = mm(jnp.concatenate(products, axis=0), reaches)
        for part, head in enumerate((2 * pair, 2 * pair + 1)):
            block = reach[part * CHUNK : (part + 1) * CHUNK, :]
            da_rows[head : head + 1, :] = jnp.sum(
                jnp.where(rows < columns, block, 0.0), axis=0, keepdims=True
            )
        x_grad = mm(jnp.concatenate(mixing, axis=1), split_heads(dy_low))
        grown = jnp.exp(cum_pair)
        dye = dy_pair * grown
        dye_low = dye.astype(bf16)
        dye_parts.append(dye_low)
        carry_terms.append((dye * carried[:, at]).astype(bf16))
        tail = jnp.exp(last - cum_pair)
        x_tail = tail * from_next[:, at]
        tail_terms.append((x_step * x_tail).astype(bf16))
        xw_parts.append((x_step * tail).astype(bf16))
        x_grad = x_grad + x_tail
        step_terms.append((x_pair * x_grad).astype(bf16))
        skip_gain = pair_columns(hp_ref[2:3, :], pair)
        uc_grad = step_pair * x_grad + skip_gain * dy_pair
        v_pair, s_pair = v_x[:, at], sig_x[:, at]
        after_u[0:CHUNK, at] = uc_grad * (s_pair * (1.0 + v_pair * (1.0 - s_pair)))
        wide_ref[taps + 1 : taps + 2, at] += jnp.sum(dy_pair * x_pair, axis=0, keepdims=True)
        held_scale = jnp.exp(last)
        kept = next_grad[:, at] * held_scale
        held_terms.append(jnp.sum(kept * held_low[:, at].astype(f32), axis=0, keepdims=True))
        state[:, at] = kept
    dye_all = jnp.concatenate(dye_parts, axis=1)
    xw_all = jnp.concatenate(xw_parts, axis=1)
    state[...] += mm(c_low, dye_all, TN)
    inner_grad_low = inner_grad.astype(bf16)
    b_grad = mm(inner_grad_low, c_low) + mm(xw_all, next_low, NT)
    c_grad = mm(inner_grad_low, b_low, TN) + mm(dye_all, held_low, NT)
    sc_grad = jnp.concatenate([b_grad, c_grad], axis=1)
    after_bc[0:CHUNK, :] = sc_grad * (sig_bc * (1.0 + v_bc * (1.0 - sig_bc)))

    head_ids = lax.broadcasted_iota(jnp.int32, (HEAD_ROWS, inner_cols), 0)
    channels = lax.broadcasted_iota(jnp.int32, (HEAD_ROWS, inner_cols), 1)
    members = (lax.div(channels, P_SIZE) == head_ids).astype(bf16)
    carry_row = mm(members, jnp.concatenate(carry_terms, axis=1), NT)
    tail_row = mm(members, jnp.concatenate(tail_terms, axis=1), NT)
    step_row = mm(members, jnp.concatenate(step_terms, axis=1), NT)
    held_row = jnp.concatenate(held_terms, axis=1)
    held_col = jnp.sum(
        jnp.where(lax.div(channels, P_SIZE) == head_ids, held_row, 0.0), axis=1, keepdims=True
    )
    decay_grad = (
        da_rows[...]
        + mm_exact(carry_row, causal.astype(f32))
        + mm_exact(tail_row, (rows < columns).astype(f32))
        + held_col
    )
    raw_t = raw.T[:HEAD_ROWS, :] + hpt_ref[:, 0:1]
    step_t = softplus(raw_t)
    rate = -jnp.exp(hpt_ref[:, 1:2])
    step_grad = step_row + decay_grad * rate
    real = lax.broadcasted_iota(jnp.int32, (HEAD_ROWS, CHUNK), 0) < 2 * pairs
    raw_grad = jnp.where(real, step_grad * sigmoid(raw_t), 0.0)
    head_ref[0:HEAD_ROWS, :] += raw_grad
    head_ref[HEAD_ROWS:, :] += jnp.where(real, decay_grad * rate * step_t, 0.0)
    raw_grad_cols = jnp.concatenate(
        [raw_grad, jnp.zeros((LANES - HEAD_ROWS, CHUNK), f32)], axis=0
    ).T

    base = 2 * inner_cols
    for ext_ref, after_ref, taps_ref, acc_ref, start in (
        (ext_u, after_u, cx_ref, wide_ref, inner_cols),
        (ext_bc, after_bc, cbc_ref, bc_acc_ref, base),
    ):
        width = after_ref.shape[1]
        conv_grad = after_ref[0:CHUNK, :]
        value_grad = after_ref[taps - 1 : taps - 1 + CHUNK, :] * taps_ref[0:1, :]
        for k in range(1, taps):
            shift = taps - 1 - k
            value_grad = value_grad + after_ref[shift : shift + CHUNK, :] * taps_ref[k : k + 1, :]
        dproj_ref[:, start : start + width] = value_grad.astype(bf16)
        for k in range(taps):
            acc_ref[k : k + 1, :] += jnp.sum(
                conv_grad * ext_ref[5 + k : 5 + k + CHUNK, :], axis=0, keepdims=True
            )
        acc_ref[taps : taps + 1, :] += jnp.sum(conv_grad, axis=0, keepdims=True)
    att_cols = att_ref.shape[1]
    dproj_ref[:, base + bc_cols : base + bc_cols + att_cols] = att_ref[...]
    dproj_ref[:, base + bc_cols + att_cols :] = raw_grad_cols.astype(bf16)


def swap_halves(values):
    half = P_SIZE // 2
    lane = lax.broadcasted_iota(jnp.int32, values.shape, 1)
    first = lax.rem(lane, P_SIZE) < half
    return jnp.where(
        first, pltpu.roll(values, LANES - half, axis=1), pltpu.roll(values, half, axis=1)
    )


def rotated(values, cosine, sine):
    return values * cosine + swap_halves(values) * sine


def rotated_back(values, cosine, sine):
    return values * cosine - swap_halves(values) * sine


def keys_and_values(kv_ref, cos_ref, sin_ref):
    kv = kv_ref[...]
    low = low_lanes(kv.shape)
    turned = rotated(kv, cos_ref[...], sin_ref[...])
    keys = jnp.where(low, turned, pltpu.roll(turned, P_SIZE, axis=1)).astype(bf16)
    values = jnp.where(low, pltpu.roll(kv, P_SIZE, axis=1), kv).astype(bf16)
    return keys, values


def score_weights(queries, keys, start):
    scores = mm(queries, keys, NT)
    rows = lax.broadcasted_iota(jnp.int32, scores.shape, 0) + start
    columns = lax.broadcasted_iota(jnp.int32, scores.shape, 1)
    scores = jnp.where(rows >= columns, scores, masked_score)
    weights = jnp.exp(scores - jnp.max(scores, axis=1, keepdims=True))
    return weights * (1.0 / jnp.sum(weights, axis=1, keepdims=True))


def rotated_queries(q_ref, cos_ref, sin_ref, here, at):
    turned = rotated(q_ref[here, at], cos_ref[here, :], sin_ref[here, :]).astype(bf16)
    return turned * jnp.asarray(P_SIZE**-0.5, bf16)


def attention_forward_kernel(q_ref, kv_ref, cos_ref, sin_ref, o_ref):
    keys, values = keys_and_values(kv_ref, cos_ref, sin_ref)
    for block in range(LEN // QBLOCK):
        here = slice(block * QBLOCK, (block + 1) * QBLOCK)
        seen = (block + 1) * QBLOCK
        for pair in range(q_ref.shape[1] // LANES):
            at = slice(pair * LANES, (pair + 1) * LANES)
            queries = rotated_queries(q_ref, cos_ref, sin_ref, here, at)
            low = low_lanes(queries.shape)
            zero = jnp.zeros_like(queries)
            outs = []
            for chosen in (jnp.where(low, queries, zero), jnp.where(low, zero, queries)):
                weights = score_weights(chosen, keys[:seen], block * QBLOCK)
                outs.append(mm(weights.astype(bf16), values[:seen]))
            o_ref[here, at] = jnp.where(low_lanes(outs[0].shape), outs[0], outs[1]).astype(bf16)


def attention_backward_kernel(
    q_ref, kv_ref, cos_ref, sin_ref, do_ref, grad_ref, key_grad, value_grad
):
    keys, values = keys_and_values(kv_ref, cos_ref, sin_ref)
    key_grad[...] = jnp.zeros_like(key_grad)
    value_grad[...] = jnp.zeros_like(value_grad)
    q_cols = q_ref.shape[1]
    for block in range(LEN // QBLOCK):
        here = slice(block * QBLOCK, (block + 1) * QBLOCK)
        seen = (block + 1) * QBLOCK
        for pair in range(q_cols // LANES):
            at = slice(pair * LANES, (pair + 1) * LANES)
            queries = rotated_queries(q_ref, cos_ref, sin_ref, here, at)
            out_grad = do_ref[here, at].astype(bf16)
            low = low_lanes(queries.shape)
            zero = jnp.zeros_like(queries)
            parts = []
            for is_low in (True, False):
                q_one = jnp.where(low, queries, zero) if is_low else jnp.where(low, zero, queries)
                g_one = jnp.where(low, out_grad, zero) if is_low else jnp.where(low, zero, out_grad)
                weights = score_weights(q_one, keys[:seen], block * QBLOCK)
                weight_grad = mm(g_one, values[:seen], NT)
                inner = jnp.sum(weights * weight_grad, axis=1, keepdims=True)
                score_grad = (weights * (weight_grad - inner)).astype(bf16)
                parts.append(mm(score_grad, keys[:seen]))
                key_grad[:seen, :] += mm(score_grad, q_one, TN)
                value_grad[:seen, :] += mm(weights.astype(bf16), g_one, TN)
            turned = jnp.where(low_lanes(parts[0].shape), parts[0], parts[1]) * P_SIZE**-0.5
            grad_ref[here, at] = rotated_back(turned, cos_ref[here, :], sin_ref[here, :]).astype(
                bf16
            )
    keys_sum = key_grad[...]
    keys_sum = keys_sum + pltpu.roll(keys_sum, P_SIZE, axis=1)
    values_sum = value_grad[...]
    values_sum = values_sum + pltpu.roll(values_sum, P_SIZE, axis=1)
    keys_sum = rotated_back(keys_sum, cos_ref[...], sin_ref[...])
    grad_ref[:, q_cols:] = jnp.where(low_lanes(keys_sum.shape), keys_sum, values_sum).astype(bf16)


def rotary_tables():
    half = P_SIZE // 2
    frequency = jnp.exp(jnp.arange(half, dtype=f32) * (-2.0 * math.log(rope_base) / P_SIZE))
    angles = jnp.arange(LEN, dtype=f32)[:, None] * frequency[None, :]
    cosine, sine = jnp.cos(angles), jnp.sin(angles)
    return (
        jnp.concatenate([cosine, cosine, cosine, cosine], axis=1),
        jnp.concatenate([-sine, sine, -sine, sine], axis=1),
    )


def vmem_params(megabytes):
    return pltpu.CompilerParams(
        vmem_limit_bytes=megabytes * 1024 * 1024, dimension_semantics=("arbitrary",)
    )


def mixer_forward(proj, conv_x, conv_bc, heads, inner_cols, bc_cols):
    rows_all = proj.shape[0]
    states = bc_cols // 2
    bc_at = 2 * inner_cols // bc_cols
    dt_at = proj.shape[1] // LANES - 1
    steps = rows_all // CHUNK
    return pl.pallas_call(
        mixer_forward_kernel,
        grid=(steps,),
        in_specs=[
            pl.BlockSpec((CHUNK, inner_cols), lambda i: (i, 0)),
            pl.BlockSpec((CHUNK, inner_cols), lambda i: (i, 1)),
            pl.BlockSpec((CHUNK, bc_cols), lambda i: (i, bc_at)),
            pl.BlockSpec((CHUNK, LANES), lambda i: (i, dt_at)),
            pl.BlockSpec(conv_x.shape, lambda i: (0, 0)),
            pl.BlockSpec(conv_bc.shape, lambda i: (0, 0)),
            pl.BlockSpec(heads.shape, lambda i: (0, 0)),
        ],
        out_specs=[
            pl.BlockSpec((CHUNK, inner_cols), lambda i: (i, 0)),
            pl.BlockSpec((CHUNK, inner_cols), lambda i: (i, 0)),
            pl.BlockSpec((states, inner_cols), lambda i: (i, 0)),
        ],
        out_shape=[
            jax.ShapeDtypeStruct((rows_all, inner_cols), bf16),
            jax.ShapeDtypeStruct((rows_all, inner_cols), bf16),
            jax.ShapeDtypeStruct((steps * states, inner_cols), bf16),
        ],
        scratch_shapes=[
            pltpu.VMEM((states, inner_cols), f32),
            pltpu.VMEM((CHUNK + 8, inner_cols), f32),
            pltpu.VMEM((CHUNK + 8, bc_cols), f32),
        ],
        compiler_params=vmem_params(32),
        cost_estimate=pl.CostEstimate(
            flops=rows_all * inner_cols * 1200,
            bytes_accessed=rows_all * inner_cols * 14,
            transcendentals=rows_all * inner_cols * 4,
        ),
        name="mixer_forward",
    )(proj, proj, proj, proj, conv_x, conv_bc, heads)


def mixer_backward(proj, y, dg, held, att_grad, conv_x, conv_bc, heads, inner_cols, bc_cols):
    rows_all = proj.shape[0]
    states = bc_cols // 2
    bc_at = 2 * inner_cols // bc_cols
    dt_at = proj.shape[1] // LANES - 1
    steps = rows_all // CHUNK
    chunks = LEN // CHUNK
    per = CHUNK // 8

    def at(i):
        return i // chunks * chunks + (chunks - 1 - i % chunks)

    def before(i):
        return jnp.maximum(at(i) * per - 1, 0)

    heads_t = heads[:, :HEAD_ROWS].T
    return pl.pallas_call(
        mixer_backward_kernel,
        grid=(steps,),
        in_specs=[
            pl.BlockSpec((CHUNK, inner_cols), lambda i: (at(i), 0)),
            pl.BlockSpec((CHUNK, inner_cols), lambda i: (at(i), 1)),
            pl.BlockSpec((CHUNK, bc_cols), lambda i: (at(i), bc_at)),
            pl.BlockSpec((CHUNK, LANES), lambda i: (at(i), dt_at)),
            pl.BlockSpec((8, inner_cols), lambda i: (before(i), 1)),
            pl.BlockSpec((8, bc_cols), lambda i: (before(i), bc_at)),
            pl.BlockSpec((CHUNK, inner_cols), lambda i: (at(i), 0)),
            pl.BlockSpec((CHUNK, inner_cols), lambda i: (at(i), 0)),
            pl.BlockSpec((states, inner_cols), lambda i: (at(i), 0)),
            pl.BlockSpec((CHUNK, att_grad.shape[1]), lambda i: (at(i), 0)),
            pl.BlockSpec(conv_x.shape, lambda i: (0, 0)),
            pl.BlockSpec(conv_bc.shape, lambda i: (0, 0)),
            pl.BlockSpec(heads.shape, lambda i: (0, 0)),
            pl.BlockSpec(heads_t.shape, lambda i: (0, 0)),
        ],
        out_specs=[
            pl.BlockSpec((CHUNK, proj.shape[1]), lambda i: (at(i), 0)),
            pl.BlockSpec((8, inner_cols), lambda i: (0, 0)),
            pl.BlockSpec((8, bc_cols), lambda i: (0, 0)),
            pl.BlockSpec((2 * HEAD_ROWS, CHUNK), lambda i: (0, 0)),
        ],
        out_shape=[
            jax.ShapeDtypeStruct(proj.shape, bf16),
            jax.ShapeDtypeStruct((8, inner_cols), f32),
            jax.ShapeDtypeStruct((8, bc_cols), f32),
            jax.ShapeDtypeStruct((2 * HEAD_ROWS, CHUNK), f32),
        ],
        scratch_shapes=[
            pltpu.VMEM((states, inner_cols), f32),
            pltpu.VMEM((CHUNK + 8, inner_cols), f32),
            pltpu.VMEM((CHUNK + 8, bc_cols), f32),
            pltpu.VMEM((CHUNK + 8, inner_cols), f32),
            pltpu.VMEM((CHUNK + 8, bc_cols), f32),
            pltpu.VMEM((HEAD_ROWS, CHUNK), f32),
        ],
        compiler_params=vmem_params(48),
        cost_estimate=pl.CostEstimate(
            flops=rows_all * inner_cols * 4000,
            bytes_accessed=rows_all * inner_cols * 26,
            transcendentals=rows_all * inner_cols * 8,
        ),
        name="mixer_backward",
    )(
        proj, proj, proj, proj, proj, proj, y, dg, held, att_grad, conv_x, conv_bc, heads, heads_t
    )


def attention_forward(proj, tables, q_cols, q_at, kv_at):
    rows_all = proj.shape[0]
    return pl.pallas_call(
        attention_forward_kernel,
        grid=(rows_all // LEN,),
        in_specs=[
            pl.BlockSpec((LEN, q_cols), lambda i: (i, q_at)),
            pl.BlockSpec((LEN, LANES), lambda i: (i, kv_at)),
            pl.BlockSpec((LEN, LANES), lambda i: (0, 0)),
            pl.BlockSpec((LEN, LANES), lambda i: (0, 0)),
        ],
        out_specs=pl.BlockSpec((LEN, q_cols), lambda i: (i, 0)),
        out_shape=jax.ShapeDtypeStruct((rows_all, q_cols), bf16),
        compiler_params=vmem_params(40),
        cost_estimate=pl.CostEstimate(
            flops=rows_all * LEN * q_cols * 8,
            bytes_accessed=rows_all * q_cols * 12,
            transcendentals=rows_all * LEN * 3,
        ),
        name="attention_forward",
    )(proj, proj, *tables)


def attention_backward(proj, tables, out_grad, q_cols, q_at, kv_at):
    rows_all = proj.shape[0]
    return pl.pallas_call(
        attention_backward_kernel,
        grid=(rows_all // LEN,),
        in_specs=[
            pl.BlockSpec((LEN, q_cols), lambda i: (i, q_at)),
            pl.BlockSpec((LEN, LANES), lambda i: (i, kv_at)),
            pl.BlockSpec((LEN, LANES), lambda i: (0, 0)),
            pl.BlockSpec((LEN, LANES), lambda i: (0, 0)),
            pl.BlockSpec((LEN, q_cols), lambda i: (i, out_grad.shape[1] // q_cols - 1)),
        ],
        out_specs=pl.BlockSpec((LEN, q_cols + LANES), lambda i: (i, 0)),
        out_shape=jax.ShapeDtypeStruct((rows_all, q_cols + LANES), bf16),
        scratch_shapes=[pltpu.VMEM((LEN, LANES), f32), pltpu.VMEM((LEN, LANES), f32)],
        compiler_params=vmem_params(48),
        cost_estimate=pl.CostEstimate(
            flops=rows_all * LEN * q_cols * 20,
            bytes_accessed=rows_all * q_cols * 16,
            transcendentals=rows_all * LEN * 3,
        ),
        name="attention_backward",
    )(proj, proj, *tables, out_grad)


def inverse_rms(values):
    return lax.rsqrt(jnp.mean(values * values, axis=-1, keepdims=True) + epsilon)


def normalize_back(grad, values, inverse, gain_row):
    unit = values * inverse
    scaled = grad * gain_row
    return (scaled - unit * jnp.mean(scaled * unit, axis=-1, keepdims=True)) * inverse


def swap_tensor(values):
    return lax.ppermute(values, "tensor", [(0, 1), (1, 0)])


def both_halves(mine):
    other = swap_tensor(mine)
    return jnp.where(
        lax.axis_index("tensor") == 0,
        jnp.concatenate([mine, other], axis=0),
        jnp.concatenate([other, mine], axis=0),
    )


def half_rows(values, index):
    rows = values.shape[0] // 2
    return lax.dynamic_slice_in_dim(values, index * rows, rows, 0)


def sum_own_half(values, index):
    arrived = swap_tensor(half_rows(values, 1 - index))
    return half_rows(values, index).astype(f32) + arrived.astype(f32)


def scatter_sum(values, dp_count):
    pairs = dp_count // 2
    core = lax.rem(lax.axis_index("dp"), 2)
    by_core = values.reshape(pairs, 2, values.shape[0] // dp_count, values.shape[1])
    kept = lax.dynamic_index_in_dim(by_core, core, 1, keepdims=False)
    sent = lax.dynamic_index_in_dim(by_core, 1 - core, 1, keepdims=False)
    arrived = lax.ppermute(sent, "dp", [(i, i ^ 1) for i in range(dp_count)])
    summed = (kept.astype(f32) + arrived.astype(f32)).astype(bf16)
    groups = [[core_id + 2 * i for i in range(pairs)] for core_id in range(2)]
    blocks = lax.all_to_all(summed, "dp", 0, 0, tiled=True, axis_index_groups=groups)
    return jnp.sum(blocks.astype(f32), axis=0)


def local(
    tokens,
    gains,
    w_zx,
    w_bc,
    w_dt,
    conv_x,
    conv_bc,
    head_params,
    w_mo,
    w_q,
    w_kv,
    w_ao,
    w_gu,
    w_down,
    cotangent,
):
    dp_count = lax.axis_size("dp")
    side = lax.axis_index("tensor")
    width = tokens.shape[1]
    here = width // dp_count
    inner_cols, bc_cols, head_cols = w_zx.shape[2], w_bc.shape[1], w_dt.shape[1]
    q_cols, kv_cols = w_q.shape[1], 2 * w_kv.shape[2]
    hidden, mo_cols, ao_cols = w_gu.shape[2], w_mo.shape[0], w_ao.shape[0]

    shared = both_halves(jnp.concatenate([w_bc, gains.T], axis=1))
    in_pack = jnp.concatenate(
        [
            w_zx[:, 0],
            w_zx[:, 1],
            shared[:, :bc_cols],
            w_q,
            w_kv.reshape(here, kv_cols),
            w_dt,
            shared[:, bc_cols:],
            jnp.zeros((here, LANES - head_cols - 2), bf16),
        ],
        axis=1,
    )
    w_in = lax.all_gather(in_pack, "dp", axis=0, tiled=True)
    out_pack = jnp.concatenate(
        [w_gu.reshape(here, 2 * hidden), w_down.T, w_mo.T, w_ao.T], axis=1
    )
    w_out = lax.all_gather(out_pack, "dp", axis=0, tiled=True)
    tokens_all = both_halves(tokens)
    cotangent_all = both_halves(cotangent)
    tables = rotary_tables()

    gu_full = w_out[:, : 2 * hidden]
    down_full = w_out[:, 2 * hidden : 3 * hidden]
    mix_full = w_out[:, 3 * hidden :]
    dt_start = w_in.shape[1] - LANES
    gain_full = w_in[:, dt_start + head_cols : dt_start + head_cols + 2].T.astype(f32)
    gain_one, gain_two = gain_full[0:1], gain_full[1:2]
    heads = jnp.pad(head_params, ((0, 5), (0, LANES - head_cols)))
    q_at = (2 * inner_cols + bc_cols) // q_cols
    kv_at = (2 * inner_cols + bc_cols + q_cols) // LANES

    seq_in = tokens_all.astype(f32)
    inverse_one = inverse_rms(seq_in)
    n1 = (seq_in * inverse_one * gain_one).astype(bf16)
    proj = mm(n1, w_in)
    gated, y, held = mixer_forward(proj, conv_x, conv_bc, heads, inner_cols, bc_cols)
    attended = attention_forward(proj, tables, q_cols, q_at, kv_at)
    branch_part = mm(gated, mix_full[:, :mo_cols], NT) + mm(attended, mix_full[:, mo_cols:], NT)
    branch_low = branch_part.astype(bf16)
    branch = branch_low.astype(f32) + swap_tensor(branch_low).astype(f32)
    hidden_one = seq_in + branch
    inverse_two = inverse_rms(hidden_one)
    n2 = (hidden_one * inverse_two * gain_two).astype(bf16)
    gate_up = mm(n2, gu_full)
    gate, up = gate_up[:, :hidden], gate_up[:, hidden:]
    sig = sigmoid(gate)
    activated = (gate * sig * up).astype(bf16)
    ffn_low = mm(activated, down_full, NT).astype(bf16)
    layer_out = (half_rows(hidden_one, side) + sum_own_half(ffn_low, side)).astype(bf16)

    act_grad = mm(cotangent_all, down_full)
    gate_up_grad = jnp.concatenate(
        [act_grad * up * (sig * (1.0 + gate * (1.0 - sig))), act_grad * (gate * sig)], axis=1
    ).astype(bf16)
    n2_grad_low = mm(gate_up_grad, gu_full, NT).astype(bf16)
    ffn_grads = jnp.concatenate(
        [
            mm(n2, gate_up_grad, TN).astype(bf16),
            mm(cotangent_all, activated, TN).astype(bf16),
        ],
        axis=1,
    )
    ffn_grads = lax.psum_scatter(ffn_grads, "dp", scatter_dimension=0, tiled=True)
    n2_grad = n2_grad_low.astype(f32) + swap_tensor(n2_grad_low).astype(f32)
    gain_two_grad = jnp.sum(n2_grad_low.astype(f32) * (hidden_one * inverse_two), axis=0)
    hidden_grad = cotangent_all.astype(f32) + normalize_back(
        n2_grad, hidden_one, inverse_two, gain_two
    )
    branch_grad = hidden_grad.astype(bf16)
    mix_grad = mm(branch_grad, mix_full).astype(bf16)
    mo_grad = mm(branch_grad, gated, TN).astype(bf16)
    ao_grad = mm(branch_grad, attended, TN).astype(bf16)
    att_grad = attention_backward(proj, tables, mix_grad, q_cols, q_at, kv_at)
    proj_grad, wide_sums, bc_sums, head_sums = mixer_backward(
        proj, y, mix_grad, held, att_grad, conv_x, conv_bc, heads, inner_cols, bc_cols
    )
    n1_grad_low = mm(proj_grad, w_in, NT).astype(bf16)
    gain_one_grad = jnp.sum(n1_grad_low.astype(f32) * (seq_in * inverse_one), axis=0)
    in_grads = mm(n1, proj_grad, TN).astype(bf16)
    n1_grad = sum_own_half(n1_grad_low, side)
    seq_own = tokens.astype(f32)
    input_grad = (
        half_rows(hidden_grad, side)
        + normalize_back(n1_grad, seq_own, inverse_rms(seq_own), gain_one)
    ).astype(bf16)

    taps = conv_x.shape[0]
    head_grads = jnp.stack(
        [
            jnp.sum(head_sums[:head_cols], axis=1),
            jnp.sum(head_sums[HEAD_ROWS : HEAD_ROWS + head_cols], axis=1),
            jnp.sum(wide_sums[taps].reshape(head_cols, P_SIZE), axis=1),
        ]
    )
    pieces = [wide_sums[:taps], bc_sums[:taps], head_grads]
    flat = jnp.concatenate([piece.reshape(-1) for piece in pieces])
    flat_cols = -(-flat.shape[0] // here)
    flat_cols = -(-(flat_cols + 2) // LANES) * LANES - 2
    flat = jnp.pad(flat, (0, here * flat_cols - flat.shape[0])).reshape(here, flat_cols)
    gain_cols = jnp.stack([gain_one_grad, gain_two_grad], axis=1)
    small = jnp.concatenate([gain_cols, jnp.tile(flat, (dp_count, 1))], axis=1).astype(bf16)
    summed = scatter_sum(
        jnp.concatenate([in_grads, mo_grad, ao_grad, small], axis=1), dp_count
    )

    in_cols = in_grads.shape[1]
    bc_start = 2 * inner_cols
    q_start = bc_start + bc_cols
    kv_start = q_start + q_cols
    mo_start = in_cols
    ao_start = mo_start + mo_cols
    gain_start = ao_start + ao_cols
    flat_sum = summed[:, gain_start + 2 :].reshape(-1)
    x_size, bc_size = taps * inner_cols, taps * bc_cols
    grad_conv_x = flat_sum[:x_size].reshape(taps, inner_cols)
    conv_bc_half = flat_sum[x_size : x_size + bc_size].reshape(taps, bc_cols)
    grad_head = flat_sum[x_size + bc_size : x_size + bc_size + 3 * head_cols].reshape(3, head_cols)
    shared_half = jnp.concatenate(
        [summed[:, bc_start:q_start], summed[:, gain_start : gain_start + 2]], axis=1
    )
    to_send = jnp.concatenate(
        [half_rows(shared_half, 1 - side).reshape(-1), conv_bc_half.reshape(-1)]
    )
    arrived = swap_tensor(to_send)
    shared_sum = half_rows(shared_half, side) + arrived[: shared_half.size // 2].reshape(
        here // 2, bc_cols + 2
    )
    grad_conv_bc = conv_bc_half + arrived[shared_half.size // 2 :].reshape(taps, bc_cols)
    ffn_sum = ffn_grads.astype(f32)
    return (
        layer_out,
        input_grad,
        shared_sum[:, bc_cols:].T,
        summed[:, :bc_start].reshape(here, 2, inner_cols),
        shared_sum[:, :bc_cols],
        summed[:, dt_start : dt_start + head_cols],
        grad_conv_x,
        grad_conv_bc,
        grad_head,
        summed[:, mo_start:ao_start].T,
        summed[:, q_start:kv_start],
        summed[:, kv_start : kv_start + kv_cols].reshape(here, 2, kv_cols // 2),
        summed[:, ao_start:gain_start].T,
        ffn_sum[:, : 2 * hidden].reshape(here, 2, hidden),
        ffn_sum[:, 2 * hidden :].T,
    )


def solution(mesh):
    placed = (
        P(("dp", "tensor"), None),
        P(None, ("dp", "tensor")),
        P("dp", None, "tensor"),
        P(("dp", "tensor"), None),
        P("dp", "tensor"),
        P(None, "tensor"),
        P(),
        P(None, "tensor"),
        P("tensor", "dp"),
        P("dp", "tensor"),
        P("dp", None, "tensor"),
        P("tensor", "dp"),
        P("dp", None, "tensor"),
        P("tensor", "dp"),
        P(("dp", "tensor"), None),
    )
    return jax.shard_map(
        local,
        mesh=mesh,
        in_specs=placed,
        out_specs=(
            P(("dp", "tensor"), None),
            P(("dp", "tensor"), None),
            P(None, ("dp", "tensor")),
            P("dp", None, "tensor"),
            P(("dp", "tensor"), None),
            P("dp", "tensor"),
            P(None, "tensor"),
            P(),
            P(None, "tensor"),
            P("tensor", "dp"),
            P("dp", "tensor"),
            P("dp", None, "tensor"),
            P("tensor", "dp"),
            P("dp", None, "tensor"),
            P("tensor", "dp"),
        ),
        check_vma=False,
    )
```

time: 2130 us -> 557 us (0.26)
  waiting for transfers between devices: 1040 us -> 280 us
  blocking collectives: 261 us -> 0 us
  matrix products: 338 us -> 78.5 us
  local copies, waits for them, and re-layouts: 292 us -> 47.6 us
  other arithmetic: 126 us -> 44.5 us
  Pallas kernels: 0 us -> 66.2 us
  loops' own time: 36.4 us -> 0 us
    reduce_scatter x13 -> x1, waiting for transfers between devices: 736 us -> 53.9 us  [local(): lax.psum_scatter(ffn_grads, 'dp', scatter_dimension=0, tiled=True)]
    dot_general x151 -> x14, matrix products: 334 us -> 78.5 us  [mm(): return lax.dot_general(left, right, dims, preferred_element_type=f32)]
    all_gather x6 -> x0, blocking collectives: 221 us -> none  [the longest x1 72.4 us: collect(): lax.all_gather(w_bc, ('dp', 'tensor'), axis=0, tiled=True)]
    ppermute x0 -> x9, waiting for transfers between devices: none -> 157 us  [the longest x8 157 us: swap_tensor(): return lax.ppermute(values, 'tensor', [(0, 1), (1, 0)])]
    unnamed x25 -> x3, waiting for transfers between devices: 135 us -> 0.05 us
    dynamic_update_slice x29 -> x0, local copies, waits for them, and re-layouts: 111 us -> none  [the longest x24 88.6 us: mamba_mix(): final_state, outputs = lax.scan(jax.checkpoint(scan_block), initial, pieces)]
    all_gather x8 -> x2, waiting for transfers between devices: 171 us -> 68.6 us  [the longest x1 43.4 us: local(): w_out = lax.all_gather(out_pack, 'dp', axis=0, tiled=True)]
    pallas_call x0 -> x4, Pallas kernels: none -> 66.2 us  [the longest x1 29.3 us: mixer_backward(): pl.pallas_call(mixer_backward_kernel, grid=(steps,), in_specs=[pl.BlockSp...]
  transfers between devices with their start and end apart: 23 -> 13, of which waited for: 18 -> 9; matrix products, arithmetic and copies ran while one was open for 14% -> 15% of each run, Pallas kernels for 0% -> 4%
where the time goes in v1:
time: 557 us; the launch traced here: 547 us
  waiting for transfers between devices  280 us (50%)
  matrix products  78.5 us (14%)
  Pallas kernels  66.2 us (12%)
  local copies, waits for them, and re-layouts  47.6 us (9%)
  other arithmetic  44.5 us (8%)
  starting transfers between devices  15.7 us (3%)
  between operations  15 us (3%)
    ppermute x8, waiting for transfers between devices, swap_tensor(): return lax.ppermute(values, 'tensor', [(0, 1), (1, 0)])  157 us
    dot_general x14, matrix products, mm(): return lax.dot_general(left, right, dims, preferred_element_type=f32)  78.5 us
    reduce_scatter x1, waiting for transfers between devices, local(): lax.psum_scatter(ffn_grads, 'dp', scatter_dimension=0, tiled=True)  53.9 us
    all_gather x1, waiting for transfers between devices, local(): w_out = lax.all_gather(out_pack, 'dp', axis=0, tiled=True)  43.4 us
    pallas_call x1, Pallas kernels, mixer_backward(): pl.pallas_call(mixer_backward_kernel, grid=(steps,), in_specs=[pl.BlockSp...  29.3 us
    all_gather x1, waiting for transfers between devices, local(): w_in = lax.all_gather(in_pack, 'dp', axis=0, tiled=True)  25.2 us
    unnamed x81, local copies, waits for them, and re-layouts  16.2 us
    pallas_call x1, Pallas kernels, attention_backward(): pl.pallas_call(attention_backward_kernel, grid=(rows_all // LEN,), in_spe...  16 us
  transfers between devices with their start and end apart: 13, of which 9 were waited for; matrix products, arithmetic and copies ran while one was open for 15% of the time, Pallas kernels for 4%

profile of v1, /device:TPU:0, one launch (start us, length us, event | category | flops | bytes accessed | tf_op | source)
XLA Modules:
  0.0 547.4 jit_solution(4890025417026927320)
XLA Ops:
  24.6 20.8 %collective-permute-done = bf16[512,1024]{0,1:T(8,128)(2,1)S(1)} collective-permute-done((bf16[512,1024]{0,1:T(8,128)(2,1)S(1)}, bf16[512,1024]{0,1:T(8,128)(2,1)S(1)}, u32[]{:S(2)}, u32[]{:S(2)}) %collective-permute-start) | collective-permute-done | bytes 1048608 | tf_op jit(solution)/shard_map/ppermute | solution.py:611
  46.2 25.2 %all-gather.3.cloned.1.call-done = bf16[1024,2304]{1,0:T(8,128)(2,1)} async-done(((bf16[64,2304]{1,0:T(8,128)(2,1)}), bf16[1024,2304]{1,0:T(8,128)(2,1)}) %all-gather.3.cloned.1.call-update) | async-done | bytes 4718608 | tf_op jit(solution)/shard_map/all_gather | solution.py:685
  73.0 7.8 %fusion.35.z_ref.u_ref.bc_ref.dr_ref.q_ref.kv_ref.u_before_ref.bc_before_ref = f32[1024,2304]{1,0:T(8,128)S(1)} fusion(bf16[1024,2304]{1,0:T(8,128)(2,1)} %all-gather.3.cloned.1.call-done, f32[1024]{0:T(1024)S(1)} %get-tuple-element.62, f32[1024]{0:T(1024)S(1)} %add_rsqrt_fusion.1, bf16[512,1024]{0,1:T(8,128)(2,1)S(1)} %collective-permute-done, ...), kind=kOutput, calls=%fused_computation.62 | convolution fusion | flops 4845469696 | bytes 16261121 | tf_op jit(solution)/shard_map/dot_general | solution.py:30
  80.8 12.7 %mixer_forward.1 = (bf16[1024,768]{1,0:T(8,128)(2,1)S(1)}, bf16[1024,768]{1,0:T(8,128)(2,1)S(1)}, bf16[1024,768]{1,0:T(8,128)(2,1)S(1)}) custom-call(f32[1024,2304]{1,0:T(8,128)S(1)} %fusion.35.z_ref.u_ref.bc_ref.dr_ref.q_ref.kv_ref.u_before_ref.bc_before_ref, f32[1024,2304]{1,0:T(8,128)S(1)} %fusion.35.z_ref.u_ref.bc_ref.dr_ref.q_ref.kv_ref.u_before_ref.bc_before_ref, ...), custom_call_target="tpu_custom_call" | custom-call | flops 943718400 | bytes 11010048 | tf_op jit(solution)/shard_map/mixer_forward/pallas_call | solution.py:448
  95.8 8.3 %attention_forward.1 = bf16[1024,256]{1,0:T(8,128)(2,1)S(1)} custom-call(f32[1024,2304]{1,0:T(8,128)S(1)} %fusion.35.z_ref.u_ref.bc_ref.dr_ref.q_ref.kv_ref.u_before_ref.bc_before_ref, f32[1024,2304]{1,0:T(8,128)S(1)} %fusion.35.z_ref.u_ref.bc_ref.dr_ref.q_ref.kv_ref.u_before_ref.bc_before_ref, f32[1024,128]{1,0:T(8,128)S(1)} %get-tuple-element.82.cos_ref, ...), custom_call_target="tpu_custom_call" | custom-call | flops 2147483648 | bytes 3145728 | tf_op jit(solution)/shard_map/attention_forward/pallas_call | solution.py:554
  104.1 43.4 %all-gather.5.cloned.1.call-done = bf16[1024,4096]{1,0:T(8,128)(2,1)} async-done(((bf16[64,4096]{1,0:T(8,128)(2,1)}), bf16[1024,4096]{1,0:T(8,128)(2,1)}) %all-gather.5.cloned.1.call-update) | async-done | bytes 8388624 | tf_op jit(solution)/shard_map/all_gather | solution.py:689
  158.7 44.5 %collective-permute-done.2 = bf16[1024,1024]{0,1:T(8,128)(2,1)} collective-permute-done((bf16[1024,1024]{0,1:T(8,128)(2,1)}, bf16[1024,1024]{0,1:T(8,128)(2,1)}, u32[]{:S(2)}, u32[]{:S(2)}) %collective-permute-start.2) | collective-permute-done | bytes 2097184 | tf_op jit(solution)/shard_map/ppermute | solution.py:611
  208.2 8.3 %fusion.11 = f32[1024,2048]{1,0:T(8,128)S(1)} fusion(bf16[1024,4096]{1,0:T(8,128)(2,1)} %all-gather.5.cloned.1.call-done, f32[1024,1024]{0,1:T(8,128)S(1)} %get-tuple-element.66, f32[1024]{0:T(1024)S(1)} %get-tuple-element.61, f32[1024]{0:T(1024)S(1)} %add_rsqrt_fusion), kind=kOutput, calls=%fused_computation.31 | convolution fusion | flops 4298113024 | bytes 16785408 | tf_op jit(solution)/shard_map/dot_general | solution.py:30
  216.5 8.4 %collective-permute-done.4 = bf16[512,1024]{0,1:T(8,128)(2,1)S(1)} collective-permute-done((bf16[512,1024]{0,1:T(8,128)(2,1)}, bf16[512,1024]{0,1:T(8,128)(2,1)S(1)}, u32[]{:S(2)}, u32[]{:S(2)}) %collective-permute-start.4) | collective-permute-done | bytes 1048608 | tf_op jit(solution)/shard_map/ppermute | solution.py:611
  224.9 6.0 %multiply_convert_fusion.1 = (bf16[1024,1024]{1,0:T(8,128)(2,1)S(1)}, bf16[1024,1024]{1,0:T(8,128)(2,1)}, bf16[1024,1024]{1,0:T(8,128)(2,1)}) fusion(f32[1024,2048]{1,0:T(8,128)S(1)} %fusion.11, bf16[1024,4096]{1,0:T(8,128)(2,1)S(1)} %bitcast.52, bf16[512,1024]{0,1:T(8,128)(2,1)S(1)} %collective-permute-done.4, bf16[512,1024]{0,1:T(8,128)(2,1)S(1)} %copy-done.18, ...), kind=kOutput, calls=%fused_computation.21 | convolution fusion | flops 2172649472 | bytes 18874368 | tf_op jit(solution)/shard_map/dot_general | solution.py:30
  230.9 8.1 %fusion.26 = bf16[1024,1024]{0,1:T(8,128)(2,1)} fusion(bf16[1024,4096]{1,0:T(8,128)(2,1)S(1)} %bitcast.52, bf16[1024,1024]{1,0:T(8,128)(2,1)} %get-tuple-element.68, bf16[1024,1024]{1,0:T(8,128)(2,1)S(1)} %get-tuple-element.67), kind=kOutput, calls=%fused_computation.51 | convolution fusion | flops 4304404480 | bytes 10485760 | tf_op jit(solution)/shard_map/dot_general | solution.py:30
  240.5 45.8 %collective-permute-done.5 = bf16[1024,1024]{0,1:T(8,128)(2,1)} collective-permute-done((bf16[1024,1024]{0,1:T(8,128)(2,1)}, bf16[1024,1024]{0,1:T(8,128)(2,1)}, u32[]{:S(2)}, u32[]{:S(2)}) %collective-permute-start.5) | collective-permute-done | bytes 2097184 | tf_op jit(solution)/shard_map/ppermute | solution.py:611
  286.3 5.1 fusion.6
  304.4 16.0 %attention_backward.1.att_ref = bf16[1024,384]{1,0:T(8,128)(2,1)S(1)} custom-call(f32[1024,2304]{1,0:T(8,128)} %copy-done, f32[1024,2304]{1,0:T(8,128)} %copy-done, f32[1024,128]{1,0:T(8,128)S(1)} %get-tuple-element.82.cos_ref, f32[1024,128]{1,0:T(8,128)S(1)} %get-tuple-element.83.sin_ref, bf16[1024,1024]{1,0:T(8,128)(2,1)S(1)} %fusion.23.do_ref.dg_ref), custom_call_target="tpu_custom_call" | custom-call | flops 5368709120 | bytes 4194304 | tf_op jit(solution)/shard_map/attention_backward/pallas_call | solution.py:577
  320.4 29.3 %mixer_backward.1 = (bf16[1024,2304]{1,0:T(8,128)(2,1)}, f32[8,768]{1,0:T(8,128)S(1)}, f32[8,256]{1,0:T(8,128)S(1)}, f32[32,128]{1,0:T(8,128)S(1)}) custom-call(f32[1024,2304]{1,0:T(8,128)} %copy-done, f32[1024,2304]{1,0:T(8,128)} %copy-done, f32[1024,2304]{1,0:T(8,128)} %copy-done, f32[1024,2304]{1,0:T(8,128)} %copy-done, f32[1024,2304]{1,0:T(8,128)} %copy-done, ...), custom_call_target="tpu_custom_call" | custom-call | flops 3145728000 | bytes 20447232 | tf_op jit(solution)/shard_map/mixer_backward/pallas_call | solution.py:501
  349.8 8.9 %fusion.4 = (bf16[1024]{0:T(1024)(128)(2,1)S(1)}, bf16[1024,1024]{0,1:T(8,128)(2,1)}) fusion(f32[1024]{0:T(1024)S(1)} %add_rsqrt_fusion.1, bf16[512,1024]{0,1:T(8,128)(2,1)S(1)} %copy-done.11, bf16[512,1024]{0,1:T(8,128)(2,1)S(1)} %copy-done.16, pred[]{:T(512)S(6)} %eq.2, bf16[1024,2304]{1,0:T(8,128)(2,1)} %get-tuple-element.25, ...), kind=kOutput, calls=%fused_computation.13 | convolution fusion | flops 4847565824 | bytes 13637633 | tf_op jit(solution)/shard_map/dot_general | solution.py:30
  359.8 9.7 %convolution_convert_fusion = bf16[1024,2304]{1,0:T(8,128)(2,1)} fusion(bf16[1024,2304]{1,0:T(8,128)(2,1)} %get-tuple-element.25, f32[1024]{0:T(1024)S(1)} %get-tuple-element.62, f32[1024]{0:T(1024)S(1)} %add_rsqrt_fusion.1, bf16[512,1024]{0,1:T(8,128)(2,1)S(1)} %copy-done.17, bf16[512,1024]{0,1:T(8,128)(2,1)S(1)} %copy-done.12, pred[]{:T(512)S(6)} %eq.2), kind=kOutput, calls=%fused_computation.7 | convolution fusion | flops 4847828992 | bytes 11542529 | tf_op jit(solution)/shard_map/dot_general | solution.py:30
  369.6 10.9 %concatenate.68 = bf16[1024,3456]{1,0:T(8,128)(2,1)} concatenate(bf16[1024,2304]{1,0:T(8,128)(2,1)} %convolution_convert_fusion, bf16[1024,768]{1,0:T(8,128)(2,1)} %convolution_convert_fusion.5, bf16[1024,256]{1,0:T(8,128)(2,1)S(1)} %copy-done.21, bf16[1024,1]{1,0:T(8,128)(2,1)S(1)} %stack.26, bf16[1024,1]{1,0:T(8,128)(2,1)S(1)} %stack.27, bf16[1024,126]{1,0:T(8,128)(2,1)S(1)} %bitcast.44), dimensions={1} | concatenate | bytes 14155776 | tf_op jit(solution)/shard_map/concatenate | solution.py:775
  385.7 6.8 %convolution_convert_fusion.1 = bf16[1024,2048]{1,0:T(8,128)(2,1)S(1)} fusion(bf16[1024,1024]{1,0:T(8,128)(2,1)} %get-tuple-element.68, bf16[1024,1024]{1,0:T(8,128)(2,1)S(1)} %copy-done.30, f32[1024,1024]{0,1:T(8,128)S(1)} %copy-done.9, f32[1024]{0:T(1024)S(1)} %get-tuple-element.61, f32[1024]{0:T(1024)S(1)} %add_rsqrt_fusion), kind=kOutput, calls=%fused_computation.28 | convolution fusion | flops 4308598784 | bytes 12591104 | tf_op jit(solution)/shard_map/dot_general | solution.py:30
  398.1 5.6 %fusion = bf16[8,64,3456]{2,1,0:T(8,128)(2,1)} fusion(bf16[8,64,3456]{2,1,0:T(8,128)(2,1)} %collective-permute-done.7, bf16[8,2,64,3456]{3,2,1,0:T(8,128)(2,1)} %bitcast.43, s32[]{:T(128)S(6)} %select_n.50), kind=kLoop, calls=%fused_computation.1 | loop fusion | flops 7077888 | bytes 10616836 | tf_op jit(solution)/shard_map/convert_element_type | solution.py:640
  408.5 5.0 convolution_convert_fusion.4
  419.4 23.0 %collective-permute-done.3 = bf16[512,1024]{0,1:T(8,128)(2,1)} collective-permute-done((bf16[512,1024]{0,1:T(8,128)(2,1)}, bf16[512,1024]{0,1:T(8,128)(2,1)}, u32[]{:S(2)}, u32[]{:S(2)}) %collective-permute-start.3) | collective-permute-done | bytes 1048608 | tf_op jit(solution)/shard_map/ppermute | solution.py:611
  448.3 14.8 %collective-permute-done.6 = bf16[512,1024]{0,1:T(8,128)(2,1)} collective-permute-done((bf16[512,1024]{0,1:T(8,128)(2,1)}, bf16[512,1024]{0,1:T(8,128)(2,1)}, u32[]{:S(2)}, u32[]{:S(2)}) %collective-permute-start.6) | collective-permute-done | bytes 1048608 | tf_op jit(solution)/shard_map/ppermute | solution.py:611
  470.8 53.9 %reduce-scatter.2.cloned.1.call-done = bf16[64,3072]{1,0:T(8,128)(2,1)} async-done(((bf16[1024,3072]{1,0:T(8,128)(2,1)}), bf16[64,3072]{1,0:T(8,128)(2,1)}) %reduce-scatter.2.cloned.1.call-update) | async-done | bytes 393232 | tf_op jit(solution)/shard_map/reduce_scatter | solution.py:735
  (187 shorter events, 103.9 us)
Async XLA Ops:
  7.2 64.1 %all-gather.3.cloned.1.call-start = ((), (), s32[]{:S(2)}) async-start(), calls=%async_computation.2 | async-start | bytes 5013504 | tf_op jit(solution)/shard_map/all_gather | solution.py:685
  8.8 6.0 %collective-permute-start.1 = (bf16[32,258]{1,0:T(8,128)(2,1)S(1)}, bf16[32,258]{1,0:T(8,128)(2,1)S(1)}, u32[]{:S(2)}, u32[]{:S(2)}) collective-permute-start(bf16[32,258]{1,0:T(8,128)(2,1)S(1)} %pad_maximum_fusion.10), channel_id=1, source_target_pairs={{0,1},{1,0},{2,3},{3,2},{4,5},{5,4},{6,7},{7,6},{8,9},{9,8},{10,11... | collective-permute-start | bytes 49544 | tf_op jit(solution)/shard_map/ppermute | solution.py:611
  17.2 130.3 %all-gather.5.cloned.1.call-start = ((), (), s32[]{:S(2)}) async-start(), calls=%async_computation.3 | async-start | bytes 8912896 | tf_op jit(solution)/shard_map/all_gather | solution.py:689
  20.1 504.6 %reduce-scatter.2.cloned.1.call-start = ((), (), s32[]{:S(2)}) async-start(), calls=%async_computation.4 | async-start | bytes 6684672 | tf_op jit(solution)/shard_map/reduce_scatter | solution.py:735
  20.7 52.2 %copy-start.10 = (bf16[512,1024]{0,1:T(8,128)(2,1)}, bf16[512,1024]{0,1:T(8,128)(2,1)S(1)}, u32[]{:S(2)}) copy-start(bf16[512,1024]{0,1:T(8,128)(2,1)S(1)} %copy.56) | copy-start | bytes 3145732
  20.7 24.7 %collective-permute-start = (bf16[512,1024]{0,1:T(8,128)(2,1)S(1)}, bf16[512,1024]{0,1:T(8,128)(2,1)S(1)}, u32[]{:S(2)}, u32[]{:S(2)}) collective-permute-start(bf16[512,1024]{0,1:T(8,128)(2,1)S(1)} %copy.56), channel_id=1, source_target_pairs={{0,1},{1,0},{2,3},{3,2},{4,5},{5,4},{6,7},{7,6},{8,9},{9,8},{10,11... | collective-permute-start | bytes 3145736 | tf_op jit(solution)/shard_map/ppermute | solution.py:611
  45.4 27.5 %copy-start.15 = (bf16[512,1024]{0,1:T(8,128)(2,1)}, bf16[512,1024]{0,1:T(8,128)(2,1)S(1)}, u32[]{:S(2)}) copy-start(bf16[512,1024]{0,1:T(8,128)(2,1)S(1)} %collective-permute-done) | copy-start | bytes 3145732
  154.4 48.8 %collective-permute-start.2 = (bf16[1024,1024]{0,1:T(8,128)(2,1)}, bf16[1024,1024]{0,1:T(8,128)(2,1)}, u32[]{:S(2)}, u32[]{:S(2)}) collective-permute-start(bf16[1024,1024]{0,1:T(8,128)(2,1)} %add_convert_fusion), channel_id=1, source_target_pairs={{0,1},{1,0},{2,3},{3,2},{4,5},{5,4},{6,7},{7,6},{8,9},{9,8},{10,11... | collective-permute-start | bytes 6291464 | tf_op jit(solution)/shard_map/ppermute | solution.py:611
  158.1 66.7 %collective-permute-start.4 = (bf16[512,1024]{0,1:T(8,128)(2,1)}, bf16[512,1024]{0,1:T(8,128)(2,1)S(1)}, u32[]{:S(2)}, u32[]{:S(2)}) collective-permute-start(bf16[512,1024]{0,1:T(8,128)(2,1)} %copy.66), channel_id=1, source_target_pairs={{0,1},{1,0},{2,3},{3,2},{4,5},{5,4},{6,7},{7,6},{8,9},{9,8},{10,11... | collective-permute-start | bytes 3145736 | tf_op jit(solution)/shard_map/ppermute | solution.py:611
  203.1 21.7 %slice-start = ((s8[8388608]{0:T(1024)(128)(4,1)}), s8[4194304]{0:T(1024)(128)(4,1)S(1)}, s32[]{:S(2)}) async-start(s8[8388608]{0:T(1024)(128)(4,1)} %bitcast.51), calls=%async_computation.5 | async-start | bytes 8388608
  208.1 16.7 %copy-start.18 = (bf16[512,1024]{0,1:T(8,128)(2,1)S(1)}, bf16[512,1024]{0,1:T(8,128)(2,1)}, u32[]{:S(2)}) copy-start(bf16[512,1024]{0,1:T(8,128)(2,1)} %copy.66) | copy-start | bytes 3145732
  239.0 47.3 %collective-permute-start.5 = (bf16[1024,1024]{0,1:T(8,128)(2,1)}, bf16[1024,1024]{0,1:T(8,128)(2,1)}, u32[]{:S(2)}, u32[]{:S(2)}) collective-permute-start(bf16[1024,1024]{0,1:T(8,128)(2,1)} %fusion.26), channel_id=1, source_target_pairs={{0,1},{1,0},{2,3},{3,2},{4,5},{5,4},{6,7},{7,6},{8,9},{9,8},{10,11... | collective-permute-start | bytes 6291464 | tf_op jit(solution)/shard_map/ppermute | solution.py:611
  240.5 50.9 %copy-start.8 = (f32[1024,1024]{0,1:T(8,128)S(1)}, f32[1024,1024]{0,1:T(8,128)}, u32[]{:S(2)}) copy-start(f32[1024,1024]{0,1:T(8,128)} %copy-done.7) | copy-start | bytes 12582916
  240.5 50.9 %copy-start.19 = (bf16[512,1024]{0,1:T(8,128)(2,1)S(1)}, bf16[512,1024]{0,1:T(8,128)(2,1)}, u32[]{:S(2)}) copy-start(bf16[512,1024]{0,1:T(8,128)(2,1)} %copy.66) | copy-start | bytes 3145732
  240.5 50.9 %copy-start.24 = (bf16[512,1024]{0,1:T(8,128)(2,1)S(1)}, bf16[512,1024]{0,1:T(8,128)(2,1)}, u32[]{:S(2)}) copy-start(bf16[512,1024]{0,1:T(8,128)(2,1)} %copy-done.23) | copy-start | bytes 3145732
  304.3 45.3 %slice-start.2 = ((s8[4718592]{0:T(1024)(128)(4,1)}), s8[4194304]{0:T(1024)(128)(4,1)S(1)}, s32[]{:S(2)}) async-start(s8[4718592]{0:T(1024)(128)(4,1)} %bitcast.54), calls=%async_computation.7 | async-start | bytes 8388608
  320.3 29.4 %copy-start.11 = (bf16[512,1024]{0,1:T(8,128)(2,1)S(1)}, bf16[512,1024]{0,1:T(8,128)(2,1)}, u32[]{:S(2)}) copy-start(bf16[512,1024]{0,1:T(8,128)(2,1)} %copy-done.10) | copy-start | bytes 3145732
  320.4 29.3 %copy-start.16 = (bf16[512,1024]{0,1:T(8,128)(2,1)S(1)}, bf16[512,1024]{0,1:T(8,128)(2,1)}, u32[]{:S(2)}) copy-start(bf16[512,1024]{0,1:T(8,128)(2,1)} %copy-done.15) | copy-start | bytes 3145732
  320.4 29.3 %slice-start.3 = ((s8[4718592]{0:T(1024)(128)(4,1)}), s8[524288]{0:T(1024)(128)(4,1)S(1)}, s32[]{:S(2)}) async-start(s8[4718592]{0:T(1024)(128)(4,1)} %bitcast.54), calls=%async_computation.8 | async-start | bytes 1048576
  384.6 13.4 %collective-permute-start.7 = (bf16[8,64,3456]{2,1,0:T(8,128)(2,1)}, bf16[8,64,3456]{2,1,0:T(8,128)(2,1)}, u32[]{:S(2)}, u32[]{:S(2)}) collective-permute-start(bf16[8,64,3456]{2,1,0:T(8,128)(2,1)} %dynamic-slice_bitcast_fusion), channel_id=1, source_target_pairs={{0,2},{2,0},{4,6},{6,4},{8,10},{10,8},{12,14},{14,12},{16,18},{18,... | collective-permute-start | bytes 10616840 | tf_op jit(solution)/shard_map/ppermute | solution.py:639
  403.7 125.0 %all-to-all-start = ((bf16[8,64,3456]{2,1,0:T(8,128)(2,1)}), bf16[8,64,3456]{2,1,0:T(8,128)(2,1)}, u32[]{:S(2)}, u32[]{:S(2)}) async-start(bf16[8,64,3456]{2,1,0:T(8,128)(2,1)} %fusion), calls=%async_computation | async-start | bytes 7077888 | tf_op jit(solution)/shard_map/all_to_all | solution.py:642
  416.0 26.4 %collective-permute-start.3 = (bf16[512,1024]{0,1:T(8,128)(2,1)}, bf16[512,1024]{0,1:T(8,128)(2,1)}, u32[]{:S(2)}, u32[]{:S(2)}) collective-permute-start(bf16[512,1024]{0,1:T(8,128)(2,1)} %constant_dynamic-slice_fusion.1), channel_id=1, source_target_pairs={{0,1},{1,0},{2,3},{3,2},{4,5},{5,4},{6,7},{7,6},{8,9},{9,8},{10,11... | collective-permute-start | bytes 3145736 | tf_op jit(solution)/shard_map/ppermute | solution.py:611
  418.5 44.6 %collective-permute-start.6 = (bf16[512,1024]{0,1:T(8,128)(2,1)}, bf16[512,1024]{0,1:T(8,128)(2,1)}, u32[]{:S(2)}, u32[]{:S(2)}) collective-permute-start(bf16[512,1024]{0,1:T(8,128)(2,1)} %constant_dynamic-slice_fusion), channel_id=1, source_target_pairs={{0,1},{1,0},{2,3},{3,2},{4,5},{5,4},{6,7},{7,6},{8,9},{9,8},{10,11... | collective-permute-start | bytes 3145736 | tf_op jit(solution)/shard_map/ppermute | solution.py:611
  532.4 5.9 %collective-permute-start.8 = (f32[9536]{0:T(1024)S(1)}, f32[9536]{0:T(1024)S(1)}, u32[]{:S(2)}, u32[]{:S(2)}) collective-permute-start(f32[9536]{0:T(1024)S(1)} %pad_maximum_fusion.9), channel_id=1, source_target_pairs={{0,1},{1,0},{2,3},{3,2},{4,5},{5,4},{6,7},{7,6},{8,9},{9,8},{10,11... | collective-permute-start | bytes 114440 | tf_op jit(solution)/shard_map/ppermute | solution.py:611
  (24 other events, 197.4 us)
Sparse Core Ops, SparseCore 0:
  17.4 53.9 all-gather.2
  74.0 73.4 all-gather.4
  398.2 126.4 reduce-scatter.1

commit v2 on v1

--- a/solution.py
+++ b/solution.py
@@ -1,3 +1,4 @@
+import functools
 import math
 
 import jax
@@ -13,6 +14,8 @@
 LANES = 128
 QBLOCK = 256
 HEAD_ROWS = 16
+ROW_PARTS = 2
+HIDDEN_BLOCK = 512
 
 highest = lax.Precision.HIGHEST
 epsilon = 1e-05
@@ -24,6 +27,7 @@
 NN = (((1,), (0,)), ((), ()))
 NT = (((1,), (1,)), ((), ()))
 TN = (((0,), (0,)), ((), ()))
+TT = (((0,), (1,)), ((), ()))
 
 
 def mm(left, right, dims=NN):
@@ -142,50 +146,36 @@
     y_ref,
     dg_ref,
     h_ref,
-    att_ref,
     cx_ref,
     cbc_ref,
     hp_ref,
     hpt_ref,
-    dproj_ref,
-    wide_ref,
-    bc_acc_ref,
-    head_ref,
-    state,
-    ext_u,
-    ext_bc,
-    after_u,
-    after_bc,
-    da_rows,
+    carry_in_ref,
+    *rest,
+    is_start_part,
 ):
-    chunks = LEN // CHUNK
+    dproj_ref, carry_ref, ext_u, ext_bc, after_u, after_bc, da_rows = rest[-7:]
     step_id = pl.program_id(0)
-    within = lax.rem(step_id, chunks)
     inner_cols = u_ref.shape[1]
     bc_cols = bc_ref.shape[1]
     pairs = inner_cols // LANES
     states = bc_cols // 2
     taps = cx_ref.shape[0] - 1
+    state = carry_ref.at[0:states, :]
+    kept_u = carry_ref.at[states : states + 8, :]
+    wide_ref = carry_ref.at[states + 8 : states + 16, :]
+    kept_bc = carry_ref.at[states + 16 : states + 24, 0:bc_cols]
+    bc_acc_ref = carry_ref.at[states + 24 : states + 32, 0:bc_cols]
+    head_ref = carry_ref.at[states + 32 : states + 32 + 2 * HEAD_ROWS, 0:CHUNK]
 
     @pl.when(step_id == 0)
     def _():
-        wide_ref[...] = jnp.zeros_like(wide_ref)
-        bc_acc_ref[...] = jnp.zeros_like(bc_acc_ref)
-        head_ref[...] = jnp.zeros_like(head_ref)
+        carry_ref[...] = carry_in_ref[...]
         da_rows[...] = jnp.zeros_like(da_rows)
 
-    @pl.when(within == 0)
-    def _():
-        state[...] = jnp.zeros_like(state)
-        after_u[CHUNK:, :] = jnp.zeros_like(after_u[CHUNK:, :])
-        after_bc[CHUNK:, :] = jnp.zeros_like(after_bc[CHUNK:, :])
-
-    @pl.when(within > 0)
-    def _():
-        after_u[CHUNK:, :] = after_u[0:8, :]
-        after_bc[CHUNK:, :] = after_bc[0:8, :]
-
-    is_start = within == chunks - 1
+    after_u[CHUNK:, :] = kept_u[...]
+    after_bc[CHUNK:, :] = kept_bc[...]
+    is_start = jnp.logical_and(is_start_part, step_id == pl.num_programs(0) - 1)
     ext_u[0:8, :] = jnp.where(is_start, 0.0, u_before_ref[...])
     ext_bc[0:8, :] = jnp.where(is_start, 0.0, bc_before_ref[...])
     ext_u[8 : 8 + CHUNK, :] = u_ref[...]
@@ -321,9 +311,9 @@
                 conv_grad * ext_ref[5 + k : 5 + k + CHUNK, :], axis=0, keepdims=True
             )
         acc_ref[taps : taps + 1, :] += jnp.sum(conv_grad, axis=0, keepdims=True)
-    att_cols = att_ref.shape[1]
-    dproj_ref[:, base + bc_cols : base + bc_cols + att_cols] = att_ref[...]
-    dproj_ref[:, base + bc_cols + att_cols :] = raw_grad_cols.astype(bf16)
+    dproj_ref[:, base + bc_cols :] = raw_grad_cols.astype(bf16)
+    kept_u[...] = after_u[0:8, :]
+    kept_bc[...] = after_bc[0:8, :]
 
 
 def swap_halves(values):
@@ -343,8 +333,8 @@
     return values * cosine - swap_halves(values) * sine
 
 
-def keys_and_values(kv_ref, cos_ref, sin_ref):
-    kv = kv_ref[...]
+def keys_and_values(qkv_ref, cos_ref, sin_ref):
+    kv = qkv_ref[:, qkv_ref.shape[1] - LANES :]
     low = low_lanes(kv.shape)
     turned = rotated(kv, cos_ref[...], sin_ref[...])
     keys = jnp.where(low, turned, pltpu.roll(turned, P_SIZE, axis=1)).astype(bf16)
@@ -361,19 +351,19 @@
     return weights * (1.0 / jnp.sum(weights, axis=1, keepdims=True))
 
 
-def rotated_queries(q_ref, cos_ref, sin_ref, here, at):
-    turned = rotated(q_ref[here, at], cos_ref[here, :], sin_ref[here, :]).astype(bf16)
+def rotated_queries(qkv_ref, cos_ref, sin_ref, here, at):
+    turned = rotated(qkv_ref[here, at], cos_ref[here, :], sin_ref[here, :]).astype(bf16)
     return turned * jnp.asarray(P_SIZE**-0.5, bf16)
 
 
-def attention_forward_kernel(q_ref, kv_ref, cos_ref, sin_ref, o_ref):
-    keys, values = keys_and_values(kv_ref, cos_ref, sin_ref)
+def attention_forward_kernel(qkv_ref, cos_ref, sin_ref, o_ref):
+    keys, values = keys_and_values(qkv_ref, cos_ref, sin_ref)
     for block in range(LEN // QBLOCK):
         here = slice(block * QBLOCK, (block + 1) * QBLOCK)
         seen = (block + 1) * QBLOCK
-        for pair in range(q_ref.shape[1] // LANES):
+        for pair in range(o_ref.shape[1] // LANES):
             at = slice(pair * LANES, (pair + 1) * LANES)
-            queries = rotated_queries(q_ref, cos_ref, sin_ref, here, at)
+            queries = rotated_queries(qkv_ref, cos_ref, sin_ref, here, at)
             low = low_lanes(queries.shape)
             zero = jnp.zeros_like(queries)
             outs = []
@@ -384,19 +374,23 @@
 
 
 def attention_backward_kernel(
-    q_ref, kv_ref, cos_ref, sin_ref, do_ref, grad_ref, key_grad, value_grad
+    qkv_ref, cos_ref, sin_ref, *rest, parts
 ):
-    keys, values = keys_and_values(kv_ref, cos_ref, sin_ref)
+    grad_ref, key_grad, value_grad = rest[-3:]
+    do_refs = rest[:parts]
+    keys, values = keys_and_values(qkv_ref, cos_ref, sin_ref)
     key_grad[...] = jnp.zeros_like(key_grad)
     value_grad[...] = jnp.zeros_like(value_grad)
-    q_cols = q_ref.shape[1]
+    q_cols = do_refs[0].shape[1]
+    block_rows = do_refs[0].shape[0]
     for block in range(LEN // QBLOCK):
         here = slice(block * QBLOCK, (block + 1) * QBLOCK)
         seen = (block + 1) * QBLOCK
         for pair in range(q_cols // LANES):
             at = slice(pair * LANES, (pair + 1) * LANES)
-            queries = rotated_queries(q_ref, cos_ref, sin_ref, here, at)
-            out_grad = do_ref[here, at].astype(bf16)
+            queries = rotated_queries(qkv_ref, cos_ref, sin_ref, here, at)
+            inside = block * QBLOCK % block_rows
+            out_grad = do_refs[block * QBLOCK // block_rows][inside : inside + QBLOCK, at]
             low = low_lanes(queries.shape)
             zero = jnp.zeros_like(queries)
             parts = []
@@ -433,6 +427,14 @@
     )
 
 
+def short_kernel():
+    return pl.CostEstimate(flops=1000, bytes_accessed=1000, transcendentals=0)
+
+
+def any_place():
+    return pl.BlockSpec(memory_space=pl.ANY)
+
+
 def vmem_params(megabytes):
     return pltpu.CompilerParams(
         vmem_limit_bytes=megabytes * 1024 * 1024, dimension_semantics=("arbitrary",)
@@ -443,7 +445,7 @@
     rows_all = proj.shape[0]
     states = bc_cols // 2
     bc_at = 2 * inner_cols // bc_cols
-    dt_at = proj.shape[1] // LANES - 1
+    dt_at = (2 * inner_cols + bc_cols) // LANES
     steps = rows_all // CHUNK
     return pl.pallas_call(
         mixer_forward_kernel,
@@ -473,33 +475,30 @@
             pltpu.VMEM((CHUNK + 8, bc_cols), f32),
         ],
         compiler_params=vmem_params(32),
-        cost_estimate=pl.CostEstimate(
-            flops=rows_all * inner_cols * 1200,
-            bytes_accessed=rows_all * inner_cols * 14,
-            transcendentals=rows_all * inner_cols * 4,
-        ),
+        cost_estimate=short_kernel(),
         name="mixer_forward",
     )(proj, proj, proj, proj, conv_x, conv_bc, heads)
 
 
-def mixer_backward(proj, y, dg, held, att_grad, conv_x, conv_bc, heads, inner_cols, bc_cols):
+def mixer_backward(proj, y, dg, held, carry, whole, part, params, inner_cols, bc_cols, *deps):
     rows_all = proj.shape[0]
     states = bc_cols // 2
     bc_at = 2 * inner_cols // bc_cols
-    dt_at = proj.shape[1] // LANES - 1
-    steps = rows_all // CHUNK
-    chunks = LEN // CHUNK
+    dt_at = (2 * inner_cols + bc_cols) // LANES
+    steps = dg.shape[0] // CHUNK
     per = CHUNK // 8
+    grad_cols = 2 * inner_cols + bc_cols + LANES
 
     def at(i):
-        return i // chunks * chunks + (chunks - 1 - i % chunks)
+        return part * steps + steps - 1 - i
 
     def before(i):
         return jnp.maximum(at(i) * per - 1, 0)
 
-    heads_t = heads[:, :HEAD_ROWS].T
+    held_out = [] if whole is None else [whole]
+    earlier = held_out + list(deps)
     return pl.pallas_call(
-        mixer_backward_kernel,
+        functools.partial(mixer_backward_kernel, is_start_part=part == 0),
         grid=(steps,),
         in_specs=[
             pl.BlockSpec((CHUNK, inner_cols), lambda i: (at(i), 0)),
@@ -509,106 +508,360 @@
             pl.BlockSpec((8, inner_cols), lambda i: (before(i), 1)),
             pl.BlockSpec((8, bc_cols), lambda i: (before(i), bc_at)),
             pl.BlockSpec((CHUNK, inner_cols), lambda i: (at(i), 0)),
-            pl.BlockSpec((CHUNK, inner_cols), lambda i: (at(i), 0)),
+            pl.BlockSpec((CHUNK, inner_cols), lambda i: (steps - 1 - i, 0)),
             pl.BlockSpec((states, inner_cols), lambda i: (at(i), 0)),
-            pl.BlockSpec((CHUNK, att_grad.shape[1]), lambda i: (at(i), 0)),
-            pl.BlockSpec(conv_x.shape, lambda i: (0, 0)),
-            pl.BlockSpec(conv_bc.shape, lambda i: (0, 0)),
-            pl.BlockSpec(heads.shape, lambda i: (0, 0)),
-            pl.BlockSpec(heads_t.shape, lambda i: (0, 0)),
-        ],
+        ]
+        + [pl.BlockSpec(value.shape, lambda i: (0, 0)) for value in params]
+        + [pl.BlockSpec(carry.shape, lambda i: (0, 0))]
+        + [pl.BlockSpec(memory_space=pl.ANY) for _ in earlier],
         out_specs=[
-            pl.BlockSpec((CHUNK, proj.shape[1]), lambda i: (at(i), 0)),
-            pl.BlockSpec((8, inner_cols), lambda i: (0, 0)),
-            pl.BlockSpec((8, bc_cols), lambda i: (0, 0)),
-            pl.BlockSpec((2 * HEAD_ROWS, CHUNK), lambda i: (0, 0)),
+            pl.BlockSpec((CHUNK, grad_cols), lambda i: (at(i), 0)),
+            pl.BlockSpec(carry.shape, lambda i: (0, 0)),
         ],
         out_shape=[
-            jax.ShapeDtypeStruct(proj.shape, bf16),
-            jax.ShapeDtypeStruct((8, inner_cols), f32),
-            jax.ShapeDtypeStruct((8, bc_cols), f32),
-            jax.ShapeDtypeStruct((2 * HEAD_ROWS, CHUNK), f32),
+            jax.ShapeDtypeStruct((rows_all, grad_cols), bf16),
+            jax.ShapeDtypeStruct(carry.shape, f32),
         ],
         scratch_shapes=[
-            pltpu.VMEM((states, inner_cols), f32),
             pltpu.VMEM((CHUNK + 8, inner_cols), f32),
             pltpu.VMEM((CHUNK + 8, bc_cols), f32),
             pltpu.VMEM((CHUNK + 8, inner_cols), f32),
             pltpu.VMEM((CHUNK + 8, bc_cols), f32),
             pltpu.VMEM((HEAD_ROWS, CHUNK), f32),
         ],
+        input_output_aliases={14: 0} if held_out else {},
         compiler_params=vmem_params(48),
-        cost_estimate=pl.CostEstimate(
-            flops=rows_all * inner_cols * 4000,
-            bytes_accessed=rows_all * inner_cols * 26,
-            transcendentals=rows_all * inner_cols * 8,
-        ),
+        cost_estimate=short_kernel(),
         name="mixer_backward",
-    )(
-        proj, proj, proj, proj, proj, proj, y, dg, held, att_grad, conv_x, conv_bc, heads, heads_t
-    )
-
-
-def attention_forward(proj, tables, q_cols, q_at, kv_at):
+    )(proj, proj, proj, proj, proj, proj, y, dg, held, *params, carry, *earlier)
+
+
+def attention_forward(proj, tables, q_cols):
     rows_all = proj.shape[0]
+    cols = q_cols + LANES
     return pl.pallas_call(
         attention_forward_kernel,
         grid=(rows_all // LEN,),
         in_specs=[
-            pl.BlockSpec((LEN, q_cols), lambda i: (i, q_at)),
-            pl.BlockSpec((LEN, LANES), lambda i: (i, kv_at)),
+            pl.BlockSpec((LEN, cols), lambda i: (i, proj.shape[1] // cols - 1)),
             pl.BlockSpec((LEN, LANES), lambda i: (0, 0)),
             pl.BlockSpec((LEN, LANES), lambda i: (0, 0)),
         ],
         out_specs=pl.BlockSpec((LEN, q_cols), lambda i: (i, 0)),
         out_shape=jax.ShapeDtypeStruct((rows_all, q_cols), bf16),
         compiler_params=vmem_params(40),
-        cost_estimate=pl.CostEstimate(
-            flops=rows_all * LEN * q_cols * 8,
-            bytes_accessed=rows_all * q_cols * 12,
-            transcendentals=rows_all * LEN * 3,
-        ),
+        cost_estimate=short_kernel(),
         name="attention_forward",
-    )(proj, proj, *tables)
-
-
-def attention_backward(proj, tables, out_grad, q_cols, q_at, kv_at):
+    )(proj, *tables)
+
+
+def attention_backward(proj, tables, out_grads, q_cols, *deps):
     rows_all = proj.shape[0]
+    cols = q_cols + LANES
     return pl.pallas_call(
-        attention_backward_kernel,
+        functools.partial(attention_backward_kernel, parts=len(out_grads)),
         grid=(rows_all // LEN,),
         in_specs=[
-            pl.BlockSpec((LEN, q_cols), lambda i: (i, q_at)),
-            pl.BlockSpec((LEN, LANES), lambda i: (i, kv_at)),
+            pl.BlockSpec((LEN, cols), lambda i: (i, proj.shape[1] // cols - 1)),
             pl.BlockSpec((LEN, LANES), lambda i: (0, 0)),
             pl.BlockSpec((LEN, LANES), lambda i: (0, 0)),
-            pl.BlockSpec((LEN, q_cols), lambda i: (i, out_grad.shape[1] // q_cols - 1)),
-        ],
-        out_specs=pl.BlockSpec((LEN, q_cols + LANES), lambda i: (i, 0)),
-        out_shape=jax.ShapeDtypeStruct((rows_all, q_cols + LANES), bf16),
+        ]
+        + [
+            pl.BlockSpec((grad.shape[0], q_cols), lambda i: (0, grad.shape[1] // q_cols - 1))
+            for grad in out_grads
+        ]
+        + [any_place() for _ in deps],
+        out_specs=pl.BlockSpec((LEN, cols), lambda i: (i, 0)),
+        out_shape=jax.ShapeDtypeStruct((rows_all, cols), bf16),
         scratch_shapes=[pltpu.VMEM((LEN, LANES), f32), pltpu.VMEM((LEN, LANES), f32)],
         compiler_params=vmem_params(48),
-        cost_estimate=pl.CostEstimate(
-            flops=rows_all * LEN * q_cols * 20,
-            bytes_accessed=rows_all * q_cols * 16,
-            transcendentals=rows_all * LEN * 3,
+        cost_estimate=short_kernel(),
+        name="attention_backward",
+    )(proj, *tables, *out_grads, *deps)
+
+
+def feed_forward_kernel(
+    x_ref, low_ref, arrived_ref, gain_ref, cot_ref, gate_w_ref, up_w_ref, down_w_ref, *rest
+):
+    mid_ref, n2_ref, act_ref, gate_grad_ref, up_grad_ref, grad_ref, normed, total = rest[-8:]
+    step_id = pl.program_id(0)
+
+    @pl.when(step_id == 0)
+    def _():
+        mid = x_ref[...].astype(f32) + (low_ref[...].astype(f32) + arrived_ref[...].astype(f32))
+        inverse = lax.rsqrt(jnp.mean(mid * mid, axis=-1, keepdims=True) + epsilon)
+        mid_ref[...] = mid
+        value = (mid * inverse * gain_ref[...]).astype(bf16)
+        normed[...] = value
+        n2_ref[...] = value
+        total[...] = jnp.zeros_like(total)
+
+    n2 = normed[...]
+    gate = mm(n2, gate_w_ref[...])
+    up = mm(n2, up_w_ref[...])
+    sig = sigmoid(gate)
+    silu = gate * sig
+    act_ref[...] = (silu * up).astype(bf16)
+    grad = mm(cot_ref[...], down_w_ref[...])
+    gate_grad = (grad * up * (sig * (1.0 + gate * (1.0 - sig)))).astype(bf16)
+    up_grad = (grad * silu).astype(bf16)
+    gate_grad_ref[...] = gate_grad
+    up_grad_ref[...] = up_grad
+    total[...] += mm(gate_grad, gate_w_ref[...], NT) + mm(up_grad, up_w_ref[...], NT)
+
+    @pl.when(step_id == pl.num_programs(0) - 1)
+    def _():
+        grad_ref[...] = total[...].astype(bf16)
+
+
+def feed_forward(tokens, low, arrived, gain, cotangent, w_out, buffers, part, *deps):
+    rows, width = low.shape
+    hidden = w_out.shape[1] // 3
+    blocks = hidden // HIDDEN_BLOCK
+    here = pl.BlockSpec((rows, width), lambda h: (part, 0))
+    only = pl.BlockSpec((rows, width), lambda h: (0, 0))
+    block_out = pl.BlockSpec((rows, HIDDEN_BLOCK), lambda h: (part, h))
+
+    def weight(offset):
+        return pl.BlockSpec((width, HIDDEN_BLOCK), lambda h: (0, offset * blocks + h))
+
+    whole = tokens.shape[0]
+    return pl.pallas_call(
+        feed_forward_kernel,
+        grid=(blocks,),
+        in_specs=[
+            here,
+            only,
+            only,
+            pl.BlockSpec((1, width), lambda h: (0, 0)),
+            here,
+            weight(0),
+            weight(1),
+            weight(2),
+        ]
+        + [any_place() for _ in (*buffers, *deps)],
+        out_specs=[here, here, block_out, block_out, block_out, only],
+        out_shape=[
+            jax.ShapeDtypeStruct((whole, width), f32),
+            jax.ShapeDtypeStruct((whole, width), bf16),
+            jax.ShapeDtypeStruct((whole, hidden), bf16),
+            jax.ShapeDtypeStruct((whole, hidden), bf16),
+            jax.ShapeDtypeStruct((whole, hidden), bf16),
+            jax.ShapeDtypeStruct((rows, width), bf16),
+        ],
+        scratch_shapes=[pltpu.VMEM((rows, width), bf16), pltpu.VMEM((rows, width), f32)],
+        input_output_aliases={8 + i: i for i in range(len(buffers))},
+        compiler_params=vmem_params(40),
+        cost_estimate=short_kernel(),
+        name="feed_forward",
+    )(tokens, low, arrived, gain, cotangent, w_out, w_out, w_out, *buffers, *deps)
+
+
+def branch_grad_kernel(mid_ref, low_ref, arrived_ref, gain_ref, cot_ref, w_ref, *rest):
+    hidden_ref, branch_ref, mix_ref = rest[-3:]
+    mid = mid_ref[...]
+    inverse = lax.rsqrt(jnp.mean(mid * mid, axis=-1, keepdims=True) + epsilon)
+    unit = mid * inverse
+    low = low_ref[...].astype(f32)
+    scaled = (low + arrived_ref[...].astype(f32)) * gain_ref[...]
+    inner = jnp.mean(scaled * unit, axis=-1, keepdims=True)
+    grad = cot_ref[...].astype(f32) + (scaled - unit * inner) * inverse
+    hidden_ref[...] = grad
+    rounded = grad.astype(bf16)
+    branch_ref[...] = rounded
+    mix_ref[...] = mm(rounded, w_ref[...]).astype(bf16)
+
+
+def branch_grad(mid, low, arrived, gain, cotangent, w_in, buffers, part, *deps):
+    rows, width = low.shape
+    whole = cotangent.shape[0]
+    mix_cols = width
+    here = pl.BlockSpec((rows, width), lambda i: (part, 0))
+    only = pl.BlockSpec((rows, width), lambda i: (0, 0))
+    row = pl.BlockSpec((1, width), lambda i: (0, 0))
+    return pl.pallas_call(
+        branch_grad_kernel,
+        grid=(1,),
+        in_specs=[here, only, only, row, here, pl.BlockSpec(w_in.shape, lambda i: (0, 0))]
+        + [any_place() for _ in (*buffers, *deps)],
+        out_specs=[here, here, pl.BlockSpec((rows, mix_cols), lambda i: (0, 0))],
+        out_shape=[
+            jax.ShapeDtypeStruct((whole, width), f32),
+            jax.ShapeDtypeStruct((whole, width), bf16),
+            jax.ShapeDtypeStruct((rows, mix_cols), bf16),
+        ],
+        input_output_aliases={6 + i: i for i in range(len(buffers))},
+        compiler_params=vmem_params(32),
+        cost_estimate=short_kernel(),
+        name="branch_grad",
+    )(mid, low, arrived, gain, cotangent, w_in, *buffers, *deps)
+
+
+def weight_grad_kernel(left_ref, right_ref, *rest, has_arrived):
+    total = mm(left_ref[...], right_ref[...])
+    if has_arrived:
+        total = (total + rest[0][...].astype(f32)).astype(bf16)
+        rows = total.shape[0] // 2
+        rest[-2][...] = total[:rows]
+        rest[-1][...] = total[rows:]
+    else:
+        rest[-1][...] = total.astype(bf16)
+
+
+def weight_grad(
+    left, half, right, right_start, right_cols, buffers, start, columns, arrived, deps
+):
+    block = 384 if right_cols % 384 == 0 else 256
+    offset = right_start // block
+    rows, tokens = left.shape
+    if half is not None:
+        rows //= 2
+    first = start // block
+    extra = [] if arrived is None else [arrived]
+    outs = 1 + len(extra)
+    return pl.pallas_call(
+        functools.partial(weight_grad_kernel, has_arrived=arrived is not None),
+        grid=(right_cols // block,),
+        in_specs=[
+            pl.BlockSpec((rows, tokens), lambda n: (half or 0, 0)),
+            pl.BlockSpec((tokens, block), lambda n: (0, offset + n)),
+        ]
+        + [pl.BlockSpec((rows, block), lambda n: (0, first + n)) for _ in extra]
+        + [any_place() for _ in (*buffers, *deps)],
+        out_specs=[pl.BlockSpec((rows // outs, block), lambda n: (0, first + n))] * outs,
+        out_shape=[jax.ShapeDtypeStruct((rows // outs, columns), bf16)] * outs,
+        input_output_aliases={2 + len(extra) + i: i for i in range(len(buffers))},
+        compiler_params=vmem_params(24),
+        cost_estimate=short_kernel(),
+        name="weight_grad",
+    )(left, right, *extra, *buffers, *deps)
+
+
+def whole(left, right):
+    return left, right, 0, right.shape[1]
+
+
+def weight_grads(pieces, half, arrived=None, deps=(), late=()):
+    columns = sum(piece[3] for piece in pieces)
+    buffers, start = (), 0
+    for left, right, right_start, right_cols in pieces:
+        buffers = weight_grad(
+            left, half, right, right_start, right_cols, buffers, start, columns, arrived, deps
+        )
+        deps, late = late, ()
+        start += right_cols
+    return buffers[0] if arrived is None else buffers
+
+
+def product_kernel(*refs, count):
+    total = mm(refs[0][...], refs[count][...], NT)
+    for i in range(1, count):
+        total = total + mm(refs[i][...], refs[count + i][...], NT)
+    refs[-1][...] = total.astype(bf16)
+
+
+def product(pairs, *deps):
+    rows, out_cols = pairs[0][0].shape[0], pairs[0][1].shape[0]
+    block = 256
+    return pl.pallas_call(
+        functools.partial(product_kernel, count=len(pairs)),
+        grid=(out_cols // block,),
+        in_specs=[pl.BlockSpec(left.shape, lambda i: (0, 0)) for left, _, _ in pairs]
+        + [
+            pl.BlockSpec((block, left.shape[1]), lambda i, at=at: (i, at))
+            for left, _, at in pairs
+        ]
+        + [any_place() for _ in deps],
+        out_specs=pl.BlockSpec((rows, block), lambda i: (0, i)),
+        out_shape=jax.ShapeDtypeStruct((rows, out_cols), bf16),
+        compiler_params=vmem_params(32),
+        cost_estimate=short_kernel(),
+        name="product",
+    )(*[left for left, _, _ in pairs], *[right for _, right, _ in pairs], *deps)
+
+
+def halves_kernel(side_ref, *refs, count):
+    total = mm(refs[0][...], refs[count][...], NT)
+    for i in range(1, count):
+        total = total + mm(refs[i][...], refs[count + i][...], NT)
+    there_ref, own_ref, held = refs[-3:]
+    held[...] = total.astype(bf16)
+    rows = there_ref.shape[0]
+    other = pl.multiple_of((1 - side_ref[0]) * rows, rows)
+    there_ref[...] = held[pl.ds(other, rows), :]
+    own_ref[...] = held[pl.ds(pl.multiple_of(side_ref[0] * rows, rows), rows), :]
+
+
+def product_halves(side, pairs, *deps):
+    rows, out_cols = pairs[0][0].shape[0], pairs[0][1].shape[0]
+    block = 256
+    return pl.pallas_call(
+        functools.partial(halves_kernel, count=len(pairs)),
+        grid=(out_cols // block,),
+        in_specs=[pl.BlockSpec(memory_space=pltpu.SMEM)]
+        + [pl.BlockSpec(left.shape, lambda i: (0, 0)) for left, _, _ in pairs]
+        + [
+            pl.BlockSpec((block, left.shape[1]), lambda i, at=at: (i, at))
+            for left, _, at in pairs
+        ]
+        + [any_place() for _ in deps],
+        out_specs=[pl.BlockSpec((rows // 2, block), lambda i: (0, i))] * 2,
+        out_shape=[jax.ShapeDtypeStruct((rows // 2, out_cols), bf16)] * 2,
+        scratch_shapes=[pltpu.VMEM((rows, block), bf16)],
+        compiler_params=vmem_params(32),
+        cost_estimate=short_kernel(),
+        name="product_halves",
+    )(side, *[left for left, _, _ in pairs], *[right for _, right, _ in pairs], *deps)
+
+
+def layer_out_kernel(side_ref, mid_ref, own_ref, there_ref, *rest):
+    total = own_ref[...].astype(f32) + there_ref[...].astype(f32)
+    rest[-1][...] = (mid_ref[...] + total).astype(bf16)
+
+
+def input_grad_kernel(side_ref, grad_ref, own_ref, there_ref, x_ref, gain_ref, *rest):
+    x = x_ref[...].astype(f32)
+    inverse = lax.rsqrt(jnp.mean(x * x, axis=-1, keepdims=True) + epsilon)
+    unit = x * inverse
+    scaled = (own_ref[...].astype(f32) + there_ref[...].astype(f32)) * gain_ref[...]
+    inner = jnp.mean(scaled * unit, axis=-1, keepdims=True)
+    rest[-1][...] = (grad_ref[...] + (scaled - unit * inner) * inverse).astype(bf16)
+
+
+def own_rows(kernel, side, whole_parts, parts, row, deps):
+    rows, columns = parts[0].shape
+    block = 128
+    steps = rows // block
+    here = pl.BlockSpec((block, columns), lambda i, side: (i, 0))
+    mine = pl.BlockSpec((block, columns), lambda i, side: (side[0] * steps + i, 0))
+    return pl.pallas_call(
+        kernel,
+        grid_spec=pltpu.PrefetchScalarGridSpec(
+            num_scalar_prefetch=1,
+            grid=(steps,),
+            in_specs=[mine for _ in whole_parts]
+            + [here for _ in parts]
+            + [pl.BlockSpec(value.shape, lambda i, side: (0, 0)) for value in row]
+            + [any_place() for _ in deps],
+            out_specs=here,
         ),
-        name="attention_backward",
-    )(proj, proj, *tables, out_grad)
+        out_shape=jax.ShapeDtypeStruct((rows, columns), bf16),
+        compiler_params=vmem_params(24),
+        cost_estimate=short_kernel(),
+        name="own_rows",
+    )(side, *whole_parts, *parts, *row, *deps)
 
 
 def inverse_rms(values):
     return lax.rsqrt(jnp.mean(values * values, axis=-1, keepdims=True) + epsilon)
 
 
-def normalize_back(grad, values, inverse, gain_row):
-    unit = values * inverse
-    scaled = grad * gain_row
-    return (scaled - unit * jnp.mean(scaled * unit, axis=-1, keepdims=True)) * inverse
-
-
 def swap_tensor(values):
     return lax.ppermute(values, "tensor", [(0, 1), (1, 0)])
+
+
+def swap_dp(values, bit):
+    return lax.ppermute(values, "dp", [(i, i ^ bit) for i in range(lax.axis_size("dp"))])
 
 
 def both_halves(mine):
@@ -625,22 +878,153 @@
     return lax.dynamic_slice_in_dim(values, index * rows, rows, 0)
 
 
-def sum_own_half(values, index):
-    arrived = swap_tensor(half_rows(values, 1 - index))
-    return half_rows(values, index).astype(f32) + arrived.astype(f32)
-
-
-def scatter_sum(values, dp_count):
-    pairs = dp_count // 2
-    core = lax.rem(lax.axis_index("dp"), 2)
-    by_core = values.reshape(pairs, 2, values.shape[0] // dp_count, values.shape[1])
-    kept = lax.dynamic_index_in_dim(by_core, core, 1, keepdims=False)
-    sent = lax.dynamic_index_in_dim(by_core, 1 - core, 1, keepdims=False)
-    arrived = lax.ppermute(sent, "dp", [(i, i ^ 1) for i in range(dp_count)])
-    summed = (kept.astype(f32) + arrived.astype(f32)).astype(bf16)
-    groups = [[core_id + 2 * i for i in range(pairs)] for core_id in range(2)]
-    blocks = lax.all_to_all(summed, "dp", 0, 0, tiled=True, axis_index_groups=groups)
-    return jnp.sum(blocks.astype(f32), axis=0)
+def after(values, *earlier):
+    return pl.pallas_call(
+        lambda *refs: None,
+        in_specs=[any_place()] * (1 + len(earlier)),
+        out_specs=any_place(),
+        out_shape=jax.ShapeDtypeStruct(values.shape, values.dtype),
+        input_output_aliases={0: 0},
+        cost_estimate=short_kernel(),
+        name="after",
+    )(values, *earlier)
+
+
+def swap_tensor(values):
+    return lax.ppermute(values, "tensor", [(0, 1), (1, 0)])
+
+
+def swap_dp(values, bit):
+    return lax.ppermute(values, "dp", [(i, i ^ bit) for i in range(lax.axis_size("dp"))])
+
+
+def both_halves(mine):
+    other = swap_tensor(mine)
+    return jnp.where(
+        lax.axis_index("tensor") == 0,
+        jnp.concatenate([mine, other], axis=0),
+        jnp.concatenate([other, mine], axis=0),
+    )
+
+
+def half_rows(values, index):
+    rows = values.shape[0] // 2
+    return lax.dynamic_slice_in_dim(values, index * rows, rows, 0)
+
+
+def chosen_half(parts, index):
+    middle = len(parts) // 2
+    return jnp.where(
+        index == 0,
+        jnp.concatenate(parts[:middle], axis=0),
+        jnp.concatenate(parts[middle:], axis=0),
+    )
+
+
+def after(values, *earlier):
+    return pl.pallas_call(
+        lambda *refs: None,
+        in_specs=[any_place()] * (1 + len(earlier)),
+        out_specs=any_place(),
+        out_shape=jax.ShapeDtypeStruct(values.shape, values.dtype),
+        input_output_aliases={0: 0},
+        cost_estimate=short_kernel(),
+        name="after",
+    )(values, *earlier)
+
+
+def sum_far_kernel(own_ref, arrived_ref, *rest):
+    rest[-1][...] = (own_ref[...].astype(f32) + arrived_ref[...].astype(f32)).astype(bf16)
+
+
+def reordering(width):
+    dp_count = lax.axis_size("dp")
+    here = width // dp_count
+    me = lax.axis_index("dp")
+    core, near = lax.rem(me, 2), lax.rem(lax.div(me, 2), 2)
+    place = jnp.arange(width, dtype=jnp.int32)
+    block, inside = place // here, place % here
+    quarter, far = block // (dp_count // 4), block % (dp_count // 4)
+    block_core = jnp.where(quarter // 2 == 0, 1 - core, core)
+    block_near = jnp.where(quarter % 2 == 0, 1 - near, near)
+    source = (far * 4 + block_near * 2 + block_core) * here + inside
+    return (source[:, None] == jnp.arange(width, dtype=jnp.int32)[None, :]).astype(bf16)
+
+
+def sum_near(halves):
+    there, own = halves
+    return own, swap_dp(there, 2)
+
+
+def sum_far_kernel(me_ref, own_ref, arrived_ref, *rest, far):
+    total = (own_ref[...].astype(f32) + arrived_ref[...].astype(f32)).astype(bf16)
+    rows = total.shape[0] // far
+    scratch = rest[-1]
+    scratch[...] = total
+    for offset, out_ref in enumerate(rest[-1 - far : -1]):
+        place = lax.rem(me_ref[0] + offset, far)
+        out_ref[...] = scratch[pl.ds(pl.multiple_of(place * rows, rows), rows), :]
+
+
+def sum_far(own, arrived, *deps):
+    far = lax.axis_size("dp") // 4
+    if far > 4:
+        return (after((own.astype(f32) + arrived.astype(f32)).astype(bf16), *deps),)
+    rows, columns = own.shape
+    me = lax.div(lax.axis_index("dp"), 4).reshape(1)
+    only = pl.BlockSpec((rows, columns), lambda i: (0, 0))
+    return pl.pallas_call(
+        functools.partial(sum_far_kernel, far=far),
+        grid=(1,),
+        in_specs=[pl.BlockSpec(memory_space=pltpu.SMEM), only, only]
+        + [any_place() for _ in deps],
+        out_specs=[pl.BlockSpec((rows // far, columns), lambda i: (0, 0))] * far,
+        out_shape=[jax.ShapeDtypeStruct((rows // far, columns), bf16)] * far,
+        scratch_shapes=[pltpu.VMEM((rows, columns), bf16)],
+        compiler_params=vmem_params(24),
+        cost_estimate=short_kernel(),
+        name="sum_far",
+    )(me, own, arrived, *deps)
+
+
+def send_far(blocks):
+    far = lax.axis_size("dp") // 4
+    if far > 4:
+        groups = [[low + 4 * i for i in range(far)] for low in range(4)]
+        summed = blocks[0].reshape(far, blocks[0].shape[0] // far, blocks[0].shape[1])
+        return [lax.all_to_all(summed, "dp", 0, 0, tiled=True, axis_index_groups=groups)]
+    arrived = []
+    for offset in range(1, far):
+        moves = [(i, (i + 4 * offset) % (4 * far)) for i in range(4 * far)]
+        arrived.append(lax.ppermute(blocks[offset], "dp", moves))
+    return arrived
+
+
+def sum_last(blocks, arrived, *deps):
+    if arrived[0].ndim == 3:
+        return jnp.sum(after(arrived[0], *deps).astype(f32), axis=0)
+    total = after(blocks[0], *deps, *arrived).astype(f32)
+    for values in arrived:
+        total = total + values.astype(f32)
+    return total
+
+
+def add_kernel(left_ref, right_ref, *rest):
+    rest[-1][...] = left_ref[...] + right_ref[...]
+
+
+def added(left, right, *deps):
+    only = pl.BlockSpec(left.shape, lambda i: (0, 0))
+    return pl.pallas_call(
+        add_kernel,
+        grid=(1,),
+        in_specs=[only, only] + [any_place() for _ in deps],
+        out_specs=only,
+        out_shape=jax.ShapeDtypeStruct(left.shape, left.dtype),
+        compiler_params=vmem_params(16),
+        cost_estimate=short_kernel(),
+        name="added",
+    )(left, right, *deps)
 
 
 def local(
@@ -667,6 +1051,11 @@
     inner_cols, bc_cols, head_cols = w_zx.shape[2], w_bc.shape[1], w_dt.shape[1]
     q_cols, kv_cols = w_q.shape[1], 2 * w_kv.shape[2]
     hidden, mo_cols, ao_cols = w_gu.shape[2], w_mo.shape[0], w_ao.shape[0]
+    bc_start = 2 * inner_cols
+    dt_start = bc_start + bc_cols
+    q_start = dt_start + LANES
+    kv_start = q_start + q_cols
+    in_cols = kv_start + kv_cols
 
     shared = both_halves(jnp.concatenate([w_bc, gains.T], axis=1))
     in_pack = jnp.concatenate(
@@ -674,121 +1063,212 @@
             w_zx[:, 0],
             w_zx[:, 1],
             shared[:, :bc_cols],
-            w_q,
-            w_kv.reshape(here, kv_cols),
             w_dt,
             shared[:, bc_cols:],
             jnp.zeros((here, LANES - head_cols - 2), bf16),
+            w_q,
+            w_kv.reshape(here, kv_cols),
+            w_mo.T,
+            w_ao.T,
         ],
         axis=1,
     )
     w_in = lax.all_gather(in_pack, "dp", axis=0, tiled=True)
-    out_pack = jnp.concatenate(
-        [w_gu.reshape(here, 2 * hidden), w_down.T, w_mo.T, w_ao.T], axis=1
-    )
-    w_out = lax.all_gather(out_pack, "dp", axis=0, tiled=True)
+    out_pack = jnp.concatenate([w_gu.reshape(here, 2 * hidden), w_down.T], axis=1)
     tokens_all = both_halves(tokens)
     cotangent_all = both_halves(cotangent)
+    out_pack = after(out_pack, w_in, tokens_all, cotangent_all)
+    w_out = lax.all_gather(out_pack, "dp", axis=0, tiled=True)
     tables = rotary_tables()
-
-    gu_full = w_out[:, : 2 * hidden]
-    down_full = w_out[:, 2 * hidden : 3 * hidden]
-    mix_full = w_out[:, 3 * hidden :]
-    dt_start = w_in.shape[1] - LANES
+    order = reordering(width)
+    unchanged = jnp.eye(width, dtype=bf16)
+    kept_rows = width // 2
+
+    mix_full = w_in[:, in_cols:]
     gain_full = w_in[:, dt_start + head_cols : dt_start + head_cols + 2].T.astype(f32)
     gain_one, gain_two = gain_full[0:1], gain_full[1:2]
     heads = jnp.pad(head_params, ((0, 5), (0, LANES - head_cols)))
-    q_at = (2 * inner_cols + bc_cols) // q_cols
-    kv_at = (2 * inner_cols + bc_cols + q_cols) // LANES
+    mixer_params = (conv_x, conv_bc, heads, heads[:, :HEAD_ROWS].T)
 
     seq_in = tokens_all.astype(f32)
     inverse_one = inverse_rms(seq_in)
     n1 = (seq_in * inverse_one * gain_one).astype(bf16)
-    proj = mm(n1, w_in)
+    proj = mm(n1, w_in[:, :in_cols])
     gated, y, held = mixer_forward(proj, conv_x, conv_bc, heads, inner_cols, bc_cols)
-    attended = attention_forward(proj, tables, q_cols, q_at, kv_at)
-    branch_part = mm(gated, mix_full[:, :mo_cols], NT) + mm(attended, mix_full[:, mo_cols:], NT)
-    branch_low = branch_part.astype(bf16)
-    branch = branch_low.astype(f32) + swap_tensor(branch_low).astype(f32)
-    hidden_one = seq_in + branch
-    inverse_two = inverse_rms(hidden_one)
-    n2 = (hidden_one * inverse_two * gain_two).astype(bf16)
-    gate_up = mm(n2, gu_full)
-    gate, up = gate_up[:, :hidden], gate_up[:, hidden:]
-    sig = sigmoid(gate)
-    activated = (gate * sig * up).astype(bf16)
-    ffn_low = mm(activated, down_full, NT).astype(bf16)
-    layer_out = (half_rows(hidden_one, side) + sum_own_half(ffn_low, side)).astype(bf16)
-
-    act_grad = mm(cotangent_all, down_full)
-    gate_up_grad = jnp.concatenate(
-        [act_grad * up * (sig * (1.0 + gate * (1.0 - sig))), act_grad * (gate * sig)], axis=1
-    ).astype(bf16)
-    n2_grad_low = mm(gate_up_grad, gu_full, NT).astype(bf16)
-    ffn_grads = jnp.concatenate(
+    attended = attention_forward(proj, tables, q_cols)
+
+    rows = tokens_all.shape[0] // ROW_PARTS
+    backward_parts = list(range(ROW_PARTS))[::-1]
+    branch_low, branch_arrived = {}, {}
+    for part in backward_parts:
+        at = slice(part * rows, (part + 1) * rows)
+        branch_low[part] = (
+            mm(gated[at], mix_full[:, :mo_cols], NT) + mm(attended[at], mix_full[:, mo_cols:], NT)
+        ).astype(bf16)
+        branch_arrived[part] = swap_tensor(branch_low[part])
+    n1_ordered = product([(order, n1, 0)])
+    cotangent_turned = product([(unchanged, cotangent_all, 0)])
+    start = backward_parts[0]
+    ready = (n1_ordered, cotangent_turned, mix_full)
+
+    n2_grad_low, n2_grad_arrived = {}, {}
+    buffers = ()
+    for part in backward_parts:
+        *buffers, grad_low = feed_forward(
+            tokens_all,
+            branch_low[part],
+            branch_arrived[part],
+            gain_two,
+            cotangent_all,
+            w_out,
+            buffers,
+            part,
+            *ready,
+        )
+        ready = ()
+        n2_grad_low[part] = grad_low
+        n2_grad_arrived[part] = swap_tensor(grad_low)
+    hidden_one, n2, activated, gate_grad, up_grad = buffers
+    n2_turned = product([(unchanged, n2, 0)])
+    ffn_pieces = [
+        whole(n2_turned, gate_grad),
+        whole(n2_turned, up_grad),
+        whole(cotangent_turned, activated),
+    ]
+    ffn_all = weight_grads(ffn_pieces, None, late=(n2_grad_arrived[start],))
+    ffn_sum = lax.psum_scatter(ffn_all, "dp", scatter_dimension=0, tiled=True)
+
+    mix_grad = {}
+    buffers, proj_grad = (), None
+    carry = jnp.zeros((bc_cols // 2 + 32 + 2 * HEAD_ROWS, inner_cols), f32)
+    step = ffn_all
+    last = backward_parts[-1]
+    for part in backward_parts:
+        *buffers, mix_grad[part] = branch_grad(
+            hidden_one,
+            n2_grad_low[part],
+            n2_grad_arrived[part],
+            gain_two,
+            cotangent_all,
+            mix_full,
+            buffers,
+            part,
+            step,
+        )
+        deps = ()
+        if part == last:
+            ffn_low = product([(activated, w_out, 2)], buffers[1])
+            ffn_there = swap_tensor(half_rows(ffn_low, 1 - side))
+            branch_ordered = product([(order, buffers[1], 0)], ffn_low)
+            mix_pieces = [whole(branch_ordered, gated), whole(branch_ordered, attended)]
+            mix_sent = weight_grads(mix_pieces, 0)
+            mix_arrived = swap_dp(mix_sent, 1)
+            out_grads = [mix_grad[each] for each in range(ROW_PARTS)]
+            att_grad = attention_backward(proj, tables, out_grads, q_cols, mix_sent)
+            att_pieces = [whole(n1_ordered, att_grad)]
+            att_sent = weight_grads(att_pieces, 0)
+            att_arrived = swap_dp(att_sent, 1)
+            mix_near = sum_near(weight_grads(mix_pieces, 1, mix_arrived, (att_sent,)))
+            att_near = sum_near(weight_grads(att_pieces, 1, att_arrived, (mix_near[0],)))
+            deps = (att_near[0], ffn_there)
+        proj_grad, carry = mixer_backward(
+            proj,
+            y,
+            mix_grad[part],
+            held,
+            carry,
+            proj_grad,
+            part,
+            mixer_params,
+            inner_cols,
+            bc_cols,
+            *deps,
+        )
+        step = carry
+
+    sums = carry[bc_cols // 2 + 8 :]
+    sums_arrived = swap_dp(sums, 1)
+    mix_step = sum_far(*mix_near, carry)
+    mix_far = send_far(mix_step)
+    att_step = sum_far(*att_near, mix_step[0])
+    att_far = send_far(att_step)
+    wide_cols = inner_cols + inner_cols // 2
+    second_cols = q_start - wide_cols
+    first_pieces = [(n1_ordered, proj_grad, 0, wide_cols)]
+    second_pieces = [(n1_ordered, proj_grad, wide_cols, second_cols)]
+    first_sent = weight_grads(first_pieces, 0, deps=(att_step[0],))
+    first_arrived = swap_dp(first_sent, 1)
+    second_sent = weight_grads(second_pieces, 0, deps=(first_sent,))
+    second_arrived = swap_dp(second_sent, 1)
+    sums = added(sums, sums_arrived, second_sent)
+    sums_arrived = swap_dp(sums, 2)
+    first_near = sum_near(weight_grads(first_pieces, 1, first_arrived, (sums,)))
+    second_near = sum_near(weight_grads(second_pieces, 1, second_arrived, (first_near[0],)))
+    sums = added(sums, sums_arrived, second_near[0])
+    sums_arrived = swap_dp(sums, 4)
+    n1_there, n1_own = product_halves(
+        side.reshape(1),
+        [(proj_grad, w_in, 0), (att_grad, w_in, q_start // (in_cols - q_start))],
+        sums,
+        *mix_far,
+        *att_far,
+    )
+    n1_arrived = swap_tensor(n1_there)
+    sums = added(sums, sums_arrived, n1_own)
+    bit = 8
+    while bit < dp_count // 2:
+        sums = added(sums, swap_dp(sums, bit))
+        bit *= 2
+    sums_arrived = swap_dp(sums, bit)
+    first_step = sum_far(*first_near, sums)
+    first_far = send_far(first_step)
+    layer_out = own_rows(
+        layer_out_kernel, side.reshape(1), [hidden_one, ffn_low], [ffn_there], [], [first_step[0]]
+    )
+    sums = added(sums, sums_arrived, layer_out)
+    second_step = sum_far(*second_near, sums, *first_far)
+    second_far = send_far(second_step)
+    input_grad = own_rows(
+        input_grad_kernel,
+        side.reshape(1),
+        [buffers[0]],
+        [n1_own, n1_arrived, tokens],
+        [gain_one],
+        [second_step[0]],
+    )
+    ffn_sum = after(ffn_sum, input_grad, *second_far).astype(f32)
+    mix_sum = sum_last(mix_step, mix_far, input_grad, *second_far)
+    att_sum = sum_last(att_step, att_far, input_grad, *second_far)
+    first_sum = sum_last(first_step, first_far, input_grad, *second_far)
+    second_sum = sum_last(second_step, second_far, input_grad)
+
+    taps = conv_x.shape[0]
+    grad_conv_x = sums[:taps]
+    conv_bc_half = sums[16 : 16 + taps, :bc_cols]
+    head_sums = jnp.sum(sums[24:, :CHUNK], axis=1)
+    grad_head = jnp.stack(
         [
-            mm(n2, gate_up_grad, TN).astype(bf16),
-            mm(cotangent_all, activated, TN).astype(bf16),
+            head_sums[:head_cols],
+            head_sums[HEAD_ROWS : HEAD_ROWS + head_cols],
+            jnp.sum(sums[taps].reshape(head_cols, P_SIZE), axis=1),
+        ]
+    )
+
+    in_low = in_pack.astype(f32)
+    gain_one_grad = (
+        jnp.sum(in_low[:, :wide_cols] * first_sum, axis=1)
+        + jnp.sum(in_low[:, wide_cols:q_start] * second_sum[:, :second_cols], axis=1)
+        + jnp.sum(in_low[:, q_start:in_cols] * att_sum, axis=1)
+    ) / shared[:, bc_cols].astype(f32)
+    gain_two_grad = jnp.sum(
+        out_pack[:, : 2 * hidden].astype(f32) * ffn_sum[:, : 2 * hidden], axis=1
+    ) / shared[:, bc_cols + 1].astype(f32)
+    shared_half = jnp.concatenate(
+        [
+            second_sum[:, bc_start - wide_cols : dt_start - wide_cols],
+            jnp.stack([gain_one_grad, gain_two_grad], axis=1),
         ],
         axis=1,
-    )
-    ffn_grads = lax.psum_scatter(ffn_grads, "dp", scatter_dimension=0, tiled=True)
-    n2_grad = n2_grad_low.astype(f32) + swap_tensor(n2_grad_low).astype(f32)
-    gain_two_grad = jnp.sum(n2_grad_low.astype(f32) * (hidden_one * inverse_two), axis=0)
-    hidden_grad = cotangent_all.astype(f32) + normalize_back(
-        n2_grad, hidden_one, inverse_two, gain_two
-    )
-    branch_grad = hidden_grad.astype(bf16)
-    mix_grad = mm(branch_grad, mix_full).astype(bf16)
-    mo_grad = mm(branch_grad, gated, TN).astype(bf16)
-    ao_grad = mm(branch_grad, attended, TN).astype(bf16)
-    att_grad = attention_backward(proj, tables, mix_grad, q_cols, q_at, kv_at)
-    proj_grad, wide_sums, bc_sums, head_sums = mixer_backward(
-        proj, y, mix_grad, held, att_grad, conv_x, conv_bc, heads, inner_cols, bc_cols
-    )
-    n1_grad_low = mm(proj_grad, w_in, NT).astype(bf16)
-    gain_one_grad = jnp.sum(n1_grad_low.astype(f32) * (seq_in * inverse_one), axis=0)
-    in_grads = mm(n1, proj_grad, TN).astype(bf16)
-    n1_grad = sum_own_half(n1_grad_low, side)
-    seq_own = tokens.astype(f32)
-    input_grad = (
-        half_rows(hidden_grad, side)
-        + normalize_back(n1_grad, seq_own, inverse_rms(seq_own), gain_one)
-    ).astype(bf16)
-
-    taps = conv_x.shape[0]
-    head_grads = jnp.stack(
-        [
-            jnp.sum(head_sums[:head_cols], axis=1),
-            jnp.sum(head_sums[HEAD_ROWS : HEAD_ROWS + head_cols], axis=1),
-            jnp.sum(wide_sums[taps].reshape(head_cols, P_SIZE), axis=1),
-        ]
-    )
-    pieces = [wide_sums[:taps], bc_sums[:taps], head_grads]
-    flat = jnp.concatenate([piece.reshape(-1) for piece in pieces])
-    flat_cols = -(-flat.shape[0] // here)
-    flat_cols = -(-(flat_cols + 2) // LANES) * LANES - 2
-    flat = jnp.pad(flat, (0, here * flat_cols - flat.shape[0])).reshape(here, flat_cols)
-    gain_cols = jnp.stack([gain_one_grad, gain_two_grad], axis=1)
-    small = jnp.concatenate([gain_cols, jnp.tile(flat, (dp_count, 1))], axis=1).astype(bf16)
-    summed = scatter_sum(
-        jnp.concatenate([in_grads, mo_grad, ao_grad, small], axis=1), dp_count
-    )
-
-    in_cols = in_grads.shape[1]
-    bc_start = 2 * inner_cols
-    q_start = bc_start + bc_cols
-    kv_start = q_start + q_cols
-    mo_start = in_cols
-    ao_start = mo_start + mo_cols
-    gain_start = ao_start + ao_cols
-    flat_sum = summed[:, gain_start + 2 :].reshape(-1)
-    x_size, bc_size = taps * inner_cols, taps * bc_cols
-    grad_conv_x = flat_sum[:x_size].reshape(taps, inner_cols)
-    conv_bc_half = flat_sum[x_size : x_size + bc_size].reshape(taps, bc_cols)
-    grad_head = flat_sum[x_size + bc_size : x_size + bc_size + 3 * head_cols].reshape(3, head_cols)
-    shared_half = jnp.concatenate(
-        [summed[:, bc_start:q_start], summed[:, gain_start : gain_start + 2]], axis=1
     )
     to_send = jnp.concatenate(
         [half_rows(shared_half, 1 - side).reshape(-1), conv_bc_half.reshape(-1)]
@@ -798,21 +1278,22 @@
         here // 2, bc_cols + 2
     )
     grad_conv_bc = conv_bc_half + arrived[shared_half.size // 2 :].reshape(taps, bc_cols)
-    ffn_sum = ffn_grads.astype(f32)
     return (
         layer_out,
         input_grad,
         shared_sum[:, bc_cols:].T,
-        summed[:, :bc_start].reshape(here, 2, inner_cols),
+        jnp.concatenate([first_sum, second_sum[:, : bc_start - wide_cols]], axis=1).reshape(
+            here, 2, inner_cols
+        ),
         shared_sum[:, :bc_cols],
-        summed[:, dt_start : dt_start + head_cols],
+        second_sum[:, dt_start - wide_cols : dt_start - wide_cols + head_cols],
         grad_conv_x,
         grad_conv_bc,
         grad_head,
-        summed[:, mo_start:ao_start].T,
-        summed[:, q_start:kv_start],
-        summed[:, kv_start : kv_start + kv_cols].reshape(here, 2, kv_cols // 2),
-        summed[:, ao_start:gain_start].T,
+        mix_sum[:, :mo_cols].T,
+        att_sum[:, :q_cols],
+        att_sum[:, q_cols:].reshape(here, 2, kv_cols // 2),
+        mix_sum[:, mo_cols:].T,
         ffn_sum[:, : 2 * hidden].reshape(here, 2, hidden),
         ffn_sum[:, 2 * hidden :].T,
     )

time: 557 us -> 433 us (0.78); the launches traced: 547 us -> 429 us
  waiting for transfers between devices: 280 us -> 99.5 us
  Pallas kernels: 66.2 us -> 166 us
  matrix products: 78.5 us -> 9.93 us
  local copies, waits for them, and re-layouts: 47.6 us -> 78.1 us
  starting transfers between devices: 15.7 us -> 41.3 us
  other arithmetic: 44.5 us -> 19.4 us
    pallas_call x2 -> x42, Pallas kernels: 45.2 us -> 144 us  [the longest x13 31.2 us: weight_grad(): pl.pallas_call(functools.partial(weight_grad_kernel, has_arrived=arrived...]
    ppermute x8 -> x10, waiting for transfers between devices: 157 us -> 63.9 us  [swap_tensor(): return lax.ppermute(values, 'tensor', [(0, 1), (1, 0)])]
    dot_general x14 -> x5, matrix products: 78.5 us -> 9.93 us  [mm(): return lax.dot_general(left, right, dims, preferred_element_type=f32)]
    reduce_scatter x1, waiting for transfers between devices: 53.9 us -> 0.01 us  [local(): ffn_sum = lax.psum_scatter(ffn_all, 'dp', scatter_dimension=0, tiled=True)]
    all_gather x1, waiting for transfers between devices: 43.4 us -> 0.01 us  [local(): w_out = lax.all_gather(out_pack, 'dp', axis=0, tiled=True)]
    unnamed x81 -> x249, local copies, waits for them, and re-layouts: 16.2 us -> 59.5 us
    ppermute x1 -> x24, starting transfers between devices: 0.01 us -> 27.2 us  [the longest x12 17.7 us: send_far(): arrived.append(lax.ppermute(blocks[offset], 'dp', moves))]
    ppermute x1 -> x24, waiting for transfers between devices: 0.01 us -> 19 us  [the longest x12 12.6 us: send_far(): arrived.append(lax.ppermute(blocks[offset], 'dp', moves))]
  transfers between devices with their start and end apart: 13 -> 37, of which waited for: 9 -> 13; matrix products, arithmetic and copies ran while one was open for 15% -> 10% of each run, Pallas kernels for 4% -> 37%
where the time goes in v2:
time: 433 us; the launch traced here: 429 us
  Pallas kernels  166 us (38%)
  waiting for transfers between devices  99.5 us (23%)
  local copies, waits for them, and re-layouts  78.1 us (18%)
  starting transfers between devices  41.3 us (10%)
  other arithmetic  19.4 us (4%)
  between operations  15.4 us (4%)
  matrix products  9.93 us (2%)
    ppermute x10, waiting for transfers between devices, swap_tensor(): return lax.ppermute(values, 'tensor', [(0, 1), (1, 0)])  63.9 us
    unnamed x249, local copies, waits for them, and re-layouts  59.5 us
    pallas_call x13, Pallas kernels, weight_grad(): pl.pallas_call(functools.partial(weight_grad_kernel, has_arrived=arrived...  31.2 us
    pallas_call x2, Pallas kernels, mixer_backward(): pl.pallas_call(functools.partial(mixer_backward_kernel, is_start_part=par...  31 us
    pallas_call x2, Pallas kernels, feed_forward(): pl.pallas_call(feed_forward_kernel, grid=(blocks,), in_specs=[here, only,...  23.6 us
    ppermute x12, starting transfers between devices, send_far(): arrived.append(lax.ppermute(blocks[offset], 'dp', moves))  17.7 us
    all_gather x1, waiting for transfers between devices, local(): w_in = lax.all_gather(in_pack, 'dp', axis=0, tiled=True)  16.5 us
    pallas_call x5, Pallas kernels, product(): pl.pallas_call(functools.partial(product_kernel, count=len(pairs)), grid=...  16.3 us
  transfers between devices with their start and end apart: 37, of which 13 were waited for; matrix products, arithmetic and copies ran while one was open for 10% of the time, Pallas kernels for 37%

profile of v2, /device:TPU:0, one launch (start us, length us, event | category | flops | bytes accessed | tf_op | source)
XLA Modules:
  0.0 429.1 jit_solution(9653432907476997214)
XLA Ops:
  21.1 23.2 %collective-permute-done.3 = bf16[512,1024]{1,0:T(8,128)(2,1)S(1)} collective-permute-done((bf16[512,1024]{1,0:T(8,128)(2,1)S(1)}, bf16[512,1024]{1,0:T(8,128)(2,1)S(1)}, u32[]{:S(2)}, u32[]{:S(2)}) %collective-permute-start.3) | collective-permute-done | bytes 1048608 | tf_op jit(solution)/shard_map/ppermute | solution.py:894
  46.6 18.7 %collective-permute-done = bf16[512,1024]{1,0:T(8,128)(2,1)S(1)} collective-permute-done((bf16[512,1024]{1,0:T(8,128)(2,1)S(1)}, bf16[512,1024]{1,0:T(8,128)(2,1)S(1)}, u32[]{:S(2)}, u32[]{:S(2)}) %collective-permute-start) | collective-permute-done | bytes 1048608 | tf_op jit(solution)/shard_map/ppermute | solution.py:894
  67.2 16.5 %all-gather.3.cloned.1.call-done.refs_1_.refs_2_.refs_3_ = bf16[1024,3328]{1,0:T(8,128)(2,1)} async-done(((bf16[64,3328]{1,0:T(8,128)(2,1)}), bf16[1024,3328]{1,0:T(8,128)(2,1)}) %all-gather.3.cloned.1.call-update) | async-done | bytes 6815760 | tf_op jit(solution)/shard_map/all_gather | solution.py:1076
  92.0 5.0 %fusion.z_ref.u_ref.bc_ref.dr_ref.qkv_ref.u_before_ref.bc_before_ref = f32[1024,2304]{1,0:T(8,128)S(1)} fusion(bf16[1024,1024]{1,0:T(8,128)(2,1)S(1)} %fusion.4.refs_1_, bf16[1024,3328]{1,0:T(8,128)(2,1)S(1)} %bitcast.36), kind=kOutput, calls=%fused_computation.2 | convolution fusion | flops 4831838208 | bytes 16252928 | tf_op jit(solution)/shard_map/dot_general | solution.py:34
  97.0 8.6 %attention_forward.1.right_ref = bf16[1024,256]{1,0:T(8,128)(2,1)S(1)} custom-call(f32[1024,2304]{1,0:T(8,128)S(1)} %fusion.z_ref.u_ref.bc_ref.dr_ref.qkv_ref.u_before_ref.bc_before_ref, f32[1024,128]{1,0:T(8,128)S(1)} %get-tuple-element.188.cos_ref, f32[1024,128]{1,0:T(8,128)S(1)} %get-tuple-element.189.sin_ref), custom_call_target="tpu_custom_call" | custom-call | flops 1000 | bytes 1000 | tf_op jit(solution)/shard_map/attention_forward/pallas_call | solution.py:542
  105.7 12.6 %mixer_forward.1 = (bf16[1024,768]{1,0:T(8,128)(2,1)S(1)}, bf16[1024,768]{1,0:T(8,128)(2,1)S(1)}, bf16[1024,768]{1,0:T(8,128)(2,1)S(1)}) custom-call(f32[1024,2304]{1,0:T(8,128)S(1)} %fusion.z_ref.u_ref.bc_ref.dr_ref.qkv_ref.u_before_ref.bc_before_ref, f32[1024,2304]{1,0:T(8,128)S(1)} %fusion.z_ref.u_ref.bc_ref.dr_ref.qkv_ref.u_before_ref.bc_before_ref, ...), custom_call_target="tpu_custom_call" | custom-call | flops 1000 | bytes 1000 | tf_op jit(solution)/shard_map/mixer_forward/pallas_call | solution.py:450
  138.9 8.8 %collective-permute-done.4.arrived_ref = bf16[512,1024]{1,0:T(8,128)(2,1)} collective-permute-done((bf16[512,1024]{1,0:T(8,128)(2,1)}, bf16[512,1024]{1,0:T(8,128)(2,1)}, u32[]{:S(2)}, u32[]{:S(2)}) %collective-permute-start.4) | collective-permute-done | bytes 1048608 | tf_op jit(solution)/shard_map/ppermute | solution.py:894
  147.7 11.6 %feed_forward.2 = (f32[1024,1024]{1,0:T(8,128)}, bf16[1024,1024]{1,0:T(8,128)(2,1)S(1)}, bf16[1024,1024]{1,0:T(8,128)(2,1)S(1)}, bf16[1024,1024]{1,0:T(8,128)(2,...) custom-call(bf16[1024,1024]{1,0:T(8,128)(2,1)S(1)} %copy-done.12, ...), custom_call_target="tpu_custom_call" | custom-call | flops 1000 | bytes 1000 | tf_op jit(solution)/shard_map/feed_forward/pallas_call | solution.py:629
  160.8 9.3 %collective-permute-done.2.arrived_ref = bf16[512,1024]{1,0:T(8,128)(2,1)} collective-permute-done((bf16[512,1024]{1,0:T(8,128)(2,1)}, bf16[512,1024]{1,0:T(8,128)(2,1)}, u32[]{:S(2)}, u32[]{:S(2)}) %collective-permute-start.2) | collective-permute-done | bytes 1048608 | tf_op jit(solution)/shard_map/ppermute | solution.py:894
  170.1 12.0 %feed_forward.3 = (f32[1024,1024]{1,0:T(8,128)}, bf16[1024,1024]{1,0:T(8,128)(2,1)S(1)}, bf16[1024,1024]{1,0:T(8,128)(2,1)S(1)}, bf16[1024,1024]{1,0:T(8,128)(2,...) custom-call(bf16[1024,1024]{1,0:T(8,128)(2,1)S(1)} %copy-done.12, ...), custom_call_target="tpu_custom_call", output_to_operand_aliasing={{0}: (8, {}), {1}: (9, {}), {2}: (10, {}), {3}: (11, {}), {... | custom-call | flops 1000 | bytes 1000 | tf_op jit(solution)/shard_map/feed_forward/pallas_call | solution.py:629
  185.4 3.4 weight_grad.13.rest_0_
  191.8 3.4 weight_grad.14.rest_0_
  195.3 3.4 weight_grad.15.rest_0_
  220.0 15.5 %mixer_backward.2 = (bf16[1024,1920]{1,0:T(8,128)(2,1)}, f32[192,768]{1,0:T(8,128)S(1)}) custom-call(f32[1024,2304]{1,0:T(8,128)} %copy-done, f32[1024,2304]{1,0:T(8,128)} %copy-done, f32[1024,2304]{1,0:T(8,128)} %copy-done, f32[1024,2304]{1,0:T(8,128)} %copy-done, f32[1024,2304]{1,0:T(8,128)} %copy-done, f32[1024,2304]{1,0:T(8,128)} %copy-done, ...), custom_call_target="tpu_custom_call" | custom-call | flops 1000 | bytes 1000 | tf_op jit(solution)/shard_map/mixer_backward/pallas_call | solution.py:500
  244.6 3.4 branch_grad.3
  268.9 15.9 %attention_backward.1.right_ref.refs_1_ = bf16[1024,384]{1,0:T(8,128)(2,1)S(1)} custom-call(f32[1024,2304]{1,0:T(8,128)} %copy-done, f32[1024,128]{1,0:T(8,128)S(1)} %copy-done.44, f32[1024,128]{1,0:T(8,128)S(1)} %copy-done.46, bf16[512,1024]{1,0:T(8,128)(2,1)S(1)} %copy-done.50, bf16[512,1024]{1,0:T(8,128)(2,1)S(1)} %copy-done.54, ...), custom_call_target="tpu_custom_call" | custom-call | flops 1000 | bytes 1000 | tf_op jit(solution)/shard_map/attention_backward/pallas_call | solution.py:561
  300.0 15.5 %mixer_backward.3 = (bf16[1024,1920]{1,0:T(8,128)(2,1)}, f32[192,768]{1,0:T(8,128)S(1)}) custom-call(f32[1024,2304]{1,0:T(8,128)} %copy-done, f32[1024,2304]{1,0:T(8,128)} %copy-done, f32[1024,2304]{1,0:T(8,128)} %copy-done, f32[1024,2304]{1,0:T(8,128)} %copy-done, f32[1024,2304]{1,0:T(8,128)} %copy-done, ...), custom_call_target="tpu_custom_call", output_to_operand_aliasing={{0}: (14, {})} | custom-call | flops 1000 | bytes 1000 | tf_op jit(solution)/shard_map/mixer_backward/pallas_call | solution.py:500
  329.9 4.0 collective-permute-done.21.refs_8_.refs_5_
  347.8 7.5 %product_halves.1 = (bf16[512,1024]{1,0:T(8,128)(2,1)}, bf16[512,1024]{1,0:T(8,128)(2,1)S(1)}) custom-call(s32[1]{0:T(128)} %bitcast.side_ref, bf16[1024,1920]{1,0:T(8,128)(2,1)S(1)} %copy-done.3, bf16[1024,384]{1,0:T(8,128)(2,1)S(1)} %attention_backward.1.right_ref.refs_1_, bf16[1024,3328]{1,0:T(8,128)(2,1)S(1)} %bitcast.38, ...), custom_call_target="tpu_custom_call" | custom-call | flops 1000 | bytes 1000 | tf_op jit(solution)/shard_map/product_halves/pallas_call | solution.py:798
  358.3 4.4 %collective-permute-done.17.right_ref = f32[56,768]{1,0:T(8,128)S(1)} collective-permute-done((f32[56,768]{1,0:T(8,128)S(1)}, f32[56,768]{1,0:T(8,128)S(1)}, u32[]{:S(2)}, u32[]{:S(2)}) %collective-permute-start.17) | collective-permute-done | bytes 172064 | tf_op jit(solution)/shard_map/ppermute | solution.py:898
  373.4 3.5 own_rows.2.rest_0_
  387.8 3.8 collective-permute-done.28.rest_2_.refs_6_
  392.9 3.6 collective-permute-start.30
  401.7 3.9 own_rows.3.refs_1_
  (429 shorter events, 196.2 us)
Async XLA Ops:
  7.2 76.5 %all-gather.3.cloned.1.call-start = ((), (), s32[]{:S(2)}) async-start(), calls=%async_computation.1 | async-start | bytes 7241728 | tf_op jit(solution)/shard_map/all_gather | solution.py:1076
  18.1 129.6 %all-gather.5.cloned.1.call-start = ((), (), s32[]{:S(2)}) async-start(), calls=%async_computation.2 | async-start | bytes 6684672 | tf_op jit(solution)/shard_map/all_gather | solution.py:1081
  18.2 26.1 %collective-permute-start.3 = (bf16[512,1024]{1,0:T(8,128)(2,1)S(1)}, bf16[512,1024]{1,0:T(8,128)(2,1)S(1)}, u32[]{:S(2)}, u32[]{:S(2)}) collective-permute-start(bf16[512,1024]{1,0:T(8,128)(2,1)S(1)} %copy-done.109), channel_id=1, source_target_pairs={{0,1},{1,0},{2,3},{3,2},{4,5},{5,4},{6,7},{7,6},{8,9},{9,8},{10,11... | collective-permute-start | bytes 3145736 | tf_op jit(solution)/shard_map/ppermute | solution.py:894
  19.0 46.3 %collective-permute-start = (bf16[512,1024]{1,0:T(8,128)(2,1)S(1)}, bf16[512,1024]{1,0:T(8,128)(2,1)S(1)}, u32[]{:S(2)}, u32[]{:S(2)}) collective-permute-start(bf16[512,1024]{1,0:T(8,128)(2,1)S(1)} %copy-done.58), channel_id=1, source_target_pairs={{0,1},{1,0},{2,3},{3,2},{4,5},{5,4},{6,7},{7,6},{8,9},{9,8},{10,11... | collective-permute-start | bytes 3145736 | tf_op jit(solution)/shard_map/ppermute | solution.py:894
  83.8 330.7 %reduce-scatter.2.cloned.1.call-start = ((), (), s32[]{:S(2)}) async-start(), calls=%async_computation.3 | async-start | bytes 6684672 | tf_op jit(solution)/shard_map/reduce_scatter | solution.py:1139
  121.4 26.3 %collective-permute-start.4 = (bf16[512,1024]{1,0:T(8,128)(2,1)}, bf16[512,1024]{1,0:T(8,128)(2,1)}, u32[]{:S(2)}, u32[]{:S(2)}) collective-permute-start(bf16[512,1024]{1,0:T(8,128)(2,1)} %add_convert_fusion.low_ref), channel_id=1, source_target_pairs={{0,1},{1,0},{2,3},{3,2},{4,5},{5,4},{6,7},{7,6},{8,9},{9,8},{10,11... | collective-permute-start | bytes 3145736 | tf_op jit(solution)/shard_map/ppermute | solution.py:894
  125.3 44.8 %collective-permute-start.2 = (bf16[512,1024]{1,0:T(8,128)(2,1)}, bf16[512,1024]{1,0:T(8,128)(2,1)}, u32[]{:S(2)}, u32[]{:S(2)}) collective-permute-start(bf16[512,1024]{1,0:T(8,128)(2,1)} %add_convert_fusion.1.low_ref), channel_id=1, source_target_pairs={{0,1},{1,0},{2,3},{3,2},{4,5},{5,4},{6,7},{7,6},{8,9},{9,8},{10,11... | collective-permute-start | bytes 3145736 | tf_op jit(solution)/shard_map/ppermute | solution.py:894
  159.3 32.5 %collective-permute-start.6 = (bf16[512,1024]{1,0:T(8,128)(2,1)S(1)}, bf16[512,1024]{1,0:T(8,128)(2,1)S(1)}, u32[]{:S(2)}, u32[]{:S(2)}) collective-permute-start(bf16[512,1024]{1,0:T(8,128)(2,1)S(1)} %get-tuple-element.77.low_ref), channel_id=1, source_target_pairs={{0,1},{1,0},{2,3},{3,2},{4,5},{5,4},{6,7},{7,6},{8,9},{9,8},{10,11... | collective-permute-start | bytes 3145736 | tf_op jit(solution)/shard_map/ppermute | solution.py:894
  201.3 34.3 %collective-permute-start.5 = (bf16[512,1024]{1,0:T(8,128)(2,1)}, bf16[512,1024]{1,0:T(8,128)(2,1)}, u32[]{:S(2)}, u32[]{:S(2)}) collective-permute-start(bf16[512,1024]{1,0:T(8,128)(2,1)} %copy-done.82), channel_id=1, source_target_pairs={{0,1},{1,0},{2,3},{3,2},{4,5},{5,4},{6,7},{7,6},{8,9},{9,8},{10,11... | collective-permute-start | bytes 3145736 | tf_op jit(solution)/shard_map/ppermute | solution.py:894
  264.0 21.8 %collective-permute-start.9 = (bf16[512,1024]{1,0:T(8,128)(2,1)}, bf16[512,1024]{1,0:T(8,128)(2,1)}, u32[]{:S(2)}, u32[]{:S(2)}) collective-permute-start(bf16[512,1024]{1,0:T(8,128)(2,1)} %weight_grad.17.rest_2_), channel_id=1, source_target_pairs={{0,2},{2,0},{4,6},{6,4},{8,10},{10,8},{12,14},{14,12},{16,18},{18,... | collective-permute-start | bytes 3145736 | tf_op jit(solution)/shard_map/ppermute | solution.py:898
  265.1 31.4 %collective-permute-start.7 = (bf16[512,1024]{1,0:T(8,128)(2,1)}, bf16[512,1024]{1,0:T(8,128)(2,1)}, u32[]{:S(2)}, u32[]{:S(2)}) collective-permute-start(bf16[512,1024]{1,0:T(8,128)(2,1)} %constant_dynamic-slice_fusion.1), channel_id=1, source_target_pairs={{0,1},{1,0},{2,3},{3,2},{4,5},{5,4},{6,7},{7,6},{8,9},{9,8},{10,11... | collective-permute-start | bytes 3145736 | tf_op jit(solution)/shard_map/ppermute | solution.py:894
  291.7 23.9 %collective-permute-start.11 = (bf16[256,1024]{1,0:T(8,128)(2,1)}, bf16[256,1024]{1,0:T(8,128)(2,1)}, u32[]{:S(2)}, u32[]{:S(2)}) collective-permute-start(bf16[256,1024]{1,0:T(8,128)(2,1)} %get-tuple-element.96), channel_id=1, source_target_pairs={{0,4},{2,6},{4,0},{6,2},{8,12},{10,14},{12,8},{14,10},{16,20},{18,... | collective-permute-start | bytes 1572872 | tf_op jit(solution)/shard_map/ppermute | solution.py:898
  295.0 21.9 %collective-permute-start.10 = (bf16[256,384]{1,0:T(8,128)(2,1)}, bf16[256,384]{1,0:T(8,128)(2,1)}, u32[]{:S(2)}, u32[]{:S(2)}) collective-permute-start(bf16[256,384]{1,0:T(8,128)(2,1)} %get-tuple-element.95), channel_id=1, source_target_pairs={{0,4},{2,6},{4,0},{6,2},{8,12},{10,14},{12,8},{14,10},{16,20},{18,... | collective-permute-start | bytes 589832 | tf_op jit(solution)/shard_map/ppermute | solution.py:898
  322.6 12.8 %collective-permute-start.12 = (bf16[512,1152]{1,0:T(8,128)(2,1)S(1)}, bf16[512,1152]{1,0:T(8,128)(2,1)S(1)}, u32[]{:S(2)}, u32[]{:S(2)}) collective-permute-start(bf16[512,1152]{1,0:T(8,128)(2,1)S(1)} %weight_grad.22.rest_0_), channel_id=1, source_target_pairs={{0,2},{2,0},{4,6},{6,4},{8,10},{10,8},{12,14},{14,12},{16,18},{18,... | collective-permute-start | bytes 3538952 | tf_op jit(solution)/shard_map/ppermute | solution.py:898
  324.4 18.2 %collective-permute-start.16 = (bf16[512,768]{1,0:T(8,128)(2,1)S(1)}, bf16[512,768]{1,0:T(8,128)(2,1)S(1)}, u32[]{:S(2)}, u32[]{:S(2)}) collective-permute-start(bf16[512,768]{1,0:T(8,128)(2,1)S(1)} %weight_grad.23.rest_0_), channel_id=1, source_target_pairs={{0,2},{2,0},{4,6},{6,4},{8,10},{10,8},{12,14},{14,12},{16,18},{18,... | collective-permute-start | bytes 2359304 | tf_op jit(solution)/shard_map/ppermute | solution.py:898
  327.1 13.9 %collective-permute-start.15 = (f32[56,768]{1,0:T(8,128)S(1)}, f32[56,768]{1,0:T(8,128)S(1)}, u32[]{:S(2)}, u32[]{:S(2)}) collective-permute-start(f32[56,768]{1,0:T(8,128)S(1)} %added.4.rest_1_.left_ref), channel_id=1, source_target_pairs={{0,4},{2,6},{4,0},{6,2},{8,12},{10,14},{12,8},{14,10},{16,20},{18,... | collective-permute-start | bytes 516104 | tf_op jit(solution)/shard_map/ppermute | solution.py:898
  334.0 13.1 %collective-permute-start.18 = (bf16[64,1024]{1,0:T(8,128)(2,1)S(1)}, bf16[64,1024]{1,0:T(8,128)(2,1)S(1)}, u32[]{:S(2)}, u32[]{:S(2)}) collective-permute-start(bf16[64,1024]{1,0:T(8,128)(2,1)S(1)} %get-tuple-element.103), channel_id=1, source_target_pairs={{0,8},{2,10},{4,12},{6,14},{8,16},{10,18},{12,20},{14,22},{16,24},... | collective-permute-start | bytes 393224 | tf_op jit(solution)/shard_map/ppermute | solution.py:999
  335.4 11.6 %collective-permute-start.19 = (bf16[64,1024]{1,0:T(8,128)(2,1)S(1)}, bf16[64,1024]{1,0:T(8,128)(2,1)S(1)}, u32[]{:S(2)}, u32[]{:S(2)}) collective-permute-start(bf16[64,1024]{1,0:T(8,128)(2,1)S(1)} %get-tuple-element.104), channel_id=1, source_target_pairs={{0,16},{2,18},{4,20},{6,22},{8,24},{10,26},{12,28},{14,30},{16,0},... | collective-permute-start | bytes 393224 | tf_op jit(solution)/shard_map/ppermute | solution.py:999
  335.5 11.6 %collective-permute-start.20 = (bf16[64,1024]{1,0:T(8,128)(2,1)S(1)}, bf16[64,1024]{1,0:T(8,128)(2,1)S(1)}, u32[]{:S(2)}, u32[]{:S(2)}) collective-permute-start(bf16[64,1024]{1,0:T(8,128)(2,1)S(1)} %get-tuple-element.105), channel_id=1, source_target_pairs={{0,24},{2,26},{4,28},{6,30},{8,0},{10,2},{12,4},{14,6},{16,8},{18,... | collective-permute-start | bytes 393224 | tf_op jit(solution)/shard_map/ppermute | solution.py:999
  341.1 28.0 %collective-permute-start.14 = (bf16[256,1152]{1,0:T(8,128)(2,1)}, bf16[256,1152]{1,0:T(8,128)(2,1)}, u32[]{:S(2)}, u32[]{:S(2)}) collective-permute-start(bf16[256,1152]{1,0:T(8,128)(2,1)} %get-tuple-element.101), channel_id=1, source_target_pairs={{0,4},{2,6},{4,0},{6,2},{8,12},{10,14},{12,8},{14,10},{16,20},{18,... | collective-permute-start | bytes 1769480 | tf_op jit(solution)/shard_map/ppermute | solution.py:898
  355.3 44.2 %collective-permute-start.24 = (bf16[512,1024]{1,0:T(8,128)(2,1)}, bf16[512,1024]{1,0:T(8,128)(2,1)}, u32[]{:S(2)}, u32[]{:S(2)}) collective-permute-start(bf16[512,1024]{1,0:T(8,128)(2,1)} %get-tuple-element.112), channel_id=1, source_target_pairs={{0,1},{1,0},{2,3},{3,2},{4,5},{5,4},{6,7},{7,6},{8,9},{9,8},{10,11... | collective-permute-start | bytes 3145736 | tf_op jit(solution)/shard_map/ppermute | solution.py:894
  363.7 13.3 %collective-permute-start.26 = (f32[56,768]{1,0:T(8,128)S(1)}, f32[56,768]{1,0:T(8,128)S(1)}, u32[]{:S(2)}, u32[]{:S(2)}) collective-permute-start(f32[56,768]{1,0:T(8,128)S(1)} %added.6.rest_0_.left_ref), channel_id=1, source_target_pairs={{0,16},{2,18},{4,20},{6,22},{8,24},{10,26},{12,28},{14,30},{16,0},... | collective-permute-start | bytes 516104 | tf_op jit(solution)/shard_map/ppermute | solution.py:898
  367.5 17.0 %collective-permute-start.25 = (bf16[256,768]{1,0:T(8,128)(2,1)}, bf16[256,768]{1,0:T(8,128)(2,1)}, u32[]{:S(2)}, u32[]{:S(2)}) collective-permute-start(bf16[256,768]{1,0:T(8,128)(2,1)} %get-tuple-element.113), channel_id=1, source_target_pairs={{0,4},{2,6},{4,0},{6,2},{8,12},{10,14},{12,8},{14,10},{16,20},{18,... | collective-permute-start | bytes 1179656 | tf_op jit(solution)/shard_map/ppermute | solution.py:898
  392.9 12.7 %collective-permute-start.30 = (bf16[64,768]{1,0:T(8,128)(2,1)S(1)}, bf16[64,768]{1,0:T(8,128)(2,1)S(1)}, u32[]{:S(2)}, u32[]{:S(2)}) collective-permute-start(bf16[64,768]{1,0:T(8,128)(2,1)S(1)} %get-tuple-element.118), channel_id=1, source_target_pairs={{0,8},{2,10},{4,12},{6,14},{8,16},{10,18},{12,20},{14,22},{16,24},... | collective-permute-start | bytes 294920 | tf_op jit(solution)/shard_map/ppermute | solution.py:999
  (134 other events, 848.1 us)
Sparse Core Ops, SparseCore 0:
  18.2 65.4 all-gather.2
  86.0 60.2 all-gather.4
  201.4 83.6 reduce-scatter.1

commit v3 on v2

--- a/solution.py
+++ b/solution.py
@@ -1184,7 +1184,6 @@
             bc_cols,
             *deps,
         )
-        step = carry
 
     sums = carry[bc_cols // 2 + 8 :]
     sums_arrived = swap_dp(sums, 1)
@@ -1204,30 +1203,30 @@
     sums_arrived = swap_dp(sums, 2)
     first_near = sum_near(weight_grads(first_pieces, 1, first_arrived, (sums,)))
     second_near = sum_near(weight_grads(second_pieces, 1, second_arrived, (first_near[0],)))
-    sums = added(sums, sums_arrived, second_near[0])
-    sums_arrived = swap_dp(sums, 4)
     n1_there, n1_own = product_halves(
         side.reshape(1),
         [(proj_grad, w_in, 0), (att_grad, w_in, q_start // (in_cols - q_start))],
-        sums,
+        second_near[0],
         *mix_far,
         *att_far,
     )
     n1_arrived = swap_tensor(n1_there)
     sums = added(sums, sums_arrived, n1_own)
+    sums_arrived = swap_dp(sums, 4)
+    first_step = sum_far(*first_near, n1_own)
+    first_far = send_far(first_step)
+    sums = added(sums, sums_arrived, first_step[0])
     bit = 8
     while bit < dp_count // 2:
         sums = added(sums, swap_dp(sums, bit))
         bit *= 2
     sums_arrived = swap_dp(sums, bit)
-    first_step = sum_far(*first_near, sums)
-    first_far = send_far(first_step)
     layer_out = own_rows(
-        layer_out_kernel, side.reshape(1), [hidden_one, ffn_low], [ffn_there], [], [first_step[0]]
-    )
-    sums = added(sums, sums_arrived, layer_out)
-    second_step = sum_far(*second_near, sums, *first_far)
+        layer_out_kernel, side.reshape(1), [hidden_one, ffn_low], [ffn_there], [], first_far[:1]
+    )
+    second_step = sum_far(*second_near, sums, layer_out, *first_far)
     second_far = send_far(second_step)
+    sums = added(sums, sums_arrived, second_step[0])
     input_grad = own_rows(
         input_grad_kernel,
         side.reshape(1),
@@ -1254,7 +1253,7 @@
         ]
     )
 
-    in_low = in_pack.astype(f32)
+    in_low = after(in_pack, input_grad).astype(f32)
     gain_one_grad = (
         jnp.sum(in_low[:, :wide_cols] * first_sum, axis=1)
         + jnp.sum(in_low[:, wide_cols:q_start] * second_sum[:, :second_cols], axis=1)

time: 433 us -> 423 us (0.977)
  local copies, waits for them, and re-layouts: 78.1 us -> 57.8 us
  waiting for transfers between devices: 99.5 us -> 113 us
    unnamed x249 -> x227, local copies, waits for them, and re-layouts: 59.5 us -> 40.3 us
    ppermute x10, waiting for transfers between devices: 63.9 us -> 77.7 us  [swap_tensor(): return lax.ppermute(values, 'tensor', [(0, 1), (1, 0)])]
  transfers between devices with their start and end apart: 37 -> 37, of which waited for: 13 -> 15; matrix products, arithmetic and copies ran while one was open for 10% -> 10% of each run, Pallas kernels for 37% -> 37%
where the time goes in v3:
time: 423 us; the launch traced here: 419 us
  Pallas kernels  163 us (39%)
  waiting for transfers between devices  113 us (27%)
  local copies, waits for them, and re-layouts  57.8 us (14%)
  starting transfers between devices  42.2 us (10%)
  other arithmetic  17.6 us (4%)
  between operations  15.3 us (4%)
  matrix products  9.94 us (2%)
    ppermute x10, waiting for transfers between devices, swap_tensor(): return lax.ppermute(values, 'tensor', [(0, 1), (1, 0)])  77.7 us
    unnamed x227, local copies, waits for them, and re-layouts  40.3 us
    pallas_call x2, Pallas kernels, mixer_backward(): pl.pallas_call(functools.partial(mixer_backward_kernel, is_start_part=par...  31.2 us
    pallas_call x13, Pallas kernels, weight_grad(): pl.pallas_call(functools.partial(weight_grad_kernel, has_arrived=arrived...  30.5 us
    pallas_call x2, Pallas kernels, feed_forward(): pl.pallas_call(feed_forward_kernel, grid=(blocks,), in_specs=[here, only,...  23.6 us
    ppermute x12, starting transfers between devices, send_far(): arrived.append(lax.ppermute(blocks[offset], 'dp', moves))  17.8 us
    all_gather x1, waiting for transfers between devices, local(): w_in = lax.all_gather(in_pack, 'dp', axis=0, tiled=True)  16.5 us
    pallas_call x5, Pallas kernels, product(): pl.pallas_call(functools.partial(product_kernel, count=len(pairs)), grid=...  16.3 us
  transfers between devices with their start and end apart: 37, of which 15 were waited for; matrix products, arithmetic and copies ran while one was open for 10% of the time, Pallas kernels for 37%

profile of v3, /device:TPU:0, one launch (start us, length us, event | category | flops | bytes accessed | tf_op | source)
XLA Modules:
  0.0 418.6 jit_solution(6091456454494335071)
XLA Ops:
  21.1 23.2 %collective-permute-done.3 = bf16[512,1024]{1,0:T(8,128)(2,1)S(1)} collective-permute-done((bf16[512,1024]{1,0:T(8,128)(2,1)S(1)}, bf16[512,1024]{1,0:T(8,128)(2,1)S(1)}, u32[]{:S(2)}, u32[]{:S(2)}) %collective-permute-start.3) | collective-permute-done | bytes 1048608 | tf_op jit(solution)/shard_map/ppermute | solution.py:894
  46.6 18.7 %collective-permute-done = bf16[512,1024]{1,0:T(8,128)(2,1)S(1)} collective-permute-done((bf16[512,1024]{1,0:T(8,128)(2,1)S(1)}, bf16[512,1024]{1,0:T(8,128)(2,1)S(1)}, u32[]{:S(2)}, u32[]{:S(2)}) %collective-permute-start) | collective-permute-done | bytes 1048608 | tf_op jit(solution)/shard_map/ppermute | solution.py:894
  67.2 16.5 %all-gather.3.cloned.1.call-done.refs_1_.refs_2_.refs_3_ = bf16[1024,3328]{1,0:T(8,128)(2,1)} async-done(((bf16[64,3328]{1,0:T(8,128)(2,1)}), bf16[1024,3328]{1,0:T(8,128)(2,1)}) %all-gather.3.cloned.1.call-update) | async-done | bytes 6815760 | tf_op jit(solution)/shard_map/all_gather | solution.py:1076
  91.9 5.0 %fusion.z_ref.u_ref.bc_ref.dr_ref.qkv_ref.u_before_ref.bc_before_ref = f32[1024,2304]{1,0:T(8,128)S(1)} fusion(bf16[1024,1024]{1,0:T(8,128)(2,1)S(1)} %fusion.4.refs_1_, bf16[1024,3328]{1,0:T(8,128)(2,1)S(1)} %bitcast.36), kind=kOutput, calls=%fused_computation.2 | convolution fusion | flops 4831838208 | bytes 16252928 | tf_op jit(solution)/shard_map/dot_general | solution.py:34
  97.0 8.7 %attention_forward.1.right_ref = bf16[1024,256]{1,0:T(8,128)(2,1)S(1)} custom-call(f32[1024,2304]{1,0:T(8,128)S(1)} %fusion.z_ref.u_ref.bc_ref.dr_ref.qkv_ref.u_before_ref.bc_before_ref, f32[1024,128]{1,0:T(8,128)S(1)} %get-tuple-element.188.cos_ref, f32[1024,128]{1,0:T(8,128)S(1)} %get-tuple-element.189.sin_ref), custom_call_target="tpu_custom_call" | custom-call | flops 1000 | bytes 1000 | tf_op jit(solution)/shard_map/attention_forward/pallas_call | solution.py:542
  105.8 12.6 %mixer_forward.1 = (bf16[1024,768]{1,0:T(8,128)(2,1)S(1)}, bf16[1024,768]{1,0:T(8,128)(2,1)S(1)}, bf16[1024,768]{1,0:T(8,128)(2,1)S(1)}) custom-call(f32[1024,2304]{1,0:T(8,128)S(1)} %fusion.z_ref.u_ref.bc_ref.dr_ref.qkv_ref.u_before_ref.bc_before_ref, f32[1024,2304]{1,0:T(8,128)S(1)} %fusion.z_ref.u_ref.bc_ref.dr_ref.qkv_ref.u_before_ref.bc_before_ref, ...), custom_call_target="tpu_custom_call" | custom-call | flops 1000 | bytes 1000 | tf_op jit(solution)/shard_map/mixer_forward/pallas_call | solution.py:450
  138.9 8.9 %collective-permute-done.4.arrived_ref = bf16[512,1024]{1,0:T(8,128)(2,1)} collective-permute-done((bf16[512,1024]{1,0:T(8,128)(2,1)}, bf16[512,1024]{1,0:T(8,128)(2,1)}, u32[]{:S(2)}, u32[]{:S(2)}) %collective-permute-start.4) | collective-permute-done | bytes 1048608 | tf_op jit(solution)/shard_map/ppermute | solution.py:894
  147.8 11.7 %feed_forward.2 = (f32[1024,1024]{1,0:T(8,128)}, bf16[1024,1024]{1,0:T(8,128)(2,1)S(1)}, bf16[1024,1024]{1,0:T(8,128)(2,1)S(1)}, bf16[1024,1024]{1,0:T(8,128)(2,...) custom-call(bf16[1024,1024]{1,0:T(8,128)(2,1)S(1)} %copy-done.12, ...), custom_call_target="tpu_custom_call" | custom-call | flops 1000 | bytes 1000 | tf_op jit(solution)/shard_map/feed_forward/pallas_call | solution.py:629
  160.9 9.3 %collective-permute-done.2.arrived_ref = bf16[512,1024]{1,0:T(8,128)(2,1)} collective-permute-done((bf16[512,1024]{1,0:T(8,128)(2,1)}, bf16[512,1024]{1,0:T(8,128)(2,1)}, u32[]{:S(2)}, u32[]{:S(2)}) %collective-permute-start.2) | collective-permute-done | bytes 1048608 | tf_op jit(solution)/shard_map/ppermute | solution.py:894
  170.2 12.0 %feed_forward.3 = (f32[1024,1024]{1,0:T(8,128)}, bf16[1024,1024]{1,0:T(8,128)(2,1)S(1)}, bf16[1024,1024]{1,0:T(8,128)(2,1)S(1)}, bf16[1024,1024]{1,0:T(8,128)(2,...) custom-call(bf16[1024,1024]{1,0:T(8,128)(2,1)S(1)} %copy-done.12, ...), custom_call_target="tpu_custom_call", output_to_operand_aliasing={{0}: (8, {}), {1}: (9, {}), {2}: (10, {}), {3}: (11, {}), {... | custom-call | flops 1000 | bytes 1000 | tf_op jit(solution)/shard_map/feed_forward/pallas_call | solution.py:629
  185.4 3.4 weight_grad.13.rest_0_
  191.9 3.4 weight_grad.14.rest_0_
  195.3 3.4 weight_grad.15.rest_0_.rest_2_
  212.4 13.7 %collective-permute-done.5.arrived_ref = bf16[512,1024]{1,0:T(8,128)(2,1)S(1)} collective-permute-done((bf16[512,1024]{1,0:T(8,128)(2,1)}, bf16[512,1024]{1,0:T(8,128)(2,1)S(1)}, u32[]{:S(2)}, u32[]{:S(2)}) %collective-permute-start.5) | collective-permute-done | bytes 1048608 | tf_op jit(solution)/shard_map/ppermute | solution.py:894
  232.4 3.4 product.8.refs_2_.own_ref
  247.5 16.1 %attention_backward.1.right_ref.refs_1_ = bf16[1024,384]{1,0:T(8,128)(2,1)S(1)} custom-call(f32[1024,2304]{1,0:T(8,128)} %copy-done, f32[1024,128]{1,0:T(8,128)S(1)} %copy-done.39, f32[1024,128]{1,0:T(8,128)S(1)} %copy-done.41, bf16[512,1024]{1,0:T(8,128)(2,1)S(1)} %copy-done.45, bf16[512,1024]{1,0:T(8,128)(2,1)S(1)} %copy-done.48, ...), custom_call_target="tpu_custom_call" | custom-call | flops 1000 | bytes 1000 | tf_op jit(solution)/shard_map/attention_backward/pallas_call | solution.py:561
  278.9 15.6 %mixer_backward.2 = (bf16[1024,1920]{1,0:T(8,128)(2,1)}, f32[192,768]{1,0:T(8,128)S(1)}) custom-call(f32[1024,2304]{1,0:T(8,128)} %copy-done, f32[1024,2304]{1,0:T(8,128)} %copy-done, f32[1024,2304]{1,0:T(8,128)} %copy-done, f32[1024,2304]{1,0:T(8,128)} %copy-done, f32[1024,2304]{1,0:T(8,128)} %copy-done, f32[1024,2304]{1,0:T(8,128)} %copy-done, ...), custom_call_target="tpu_custom_call" | custom-call | flops 1000 | bytes 1000 | tf_op jit(solution)/shard_map/mixer_backward/pallas_call | solution.py:500
  294.5 15.6 %mixer_backward.3 = (bf16[1024,1920]{1,0:T(8,128)(2,1)}, f32[192,768]{1,0:T(8,128)S(1)}) custom-call(f32[1024,2304]{1,0:T(8,128)} %copy-done, f32[1024,2304]{1,0:T(8,128)} %copy-done, f32[1024,2304]{1,0:T(8,128)} %copy-done, f32[1024,2304]{1,0:T(8,128)} %copy-done, f32[1024,2304]{1,0:T(8,128)} %copy-done, ...), custom_call_target="tpu_custom_call", output_to_operand_aliasing={{0}: (14, {})} | custom-call | flops 1000 | bytes 1000 | tf_op jit(solution)/shard_map/mixer_backward/pallas_call | solution.py:500
  342.9 7.5 %product_halves.1 = (bf16[512,1024]{1,0:T(8,128)(2,1)}, bf16[512,1024]{1,0:T(8,128)(2,1)S(1)}) custom-call(s32[1]{0:T(128)} %bitcast.side_ref, bf16[1024,1920]{1,0:T(8,128)(2,1)S(1)} %copy-done.3, bf16[1024,384]{1,0:T(8,128)(2,1)S(1)} %attention_backward.1.right_ref.refs_1_, bf16[1024,3328]{1,0:T(8,128)(2,1)S(1)} %bitcast.38, ...), custom_call_target="tpu_custom_call" | custom-call | flops 1000 | bytes 1000 | tf_op jit(solution)/shard_map/product_halves/pallas_call | solution.py:798
  356.9 3.8 collective-permute-done.26.right_ref
  368.2 3.6 own_rows.2.rest_1_
  371.8 6.0 %collective-permute-done.27.rest_3_.refs_6_ = bf16[64,1152]{1,0:T(8,128)(2,1)} collective-permute-done((bf16[64,1152]{1,0:T(8,128)(2,1)}, bf16[64,1152]{1,0:T(8,128)(2,1)}, u32[]{:S(2)}, u32[]{:S(2)}) %collective-permute-start.27) | collective-permute-done | bytes 147488 | tf_op jit(solution)/shard_map/ppermute | solution.py:999
  380.2 3.7 collective-permute-start.29
  391.1 3.9 own_rows.3.refs_1_
  (408 shorter events, 174.0 us)
Async XLA Ops:
  7.2 76.5 %all-gather.3.cloned.1.call-start = ((), (), s32[]{:S(2)}) async-start(), calls=%async_computation.1 | async-start | bytes 7241728 | tf_op jit(solution)/shard_map/all_gather | solution.py:1076
  18.1 129.7 %all-gather.5.cloned.1.call-start = ((), (), s32[]{:S(2)}) async-start(), calls=%async_computation.2 | async-start | bytes 6684672 | tf_op jit(solution)/shard_map/all_gather | solution.py:1081
  18.2 26.1 %collective-permute-start.3 = (bf16[512,1024]{1,0:T(8,128)(2,1)S(1)}, bf16[512,1024]{1,0:T(8,128)(2,1)S(1)}, u32[]{:S(2)}, u32[]{:S(2)}) collective-permute-start(bf16[512,1024]{1,0:T(8,128)(2,1)S(1)} %copy-done.98), channel_id=1, source_target_pairs={{0,1},{1,0},{2,3},{3,2},{4,5},{5,4},{6,7},{7,6},{8,9},{9,8},{10,11... | collective-permute-start | bytes 3145736 | tf_op jit(solution)/shard_map/ppermute | solution.py:894
  19.0 46.3 %collective-permute-start = (bf16[512,1024]{1,0:T(8,128)(2,1)S(1)}, bf16[512,1024]{1,0:T(8,128)(2,1)S(1)}, u32[]{:S(2)}, u32[]{:S(2)}) collective-permute-start(bf16[512,1024]{1,0:T(8,128)(2,1)S(1)} %copy-done.53), channel_id=1, source_target_pairs={{0,1},{1,0},{2,3},{3,2},{4,5},{5,4},{6,7},{7,6},{8,9},{9,8},{10,11... | collective-permute-start | bytes 3145736 | tf_op jit(solution)/shard_map/ppermute | solution.py:894
  83.8 320.2 %reduce-scatter.2.cloned.1.call-start = ((), (), s32[]{:S(2)}) async-start(), calls=%async_computation.3 | async-start | bytes 6684672 | tf_op jit(solution)/shard_map/reduce_scatter | solution.py:1139
  121.4 26.3 %collective-permute-start.4 = (bf16[512,1024]{1,0:T(8,128)(2,1)}, bf16[512,1024]{1,0:T(8,128)(2,1)}, u32[]{:S(2)}, u32[]{:S(2)}) collective-permute-start(bf16[512,1024]{1,0:T(8,128)(2,1)} %add_convert_fusion.low_ref), channel_id=1, source_target_pairs={{0,1},{1,0},{2,3},{3,2},{4,5},{5,4},{6,7},{7,6},{8,9},{9,8},{10,11... | collective-permute-start | bytes 3145736 | tf_op jit(solution)/shard_map/ppermute | solution.py:894
  125.4 44.8 %collective-permute-start.2 = (bf16[512,1024]{1,0:T(8,128)(2,1)}, bf16[512,1024]{1,0:T(8,128)(2,1)}, u32[]{:S(2)}, u32[]{:S(2)}) collective-permute-start(bf16[512,1024]{1,0:T(8,128)(2,1)} %add_convert_fusion.1.low_ref), channel_id=1, source_target_pairs={{0,1},{1,0},{2,3},{3,2},{4,5},{5,4},{6,7},{7,6},{8,9},{9,8},{10,11... | collective-permute-start | bytes 3145736 | tf_op jit(solution)/shard_map/ppermute | solution.py:894
  159.4 32.5 %collective-permute-start.6 = (bf16[512,1024]{1,0:T(8,128)(2,1)S(1)}, bf16[512,1024]{1,0:T(8,128)(2,1)S(1)}, u32[]{:S(2)}, u32[]{:S(2)}) collective-permute-start(bf16[512,1024]{1,0:T(8,128)(2,1)S(1)} %get-tuple-element.77.low_ref), channel_id=1, source_target_pairs={{0,1},{1,0},{2,3},{3,2},{4,5},{5,4},{6,7},{7,6},{8,9},{9,8},{10,11... | collective-permute-start | bytes 3145736 | tf_op jit(solution)/shard_map/ppermute | solution.py:894
  201.3 24.8 %collective-permute-start.5 = (bf16[512,1024]{1,0:T(8,128)(2,1)}, bf16[512,1024]{1,0:T(8,128)(2,1)S(1)}, u32[]{:S(2)}, u32[]{:S(2)}) collective-permute-start(bf16[512,1024]{1,0:T(8,128)(2,1)} %copy-done.73), channel_id=1, source_target_pairs={{0,1},{1,0},{2,3},{3,2},{4,5},{5,4},{6,7},{7,6},{8,9},{9,8},{10,11... | collective-permute-start | bytes 3145736 | tf_op jit(solution)/shard_map/ppermute | solution.py:894
  242.8 21.8 %collective-permute-start.9 = (bf16[512,1024]{1,0:T(8,128)(2,1)}, bf16[512,1024]{1,0:T(8,128)(2,1)}, u32[]{:S(2)}, u32[]{:S(2)}) collective-permute-start(bf16[512,1024]{1,0:T(8,128)(2,1)} %weight_grad.17.rest_2_), channel_id=1, source_target_pairs={{0,2},{2,0},{4,6},{6,4},{8,10},{10,8},{12,14},{14,12},{16,18},{18,... | collective-permute-start | bytes 3145736 | tf_op jit(solution)/shard_map/ppermute | solution.py:898
  243.9 50.6 %collective-permute-start.7 = (bf16[512,1024]{1,0:T(8,128)(2,1)}, bf16[512,1024]{1,0:T(8,128)(2,1)}, u32[]{:S(2)}, u32[]{:S(2)}) collective-permute-start(bf16[512,1024]{1,0:T(8,128)(2,1)} %constant_dynamic-slice_fusion.1), channel_id=1, source_target_pairs={{0,1},{1,0},{2,3},{3,2},{4,5},{5,4},{6,7},{7,6},{8,9},{9,8},{10,11... | collective-permute-start | bytes 3145736 | tf_op jit(solution)/shard_map/ppermute | solution.py:894
  270.6 39.5 %collective-permute-start.11 = (bf16[256,1024]{1,0:T(8,128)(2,1)}, bf16[256,1024]{1,0:T(8,128)(2,1)}, u32[]{:S(2)}, u32[]{:S(2)}) collective-permute-start(bf16[256,1024]{1,0:T(8,128)(2,1)} %get-tuple-element.96), channel_id=1, source_target_pairs={{0,4},{2,6},{4,0},{6,2},{8,12},{10,14},{12,8},{14,10},{16,20},{18,... | collective-permute-start | bytes 1572872 | tf_op jit(solution)/shard_map/ppermute | solution.py:898
  273.6 37.8 %collective-permute-start.10 = (bf16[256,384]{1,0:T(8,128)(2,1)}, bf16[256,384]{1,0:T(8,128)(2,1)S(1)}, u32[]{:S(2)}, u32[]{:S(2)}) collective-permute-start(bf16[256,384]{1,0:T(8,128)(2,1)} %get-tuple-element.95), channel_id=1, source_target_pairs={{0,4},{2,6},{4,0},{6,2},{8,12},{10,14},{12,8},{14,10},{16,20},{18,... | collective-permute-start | bytes 589832 | tf_op jit(solution)/shard_map/ppermute | solution.py:898
  318.6 17.2 %collective-permute-start.15 = (bf16[512,768]{1,0:T(8,128)(2,1)S(1)}, bf16[512,768]{1,0:T(8,128)(2,1)S(1)}, u32[]{:S(2)}, u32[]{:S(2)}) collective-permute-start(bf16[512,768]{1,0:T(8,128)(2,1)S(1)} %weight_grad.23.rest_0_), channel_id=1, source_target_pairs={{0,2},{2,0},{4,6},{6,4},{8,10},{10,8},{12,14},{14,12},{16,18},{18,... | collective-permute-start | bytes 2359304 | tf_op jit(solution)/shard_map/ppermute | solution.py:898
  324.0 31.9 %collective-permute-start.14 = (bf16[256,1152]{1,0:T(8,128)(2,1)S(1)}, bf16[256,1152]{1,0:T(8,128)(2,1)S(1)}, u32[]{:S(2)}, u32[]{:S(2)}) collective-permute-start(bf16[256,1152]{1,0:T(8,128)(2,1)S(1)} %get-tuple-element.101), channel_id=1, source_target_pairs={{0,4},{2,6},{4,0},{6,2},{8,12},{10,14},{12,8},{14,10},{16,20},{18,... | collective-permute-start | bytes 1769480 | tf_op jit(solution)/shard_map/ppermute | solution.py:898
  335.8 16.7 %collective-permute-start.25 = (f32[56,768]{1,0:T(8,128)S(1)}, f32[56,768]{1,0:T(8,128)S(1)}, u32[]{:S(2)}, u32[]{:S(2)}) collective-permute-start(f32[56,768]{1,0:T(8,128)S(1)} %added.4.rest_1_.left_ref), channel_id=1, source_target_pairs={{0,4},{2,6},{4,0},{6,2},{8,12},{10,14},{12,8},{14,10},{16,20},{18,... | collective-permute-start | bytes 516104 | tf_op jit(solution)/shard_map/ppermute | solution.py:898
  350.4 38.5 %collective-permute-start.23 = (bf16[512,1024]{1,0:T(8,128)(2,1)}, bf16[512,1024]{1,0:T(8,128)(2,1)}, u32[]{:S(2)}, u32[]{:S(2)}) collective-permute-start(bf16[512,1024]{1,0:T(8,128)(2,1)} %get-tuple-element.112), channel_id=1, source_target_pairs={{0,1},{1,0},{2,3},{3,2},{4,5},{5,4},{6,7},{7,6},{8,9},{9,8},{10,11... | collective-permute-start | bytes 3145736 | tf_op jit(solution)/shard_map/ppermute | solution.py:894
  351.3 20.5 %collective-permute-start.24 = (bf16[256,768]{1,0:T(8,128)(2,1)}, bf16[256,768]{1,0:T(8,128)(2,1)}, u32[]{:S(2)}, u32[]{:S(2)}) collective-permute-start(bf16[256,768]{1,0:T(8,128)(2,1)} %get-tuple-element.113), channel_id=1, source_target_pairs={{0,4},{2,6},{4,0},{6,2},{8,12},{10,14},{12,8},{14,10},{16,20},{18,... | collective-permute-start | bytes 1179656 | tf_op jit(solution)/shard_map/ppermute | solution.py:898
  360.8 25.6 %collective-permute-start.32 = (f32[56,768]{1,0:T(8,128)S(1)}, f32[56,768]{1,0:T(8,128)}, u32[]{:S(2)}, u32[]{:S(2)}) collective-permute-start(f32[56,768]{1,0:T(8,128)S(1)} %added.6.rest_0_.left_ref), channel_id=1, source_target_pairs={{0,16},{2,18},{4,20},{6,22},{8,24},{10,26},{12,28},{14,30},{16,0},... | collective-permute-start | bytes 516104 | tf_op jit(solution)/shard_map/ppermute | solution.py:898
  360.8 16.9 %collective-permute-start.27 = (bf16[64,1152]{1,0:T(8,128)(2,1)}, bf16[64,1152]{1,0:T(8,128)(2,1)}, u32[]{:S(2)}, u32[]{:S(2)}) collective-permute-start(bf16[64,1152]{1,0:T(8,128)(2,1)} %get-tuple-element.115), channel_id=1, source_target_pairs={{0,16},{2,18},{4,20},{6,22},{8,24},{10,26},{12,28},{14,30},{16,0},... | collective-permute-start | bytes 442376 | tf_op jit(solution)/shard_map/ppermute | solution.py:999
  364.5 13.2 %collective-permute-start.28 = (bf16[64,1152]{1,0:T(8,128)(2,1)}, bf16[64,1152]{1,0:T(8,128)(2,1)}, u32[]{:S(2)}, u32[]{:S(2)}) collective-permute-start(bf16[64,1152]{1,0:T(8,128)(2,1)} %get-tuple-element.116), channel_id=1, source_target_pairs={{0,24},{2,26},{4,28},{6,30},{8,0},{10,2},{12,4},{14,6},{16,8},{18,... | collective-permute-start | bytes 442376 | tf_op jit(solution)/shard_map/ppermute | solution.py:999
  380.2 14.7 %collective-permute-start.29 = (bf16[64,768]{1,0:T(8,128)(2,1)S(1)}, bf16[64,768]{1,0:T(8,128)(2,1)S(1)}, u32[]{:S(2)}, u32[]{:S(2)}) collective-permute-start(bf16[64,768]{1,0:T(8,128)(2,1)S(1)} %get-tuple-element.118), channel_id=1, source_target_pairs={{0,8},{2,10},{4,12},{6,14},{8,16},{10,18},{12,20},{14,22},{16,24},... | collective-permute-start | bytes 294920 | tf_op jit(solution)/shard_map/ppermute | solution.py:999
  383.9 11.1 %collective-permute-start.30 = (bf16[64,768]{1,0:T(8,128)(2,1)S(1)}, bf16[64,768]{1,0:T(8,128)(2,1)S(1)}, u32[]{:S(2)}, u32[]{:S(2)}) collective-permute-start(bf16[64,768]{1,0:T(8,128)(2,1)S(1)} %get-tuple-element.119), channel_id=1, source_target_pairs={{0,16},{2,18},{4,20},{6,22},{8,24},{10,26},{12,28},{14,30},{16,0},... | collective-permute-start | bytes 294920 | tf_op jit(solution)/shard_map/ppermute | solution.py:999
  384.0 11.0 %collective-permute-start.31 = (bf16[64,768]{1,0:T(8,128)(2,1)S(1)}, bf16[64,768]{1,0:T(8,128)(2,1)S(1)}, u32[]{:S(2)}, u32[]{:S(2)}) collective-permute-start(bf16[64,768]{1,0:T(8,128)(2,1)S(1)} %get-tuple-element.120), channel_id=1, source_target_pairs={{0,24},{2,26},{4,28},{6,30},{8,0},{10,2},{12,4},{14,6},{16,8},{18,... | collective-permute-start | bytes 294920 | tf_op jit(solution)/shard_map/ppermute | solution.py:999
  (123 other events, 830.7 us)
Sparse Core Ops, SparseCore 0:
  18.2 65.4 all-gather.2
  86.0 60.3 all-gather.4
  201.4 86.0 reduce-scatter.1
